TPU v7x, 32 devices: a whole 2x2x4 slice. The times are simulated.
32 devices in a mesh: dp: 8 (over z, x), group: 4 (over y, core).
Axes of the slice: x: 2, y: 2, z: 4, core: 2. Of those that a mesh axis runs over, the one named last changes fastest.
Arguments:
- token_ids: int32 [16384], P(('dp', 'group')), may hold values from 0 to 30527
- seq_lengths: int32 [32, 4], P(('dp', 'group')), may hold values from 1 to 320, 512 in all within a row
- valid_mask: int32 [16384], P(('dp', 'group')), may hold values 0 or 1
- deal_order: int32 [128], replicated, may hold values from 0 to 127, each once
- log_scale: float32 [1], replicated, may hold values from 2.5 to 3.5
- embed_master: float32 [30528, 512], P('dp'), may hold values from -6 to 6
- attn_in: float32 [2, 512, 1536], P(None, 'dp'), may hold values from -0.25 to 0.25
- attn_out: float32 [2, 512, 512], P(None, 'dp'), may hold values from -0.75 to 0.75
- ffn_in: float32 [2, 512, 4096], P(None, 'dp'), may hold values from -0.25 to 0.25
- ffn_out: float32 [2, 2048, 512], P(None, 'dp'), may hold values from -0.125 to 0.125
- head_master: float32 [512, 512], P('dp'), may hold values from -0.25 to 0.25
- norm_master: float32 [5, 2, 512], P(None, None, 'dp'), may hold values from -1.2 to 1.4, as said below
- embed_rows: float32 [30528], P('dp'), as said below
- head_rows: float32 [512], P('dp'), as said below
- layer_rows: float32 [2, 3, 512], P(None, None, 'dp'), as said below
- ffn_out_rows: float32 [2, 2048], P(None, 'dp'), as said below
- layer_cols: float32 [2, 6656], replicated, as said below
- embed_head_cols: float32 [2, 512], replicated, as said below
- norm_state: float32 [5, 2, 512], P(None, None, 'dp'), as said below
- scale_state: float32 [1], replicated, as said below
Outputs:
- pair_loss: float32 [], replicated
- new_embed: float32 [30528, 512], P('dp')
- new_attn_in: float32 [2, 512, 1536], P(None, 'dp')
- new_attn_out: float32 [2, 512, 512], P(None, 'dp')
- new_ffn_in: float32 [2, 512, 4096], P(None, 'dp')
- new_ffn_out: float32 [2, 2048, 512], P(None, 'dp')
- new_head: float32 [512, 512], P('dp')
- new_norm: float32 [5, 2, 512], P(None, None, 'dp')
- new_log_scale: float32 [1], replicated
- new_embed_rows: float32 [30528], P('dp')
- new_head_rows: float32 [512], P('dp')
- new_layer_rows: float32 [2, 3, 512], P(None, None, 'dp')
- new_ffn_out_rows: float32 [2, 2048], P(None, 'dp')
- new_layer_cols: float32 [2, 6656], replicated
- new_embed_cols: float32 [512], replicated
- new_head_cols: float32 [512], replicated
- new_norm_state: float32 [5, 2, 512], P(None, None, 'dp')
- new_scale_state: float32 [1], replicated
- update_rms: float32 [10], replicated
Inputs may be any that keep to these rules, and one draw needn't show every extreme that they name: `seq_lengths`: each row holds 4 lengths that sum to 512. `deal_order`: a permutation; sequence j < 64 is a query whose document is sequence 64 + j. `norm_master`: gains near one, biases near zero. `embed_rows`: positive. `head_rows`: positive. `layer_rows`: positive. `ffn_out_rows`: positive. `layer_cols`: positive. `embed_head_cols`: positive. `norm_state`: positive. `scale_state`: positive.
All inputs are finite; a program needn't handle non-finite values. No bound on the sum of `valid_mask` on one device may be relied on, other than what follows from the above.
Results may differ from a plain program's by a relative error of at most 0.0085.
The roundings to bfloat16 on the way count: a program that leaves them out, or rounds other values in their place, can miss the bound.
Values may be sent and summed in bfloat16 or wider, within the bound.
A program may use at most 256 MiB of HBM per device.

v0:
```python
import jax
import jax.numpy as jnp
from jax import lax
from jax.sharding import PartitionSpec as P

D = 512
HEADS = 8
HEAD_DIM = 64
FF = 2048
VOCAB = 30528
LAYERS = 2


NORM_EPS = 1e-06
UNIT_EPS = 1e-06
STATE_EPS = 1e-30
DECAY_RATE = 0.5
CLIP_LEVEL = 0.05
RATE_SCALE = 10.0
NORM_RATE = 0.1


def layer_norm(values, gain_vec, shift_vec):
    center = values - jnp.mean(values, axis=-1, keepdims=True)
    spread = jnp.mean(center * center, axis=-1, keepdims=True)
    return center * lax.rsqrt(spread + NORM_EPS) * gain_vec + shift_vec


def geglu(joined):
    half_width = joined.shape[-1] // 2
    return jax.nn.gelu(joined[:, :half_width]) * joined[:, half_width:]


def alibi_slopes(head_count):
    return 2.0 ** (-8.0 * (jnp.arange(head_count).astype(jnp.float32) + 1.0) / head_count)


def normalize(vectors):
    return vectors * lax.rsqrt(jnp.sum(vectors * vectors, axis=-1, keepdims=True) + UNIT_EPS)


def contrast(unit_all, scale_arg, deal_order):
    pair_count = deal_order.shape[0] // 2
    queries = jnp.take(unit_all, deal_order[:pair_count], axis=0)
    documents = jnp.take(unit_all, deal_order[pair_count:], axis=0)
    logits = jnp.exp(scale_arg[0]) * jnp.matmul(
        queries, documents.T, precision=lax.Precision.HIGHEST
    )
    by_row = jax.nn.logsumexp(logits, axis=1)
    by_column = jax.nn.logsumexp(logits, axis=0)
    return jnp.sum(0.5 * (by_row + by_column) - jnp.diagonal(logits))


def unfactored(grad_full, state):
    state_new = DECAY_RATE * state + (1.0 - DECAY_RATE) * (grad_full * grad_full + STATE_EPS)
    return (-NORM_RATE * grad_full * lax.rsqrt(state_new), state_new)


def block_scores(query_rows, key_all, seg_rows, segment, head_count):
    row_count = query_rows.shape[0]
    raw_scores = jnp.einsum("thc,shc->hts", query_rows, key_all, preferred_element_type=jnp.float32)
    row_pos = jnp.arange(row_count, dtype=jnp.int32)
    col_pos = jnp.arange(key_all.shape[0], dtype=jnp.int32)
    distance = jnp.abs(row_pos[:, None] - col_pos[None, :]).astype(jnp.float32)
    scores = (
        raw_scores * HEAD_DIM ** (-0.5) + -alibi_slopes(head_count)[:, None, None] * distance[None]
    )
    same_seq = seg_rows[:, None] == segment[None, :]
    return jnp.where(same_seq[None], scores, -jnp.inf)


def split_qkv(qkv_low, head_count):
    tokens = qkv_low.shape[0]
    split_heads = qkv_low.reshape(tokens, 3, head_count, qkv_low.shape[1] // (3 * head_count))
    return (split_heads[:, 0], split_heads[:, 1], split_heads[:, 2])


def attend(qkv_low, segment, head_count):
    model_width = qkv_low.shape[1] // 3
    query_all, key_all, value_all = split_qkv(qkv_low, head_count)
    scores = block_scores(query_all, key_all, segment, segment, head_count)
    row_max = jnp.max(scores, axis=-1, keepdims=True)
    exponent = jnp.exp(scores - row_max)
    row_total = jnp.sum(exponent, axis=-1, keepdims=True)
    prob_low = (exponent / row_total).astype(jnp.bfloat16)
    mixed_list = jnp.einsum(
        "hts,shc->thc", prob_low, value_all, preferred_element_type=jnp.float32
    ).reshape(-1, model_width)
    lse_list = row_max[..., 0] + jnp.log(row_total[..., 0])
    return (mixed_list, lse_list)


def attend_back(qkv_low, segment, head_count, lse_all, grad_mixed):
    tokens = qkv_low.shape[0]
    query_all, key_all, value_all = split_qkv(qkv_low, head_count)
    grad_out = grad_mixed.reshape(tokens, head_count, -1)
    block_rows = min(tokens, 512)
    scores = block_scores(query_all, key_all, segment, segment, head_count)
    prob_full = jnp.exp(scores - lse_all[:, 0:block_rows, None])
    grad_value = jnp.einsum(
        "hts,thc->shc", prob_full.astype(jnp.bfloat16), grad_out, preferred_element_type=jnp.float32
    )
    grad_prob = jnp.einsum("thc,shc->hts", grad_out, value_all, preferred_element_type=jnp.float32)
    inner = jnp.sum(prob_full * grad_prob, axis=-1, keepdims=True)
    grad_raw = (prob_full * (grad_prob - inner) * HEAD_DIM ** (-0.5)).astype(jnp.bfloat16)
    query_list = jnp.einsum("hts,shc->thc", grad_raw, key_all, preferred_element_type=jnp.float32)
    grad_key = jnp.einsum("hts,thc->shc", grad_raw, query_all, preferred_element_type=jnp.float32)
    return (
        jnp.stack([query_list, grad_key, grad_value], axis=1)
        .reshape(tokens, -1)
        .astype(jnp.bfloat16)
    )


def shards(
    token_ids,
    seq_lengths,
    valid_mask,
    deal_order,
    log_scale,
    embed_master,
    attn_in,
    attn_out,
    ffn_in,
    ffn_out,
    head_master,
    norm_master,
    embed_rows,
    head_rows,
    layer_rows,
    ffn_out_rows,
    layer_cols,
    embed_head_cols,
    norm_state,
    scale_state,
):
    tokens = token_ids.shape[0]
    model_width = embed_master.shape[1]
    seq_count = seq_lengths.shape[1]
    head_count = HEADS
    position = jnp.arange(tokens, dtype=jnp.int32)
    bounds = jnp.cumsum(seq_lengths[0])
    segment = jnp.sum((position[:, None] >= bounds[None, :]).astype(jnp.int32), axis=1)
    piece_rows = lax.all_gather(embed_master.astype(jnp.bfloat16), "dp", axis=0, tiled=True)
    local_idx = token_ids
    inside = (local_idx >= 0) & (local_idx < piece_rows.shape[0])
    picked = jnp.take(piece_rows, jnp.clip(local_idx, 0, piece_rows.shape[0] - 1), axis=0).astype(
        jnp.float32
    )
    stream = jnp.where(inside[:, None], picked, 0.0)
    w_qkv, w_attn, w_gate_up, w_down, w_head, norm_low = (
        lax.all_gather(attn_in.astype(jnp.bfloat16), "dp", axis=1, tiled=True),
        lax.all_gather(attn_out.astype(jnp.bfloat16), "dp", axis=1, tiled=True),
        lax.all_gather(ffn_in.astype(jnp.bfloat16), "dp", axis=1, tiled=True),
        lax.all_gather(ffn_out.astype(jnp.bfloat16), "dp", axis=1, tiled=True),
        lax.all_gather(head_master.astype(jnp.bfloat16), "dp", axis=0, tiled=True),
        lax.all_gather(norm_master.astype(jnp.bfloat16), "dp", axis=2, tiled=True),
    )
    norms = norm_low.astype(jnp.float32)
    kept_list = []
    for layer_idx in range(LAYERS):
        stream_low = stream.astype(jnp.bfloat16)
        qkv_low = jnp.dot(stream_low, w_qkv[layer_idx], preferred_element_type=jnp.float32).astype(
            jnp.bfloat16
        )
        mixed_heads, lse_all = attend(qkv_low, segment, head_count)
        mixed_low = mixed_heads.astype(jnp.bfloat16)
        resid_one = stream + jnp.dot(
            mixed_low, w_attn[layer_idx], preferred_element_type=jnp.float32
        )
        normed = layer_norm(resid_one, norms[2 * layer_idx, 0], norms[2 * layer_idx, 1])
        normed_low = normed.astype(jnp.bfloat16)
        joined = jnp.dot(normed_low, w_gate_up[layer_idx], preferred_element_type=jnp.float32)
        hidden_low = geglu(joined).astype(jnp.bfloat16)
        resid_two = normed + jnp.dot(
            hidden_low, w_down[layer_idx], preferred_element_type=jnp.float32
        )
        kept_list.append(
            (
                stream_low,
                qkv_low,
                lse_all,
                mixed_low,
                resid_one,
                normed_low,
                joined,
                hidden_low,
                resid_two,
            )
        )
        stream = layer_norm(resid_two, norms[2 * layer_idx + 1, 0], norms[2 * layer_idx + 1, 1])
    final = layer_norm(stream, norms[2 * LAYERS, 0], norms[2 * LAYERS, 1])
    member = (
        (segment[None, :] == jnp.arange(seq_count, dtype=jnp.int32)[:, None])
        & (valid_mask[None, :] > 0)
    ).astype(jnp.float32)
    counts = jnp.maximum(jnp.sum(member, axis=1), 1.0)
    pooled = jnp.matmul(member, final, precision=lax.Precision.HIGHEST) / counts[:, None]
    pooled_low = pooled.astype(jnp.bfloat16)
    head_out = jnp.dot(pooled_low, w_head, preferred_element_type=jnp.float32)
    unit_vecs, unit_back = jax.vjp(normalize, head_out)
    unit_every = lax.all_gather(unit_vecs, ("dp", "group"), axis=0, tiled=True)
    loss_value, loss_back = jax.vjp(
        lambda unit_all, scale_arg: contrast(unit_all, scale_arg, deal_order), unit_every, log_scale
    )
    grad_units, grad_scale = loss_back(jnp.ones_like(loss_value))
    own_rows = lax.dynamic_slice_in_dim(
        grad_units, lax.axis_index(("dp", "group")) * seq_count, seq_count, 0
    )
    grad_head_out = unit_back(own_rows)[0].astype(jnp.bfloat16)
    grad_head = jnp.dot(pooled_low.T, grad_head_out, preferred_element_type=jnp.float32)
    grad_pooled = jnp.dot(grad_head_out, w_head.T, preferred_element_type=jnp.float32)
    grad_final = jnp.matmul(
        member.T, grad_pooled / counts[:, None], precision=lax.Precision.HIGHEST
    )
    final_back = jax.vjp(layer_norm, stream, norms[2 * LAYERS, 0], norms[2 * LAYERS, 1])[1]
    grad_stream, gain_last, shift_last = final_back(grad_final)
    norm_grads = [None] * (2 * LAYERS + 1)
    norm_grads[2 * LAYERS] = jnp.stack([gain_last, shift_last])
    qkv_grads = [None] * LAYERS
    attn_grads = [None] * LAYERS
    gate_grads = [None] * LAYERS
    down_grads = [None] * LAYERS
    for layer_idx in reversed(range(LAYERS)):
        (
            stream_low,
            qkv_low,
            lse_all,
            mixed_low,
            resid_one,
            normed_low,
            joined,
            hidden_low,
            resid_two,
        ) = kept_list[layer_idx]
        norm_two_back = jax.vjp(
            layer_norm, resid_two, norms[2 * layer_idx + 1, 0], norms[2 * layer_idx + 1, 1]
        )[1]
        grad_two, gain_two, shift_two = norm_two_back(grad_stream)
        norm_grads[2 * layer_idx + 1] = jnp.stack([gain_two, shift_two])
        grad_branch = grad_two.astype(jnp.bfloat16)
        down_grads[layer_idx] = jnp.dot(
            hidden_low.T, grad_branch, preferred_element_type=jnp.float32
        )
        grad_hidden = jnp.dot(grad_branch, w_down[layer_idx].T, preferred_element_type=jnp.float32)
        grad_joined = jax.vjp(geglu, joined)[1](grad_hidden)[0].astype(jnp.bfloat16)
        gate_grads[layer_idx] = jnp.dot(
            normed_low.T, grad_joined, preferred_element_type=jnp.float32
        )
        grad_normed = grad_two + jnp.dot(
            grad_joined, w_gate_up[layer_idx].T, preferred_element_type=jnp.float32
        )
        norm_one_back = jax.vjp(
            layer_norm, resid_one, norms[2 * layer_idx, 0], norms[2 * layer_idx, 1]
        )[1]
        grad_one, gain_one, shift_one = norm_one_back(grad_normed)
        norm_grads[2 * layer_idx] = jnp.stack([gain_one, shift_one])
        grad_attended = grad_one.astype(jnp.bfloat16)
        attn_grads[layer_idx] = jnp.dot(
            mixed_low.T, grad_attended, preferred_element_type=jnp.float32
        )
        grad_mixed = jnp.dot(
            grad_attended, w_attn[layer_idx].T, preferred_element_type=jnp.float32
        ).astype(jnp.bfloat16)
        grad_qkv_low = attend_back(qkv_low, segment, head_count, lse_all, grad_mixed)
        qkv_grads[layer_idx] = jnp.dot(
            stream_low.T, grad_qkv_low, preferred_element_type=jnp.float32
        )
        grad_stream = grad_one + jnp.dot(
            grad_qkv_low, w_qkv[layer_idx].T, preferred_element_type=jnp.float32
        )
    row_count = embed_master.shape[0] * lax.axis_size("dp")
    local_idx = token_ids
    inside = (local_idx >= 0) & (local_idx < row_count)
    slot_idx = jnp.where(inside, local_idx, row_count)
    embed_grad = lax.psum_scatter(
        jnp.zeros((row_count, model_width), jnp.float32).at[slot_idx].add(grad_stream, mode="drop"),
        "dp",
        scatter_dimension=0,
        tiled=True,
    )
    grad_qkv = jnp.stack(qkv_grads)
    grad_attn = jnp.stack(attn_grads)
    grad_gate_up = jnp.stack(gate_grads)
    grad_down = jnp.stack(down_grads)
    grad_norm = jnp.stack(norm_grads)
    owned = (
        lax.psum_scatter(grad_qkv, "dp", scatter_dimension=1, tiled=True),
        lax.psum_scatter(grad_attn, "dp", scatter_dimension=1, tiled=True),
        lax.psum_scatter(grad_gate_up, "dp", scatter_dimension=1, tiled=True),
        lax.psum_scatter(grad_down, "dp", scatter_dimension=1, tiled=True),
        lax.psum_scatter(grad_head, "dp", scatter_dimension=0, tiled=True),
        lax.psum_scatter(grad_norm, "dp", scatter_dimension=2, tiled=True),
    )
    shard_qkv, shard_attn, shard_gate_up, shard_down, shard_head, shard_norm, shard_embed = (
        lax.psum((owned[0], owned[1], owned[2], owned[3], owned[4], owned[5], embed_grad), "group")
    )
    grad_list = [
        shard_embed[None],
        shard_head[None],
        shard_qkv,
        shard_attn,
        shard_gate_up,
        shard_down,
    ]
    master_list = [embed_master[None], head_master[None], attn_in, attn_out, ffn_in, ffn_out]
    state_list = [
        embed_rows[None],
        head_rows[None],
        layer_rows[:, 0],
        layer_rows[:, 1],
        layer_rows[:, 2],
        ffn_out_rows,
    ]
    col_list = [
        embed_head_cols[0:1],
        embed_head_cols[1:2],
        layer_cols[:, : 3 * D],
        layer_cols[:, 3 * D : 4 * D],
        layer_cols[:, 4 * D : 4 * D + 2 * FF],
        layer_cols[:, 4 * D + 2 * FF :],
    ]
    total_rows = [VOCAB, D, D, D, D, FF]
    wide_rate = RATE_SCALE / D**0.5
    rates = [
        RATE_SCALE,
        wide_rate,
        wide_rate,
        RATE_SCALE / (D // 8) ** 0.5,
        wide_rate,
        RATE_SCALE / FF**0.5,
    ]
    square_list = [grad_part * grad_part for grad_part in grad_list]
    rows_new = [
        DECAY_RATE * state_list[entry_idx]
        + (1.0 - DECAY_RATE) * (jnp.mean(square_list[entry_idx], axis=-1) + STATE_EPS)
        for entry_idx in range(6)
    ]
    col_parts = jnp.concatenate(
        [jnp.sum(square_part, axis=1).reshape(-1) for square_part in square_list]
    )
    row_parts = jnp.concatenate([jnp.sum(row_part, axis=-1) for row_part in rows_new])
    col_sum, row_sum = lax.psum((col_parts, row_parts), "dp")
    row_means = []
    lead_start = 0
    for entry_idx in range(6):
        lead_count = grad_list[entry_idx].shape[0]
        row_means.append(row_sum[lead_start : lead_start + lead_count] / total_rows[entry_idx])
        lead_start = lead_start + lead_count
    cols_new = []
    steps_all = []
    col_start = 0
    for entry_idx in range(6):
        lead_count = grad_list[entry_idx].shape[0]
        col_width = grad_list[entry_idx].shape[2]
        col_full = col_sum[col_start : col_start + lead_count * col_width].reshape(
            lead_count, col_width
        )
        col_state_new = DECAY_RATE * col_list[entry_idx] + (1.0 - DECAY_RATE) * (
            col_full / total_rows[entry_idx] + STATE_EPS
        )
        cols_new.append(col_state_new)
        steps_all.append(
            grad_list[entry_idx]
            * lax.rsqrt(
                rows_new[entry_idx][:, :, None]
                * col_state_new[:, None, :]
                / row_means[entry_idx][:, None, None]
            )
        )
        col_start = col_start + lead_count * col_width
    step_squares = []
    step_parts = jnp.concatenate(
        [jnp.sum(step_dir * step_dir, axis=(1, 2)) for step_dir in steps_all]
    )
    step_sum = lax.psum(step_parts, "dp")
    lead_start = 0
    for entry_idx in range(6):
        lead_count = grad_list[entry_idx].shape[0]
        step_squares.append(step_sum[lead_start : lead_start + lead_count])
        lead_start = lead_start + lead_count
    new_weights = []
    rms_list = []
    for entry_idx in range(6):
        cell_count = total_rows[entry_idx] * grad_list[entry_idx].shape[2]
        step_rms = jnp.sqrt(step_squares[entry_idx] / cell_count)
        rms_list.append(step_rms)
        delta = (
            -rates[entry_idx]
            * steps_all[entry_idx]
            / jnp.maximum(1.0, step_rms / CLIP_LEVEL)[:, None, None]
        )
        new_weights.append(master_list[entry_idx] + delta)
    norm_delta, norm_second = unfactored(shard_norm, norm_state)
    scale_delta, scale_state_new = unfactored(grad_scale, scale_state)
    return (
        loss_value,
        new_weights[0][0],
        new_weights[2],
        new_weights[3],
        new_weights[4],
        new_weights[5],
        new_weights[1][0],
        norm_master + norm_delta,
        log_scale + scale_delta,
        rows_new[0][0],
        rows_new[1][0],
        jnp.stack([rows_new[2], rows_new[3], rows_new[4]], axis=1),
        rows_new[5],
        jnp.concatenate([cols_new[2], cols_new[3], cols_new[4], cols_new[5]], axis=1),
        cols_new[0][0],
        cols_new[1][0],
        norm_second,
        scale_state_new,
        jnp.concatenate(rms_list),
    )


def solution(mesh):
    in_specs = (
        P(("dp", "group")),
        P(("dp", "group"), None),
        P(("dp", "group")),
        P(),
        P(),
        P("dp", None),
        P(None, "dp", None),
        P(None, "dp", None),
        P(None, "dp", None),
        P(None, "dp", None),
        P("dp", None),
        P(None, None, "dp"),
        P("dp"),
        P("dp"),
        P(None, None, "dp"),
        P(None, "dp"),
        P(),
        P(),
        P(None, None, "dp"),
        P(),
    )
    out_specs = (
        P(),
        P("dp", None),
        P(None, "dp", None),
        P(None, "dp", None),
        P(None, "dp", None),
        P(None, "dp", None),
        P("dp", None),
        P(None, None, "dp"),
        P(),
        P("dp"),
        P("dp"),
        P(None, None, "dp"),
        P(None, "dp"),
        P(),
        P(),
        P(),
        P(None, None, "dp"),
        P(),
        P(),
    )
    return jax.shard_map(shards, mesh=mesh, in_specs=in_specs, out_specs=out_specs, check_vma=False)
```

profile of v0, /device:TPU:0, one launch (start us, length us, event | category | flops | bytes accessed | tf_op | source)
XLA Modules:
  0.0 3159.0 jit_solution(1054017429399059691)
XLA Ops:
  7.2 5.6 convert_element_type.178
  19.8 80.8 %all_gather.27 = bf16[5,2,512]{0,1,2:T(2,128)(2,1)S(1)} all-gather(bf16[5,2,64]{0,1,2:T(2,128)(2,1)S(1)} %copy.138), channel_id=1, replica_groups=mesh['dp'=8,'group'=4] {'dp'}, dimensions={2}, use_global_device_ids=true | all-gather | bytes 11520 | tf_op jit(solution)/shard_map/all_gather | solution.py:157
  106.6 47.1 %all_gather.30 = bf16[512,512]{1,0:T(8,128)(2,1)} all-gather(bf16[64,512]{1,0:T(8,128)(2,1)S(1)} %convert_element_type.206), channel_id=1, replica_groups=mesh['dp'=8,'group'=4] {'dp'}, dimensions={0}, use_global_device_ids=true | all-gather | bytes 589824 | tf_op jit(solution)/shard_map/all_gather | solution.py:156
  153.9 17.5 slice_reduce_fusion.3
  171.4 453.8 %all-gather.7.cloned.1.call-done = bf16[30528,512]{1,0:T(8,128)(2,1)} async-done(((bf16[3816,512]{1,0:T(8,128)(2,1)}), bf16[30528,512]{1,0:T(8,128)(2,1)}) %all-gather.7.cloned.1.call-update) | async-done | bytes 31260688 | tf_op jit(solution)/shard_map/all_gather | solution.py:144
  625.2 3.8 gather_fusion
  629.3 59.2 %all-gather.9.cloned.1.call-done = bf16[2,512,1536]{2,1,0:T(8,128)(2,1)} async-done(((bf16[2,64,1536]{2,1,0:T(8,128)(2,1)}), bf16[2,512,1536]{2,1,0:T(8,128)(2,1)}) %all-gather.9.cloned.1.call-update) | async-done | bytes 3145744 | tf_op jit(solution)/shard_map/all_gather | solution.py:152
  688.4 3.6 convolution_convert_fusion.1
  694.2 4.2 fusion.203
  703.3 26.8 all-gather.11.cloned.1.call-done
  731.9 124.5 %all-gather.13.cloned.1.call-done = bf16[2,512,4096]{2,1,0:T(8,128)(2,1)} async-done(((bf16[2,64,4096]{2,1,0:T(8,128)(2,1)}), bf16[2,512,4096]{2,1,0:T(8,128)(2,1)}) %all-gather.13.cloned.1.call-update) | async-done | bytes 8388624 | tf_op jit(solution)/shard_map/all_gather | solution.py:154
  856.4 4.7 fusion.49
  866.7 63.9 %all-gather.15.cloned.1.call-done = bf16[2,2048,512]{2,1,0:T(8,128)(2,1)} async-done(((bf16[2,256,512]{2,1,0:T(8,128)(2,1)}), bf16[2,2048,512]{2,1,0:T(8,128)(2,1)}) %all-gather.15.cloned.1.call-update) | async-done | bytes 4194320 | tf_op jit(solution)/shard_map/all_gather | solution.py:155
  930.6 3.7 fusion.205
  939.7 3.7 fusion.206
  963.9 42.3 %all-gather = f32[32,4,512]{2,1,0:T(4,128)} all-gather(f32[1,4,512]{2,1,0:T(4,128)S(1)} %multiply_bitcast_fusion), channel_id=1, replica_groups=mesh['dp'=8,'group'=4] {'dp','group'}, dimensions={0}, use_global_device_ids=true | all-gather | bytes 270336 | tf_op jit(solution)/shard_map/all_gather | solution.py:202
  1013.2 3.8 scatter_fusion
  1039.3 9.5 fusion.57
  1048.9 7.3 multiply_reduce_fusion.10
  1058.2 5.7 fusion.100
  1066.2 15.7 fusion.66
  1081.8 15.8 fusion.69
  1099.3 3.7 multiply_reduce_fusion.11
  1103.5 6.8 fusion.56
  1110.9 3.6 multiply_reduce_fusion.12
  1121.9 5.5 fusion.99
  1127.5 15.6 fusion.60
  1143.1 15.6 fusion.63
  1158.7 5.1 fusion.75
  1171.0 3.3 convolution_bitcast_fusion.2
  1175.6 4.2 pad_maximum_fusion.1
  1180.6 6.2 convolution_bitcast_fusion
  1189.2 6.1 pad_maximum_fusion
  1196.7 3.4 fusion.79
  1201.7 20.0 broadcast_in_dim.106
  1221.7 61.1 %scatter_fusion.1 = f32[30528,512]{1,0:T(8,128)} fusion(f32[30528,512]{1,0:T(8,128)} %broadcast_in_dim.106, s32[512]{0:T(512)S(1)} %copy-done.126, f32[512,512]{1,0:T(8,128)S(1)} %copy.152), kind=kCustom, calls=%fused_computation.7 | custom fusion | flops 262144 | bytes 3147776 | tf_op jit(solution)/shard_map/scatter-add | solution.py:277
  1285.5 64.3 %reduce-scatter.14.cloned.1.call-done = f32[2,64,1536]{2,1,0:T(8,128)} async-done(((f32[2,512,1536]{2,1,0:T(8,128)}), f32[2,64,1536]{2,1,0:T(8,128)}) %reduce-scatter.14.cloned.1.call-update) | async-done | bytes 786448 | tf_op jit(solution)/shard_map/reduce_scatter | solution.py:288
  1349.8 152.2 %reduce-scatter.20.cloned.1.call-done = f32[2,256,512]{2,1,0:T(8,128)} async-done(((f32[2,2048,512]{2,1,0:T(8,128)}), f32[2,256,512]{2,1,0:T(8,128)}) %reduce-scatter.20.cloned.1.call-update) | async-done | bytes 1048592 | tf_op jit(solution)/shard_map/reduce_scatter | solution.py:291
  1502.0 284.7 %reduce-scatter.18.cloned.1.call-done = f32[2,64,4096]{2,1,0:T(8,128)} async-done(((f32[2,512,4096]{2,1,0:T(8,128)}), f32[2,64,4096]{2,1,0:T(8,128)}) %reduce-scatter.18.cloned.1.call-update) | async-done | bytes 2097168 | tf_op jit(solution)/shard_map/reduce_scatter | solution.py:290
  1786.7 968.8 %reduce-scatter.24.cloned.1.call-done = f32[3816,512]{1,0:T(8,128)} async-done(((f32[30528,512]{1,0:T(8,128)}), f32[3816,512]{1,0:T(8,128)}) %reduce-scatter.24.cloned.1.call-update) | async-done | bytes 7815184
  2757.6 62.0 %reduce-scatter.22.cloned.1.call-done = f32[64,10]{1,0:T(8,128)} async-done(((f32[512,10]{1,0:T(8,128)}), f32[64,10]{1,0:T(8,128)}) %reduce-scatter.22.cloned.1.call-update) | async-done | bytes 2576
  2820.7 5.9 psum.79
  2826.6 211.1 %all-reduce.9.cloned.1.call-done = (f32[3816,512]{1,0:T(8,128)}, f32[64,512]{1,0:T(8,128)}, f32[2,64,1536]{2,1,0:T(8,128)}, f32[2,64,512]{2,1,0:T(8,128)}, f32[2...) async-done(((f32[3816,512]{1,0:T(8,128)}, f32[64,512]{1,0:T(8,128)}, f32[2,64,1536]{2,1,0:T(8,128)}, f32[2,64,512]{2,1,0:T(8,128)}, f32[2,64,4096]{2,1,0:T(8,128)}, ...) | async-done | bytes 12140560 | tf_op jit(solution)/shard_map/psum | solution.py:296
  3042.8 4.1 multiply_reduce_fusion.3
  3052.7 37.6 %all-reduce.5 = (f32[10]{0:T(128)S(1)}, f32[14336]{0:T(1024)S(1)}) all-reduce(f32[10]{0:T(128)S(1)} %concatenate.21, f32[14336]{0:T(1024)S(1)} %constant_dynamic-update-slice_fusion.6), channel_id=1, replica_groups=mesh['dp'=8,'group'=4] {'dp'}, use_global_device_ids=true, to_apply=%region_71.73 | all-reduce | flops 14346 | bytes 114768 | tf_op jit(solution)/shard_map/psum | solution.py:343
  3094.7 5.9 multiply_reduce_fusion.2
  3109.2 17.7 psum.78
  3134.3 9.1 divide_add_fusion
  (554 shorter events, 148.6 us)
Async XLA Ops:
  7.2 618.0 %all-gather.7.cloned.1.call-start = ((), (), s32[]{:S(2)}) async-start(), calls=%async_computation.7 | async-start | bytes 35168256 | tf_op jit(solution)/shard_map/all_gather | solution.py:144
  12.9 675.5 %all-gather.9.cloned.1.call-start = ((), (), s32[]{:S(2)}) async-start(), calls=%async_computation.8 | async-start | bytes 3538944 | tf_op jit(solution)/shard_map/all_gather | solution.py:152
  15.1 715.0 %all-gather.11.cloned.1.call-start = ((), (), s32[]{:S(2)}) async-start(), calls=%async_computation.9 | async-start | bytes 1179648 | tf_op jit(solution)/shard_map/all_gather | solution.py:153
  15.8 90.7 %copy-start.131 = (s32[512]{0:T(512)S(1)}, s32[512]{0:T(512)}, u32[]{:S(2)}) copy-start(s32[512]{0:T(512)} %param.22) | copy-start | bytes 6148
  15.8 840.5 %all-gather.13.cloned.1.call-start = ((), (), s32[]{:S(2)}) async-start(), calls=%async_computation.10 | async-start | bytes 9437184 | tf_op jit(solution)/shard_map/all_gather | solution.py:154
  17.0 913.6 %all-gather.15.cloned.1.call-start = ((), (), s32[]{:S(2)}) async-start(), calls=%async_computation.11 | async-start | bytes 4718592 | tf_op jit(solution)/shard_map/all_gather | solution.py:155
  18.0 1267.4 %reduce-scatter.12.cloned.1.call-start = ((), (), s32[]{:S(2)}) async-start(), calls=%async_computation.12 | async-start | bytes 1179648 | tf_op jit(solution)/shard_map/reduce_scatter | solution.py:292
  18.0 676.2 %copy-start.164 = (f32[8]{0:T(128)}, f32[8]{0:T(128)S(1)}, u32[]{:S(2)}) copy-start(f32[8]{0:T(128)S(1)} %power_negate_fusion) | copy-start | bytes 100
  102.1 526.9 %copy-start.156 = (s32[64]{0:T(128)}, s32[64]{0:T(128)S(1)}, u32[]{:S(2)}) copy-start(s32[64]{0:T(128)S(1)} %get-tuple-element.107) | copy-start | bytes 772
  104.0 857.7 %copy-start.81 = (s32[512]{0:T(512)}, s32[512]{0:T(512)S(1)}, u32[]{:S(2)}) copy-start(s32[512]{0:T(512)S(1)} %convert_reduce_fusion.1) | copy-start | bytes 6148
  104.7 857.0 %copy-start.139 = (pred[512]{0:T(512)(128)(4,1)}, pred[512]{0:T(512)(128)(4,1)S(1)}, u32[]{:S(2)}) copy-start(pred[512]{0:T(512)(128)(4,1)S(1)} %broadcast_compare_fusion.1) | copy-start | bytes 1540
  106.5 623.5 %copy-start.147 = (pred[512]{0:T(512)(128)(4,1)}, pred[512]{0:T(512)(128)(4,1)S(1)}, u32[]{:S(2)}) copy-start(pred[512]{0:T(512)(128)(4,1)S(1)} %get-tuple-element.131) | copy-start | bytes 1540
  106.5 623.5 %copy-start.149 = (pred[512]{0:T(512)(128)(4,1)}, pred[512]{0:T(512)(128)(4,1)S(1)}, u32[]{:S(2)}) copy-start(pred[512]{0:T(512)(128)(4,1)S(1)} %get-tuple-element.132) | copy-start | bytes 1540
  153.9 540.4 %copy-start.55 = (pred[512,512]{0,1:T(8,128)(4,1)}, pred[512,512]{0,1:T(8,128)(4,1)S(1)}, u32[]{:S(2)}) copy-start(pred[512,512]{0,1:T(8,128)(4,1)S(1)} %broadcast_compare_fusion) | copy-start | bytes 786436
  171.4 759.2 %copy-start.51 = (f32[512]{0:T(512)}, f32[512]{0:T(512)S(1)}, u32[]{:S(2)}) copy-start(f32[512]{0:T(512)S(1)} %get-tuple-element.63) | copy-start | bytes 6148
  171.4 779.0 %copy-start.104 = (f32[512]{0:T(512)}, f32[512]{0:T(512)S(1)}, u32[]{:S(2)}) copy-start(f32[512]{0:T(512)S(1)} %get-tuple-element.62) | copy-start | bytes 6148
  171.4 779.0 %copy-start.124 = (f32[512]{0:T(512)}, f32[512]{0:T(512)S(1)}, u32[]{:S(2)}) copy-start(f32[512]{0:T(512)S(1)} %get-tuple-element.61) | copy-start | bytes 6148
  171.4 784.0 %copy-start.53 = (f32[512]{0:T(512)}, f32[512]{0:T(512)S(1)}, u32[]{:S(2)}) copy-start(f32[512]{0:T(512)S(1)} %get-tuple-element.59) | copy-start | bytes 6148
  171.4 790.4 %copy-start.69 = (f32[512]{0:T(512)}, f32[512]{0:T(512)S(1)}, u32[]{:S(2)}) copy-start(f32[512]{0:T(512)S(1)} %get-tuple-element.55) | copy-start | bytes 6148
  171.4 790.4 %copy-start.83 = (f32[512]{0:T(512)}, f32[512]{0:T(512)S(1)}, u32[]{:S(2)}) copy-start(f32[512]{0:T(512)S(1)} %get-tuple-element.58) | copy-start | bytes 6148
  171.4 790.4 %copy-start.106 = (f32[512]{0:T(512)}, f32[512]{0:T(512)S(1)}, u32[]{:S(2)}) copy-start(f32[512]{0:T(512)S(1)} %get-tuple-element.57) | copy-start | bytes 6148
  629.2 100.8 %copy-start.32 = (bf16[512,512]{0,1:T(8,128)(2,1)}, bf16[512,512]{0,1:T(8,128)(2,1)S(1)}, u32[]{:S(2)}) copy-start(bf16[512,512]{0,1:T(8,128)(2,1)S(1)} %copy.135) | copy-start | bytes 1572868
  703.3 157.8 %copy-start.46 = (bf16[8,64,512]{2,1,0:T(8,128)(2,1)}, bf16[8,64,512]{2,1,0:T(8,128)(2,1)S(1)}, u32[]{:S(2)}) copy-start(bf16[8,64,512]{2,1,0:T(8,128)(2,1)S(1)} %fusion.85) | copy-start | bytes 1572868
  731.6 198.9 %copy-start.57 = (f32[512]{0:T(512)}, f32[512]{0:T(512)S(1)}, u32[]{:S(2)}) copy-start(f32[512]{0:T(512)S(1)} %broadcast_multiply_fusion.5) | copy-start | bytes 6148
  731.8 129.3 %copy-start.94 = (f32[512]{0:T(512)}, f32[512]{0:T(512)S(1)}, u32[]{:S(2)}) copy-start(f32[512]{0:T(512)S(1)} %multiply_reduce_fusion.23) | copy-start | bytes 6148
  731.8 198.7 %copy-start.61 = (f32[512]{0:T(512)}, f32[512]{0:T(512)S(1)}, u32[]{:S(2)}) copy-start(f32[512]{0:T(512)S(1)} %fusion.137) | copy-start | bytes 6148
  961.8 45.5 %copy-start.110 = (f32[512]{0:T(512)}, f32[512]{0:T(512)S(1)}, u32[]{:S(2)}) copy-start(f32[512]{0:T(512)S(1)} %fusion.141) | copy-start | bytes 6148
  963.4 43.8 %copy-start.112 = (bf16[4,512]{1,0:T(4,128)(2,1)}, bf16[4,512]{1,0:T(4,128)(2,1)S(1)}, u32[]{:S(2)}) copy-start(bf16[4,512]{1,0:T(4,128)(2,1)S(1)} %fusion.86) | copy-start | bytes 12292
  963.8 43.5 %copy-start.65 = (f32[4,512]{1,0:T(4,128)}, f32[4,512]{1,0:T(4,128)S(1)}, u32[]{:S(2)}) copy-start(f32[4,512]{1,0:T(4,128)S(1)} %get-tuple-element.167) | copy-start | bytes 24580
  963.8 43.5 %copy-start.158 = (f32[4]{0:T(128)}, f32[4]{0:T(128)S(1)}, u32[]{:S(2)}) copy-start(f32[4]{0:T(128)S(1)} %get-tuple-element.166) | copy-start | bytes 52
  963.8 43.5 %copy-start.146 = (f32[4]{0:T(128)}, f32[4]{0:T(128)S(1)}, u32[]{:S(2)}) copy-start(f32[4]{0:T(128)S(1)} %add_rsqrt_fusion) | copy-start | bytes 52
  1009.4 24.1 copy-start.68
  1009.4 24.1 copy-start.70
  1009.4 24.1 copy-start.72
  1009.4 24.0 copy-start.84
  1009.5 24.0 copy-start.88
  1039.3 24.6 slice-start
  1097.7 187.8 %reduce-scatter.16.cloned.1.call-start = ((), (), s32[]{:S(2)}) async-start(), calls=%async_computation.14 | async-start | bytes 2359296 | tf_op jit(solution)/shard_map/reduce_scatter | solution.py:289
  1119.3 230.4 %reduce-scatter.14.cloned.1.call-start = ((), (), s32[]{:S(2)}) async-start(), calls=%async_computation.13 | async-start | bytes 7077888 | tf_op jit(solution)/shard_map/reduce_scatter | solution.py:288
  1170.9 331.1 %reduce-scatter.20.cloned.1.call-start = ((), (), s32[]{:S(2)}) async-start(), calls=%async_computation.16 | async-start | bytes 9437184 | tf_op jit(solution)/shard_map/reduce_scatter | solution.py:291
  1179.9 606.8 %reduce-scatter.18.cloned.1.call-start = ((), (), s32[]{:S(2)}) async-start(), calls=%async_computation.15 | async-start | bytes 18874368 | tf_op jit(solution)/shard_map/reduce_scatter | solution.py:290
  1195.3 1560.2 %reduce-scatter.24.cloned.1.call-start = ((), (), s32[]{:S(2)}) async-start(), calls=%async_computation.18 | async-start | bytes 70336512
  1282.8 1536.9 %reduce-scatter.22.cloned.1.call-start = ((), (), s32[]{:S(2)}) async-start(), calls=%async_computation.17 | async-start | bytes 294912
  1285.4 1752.3 %all-reduce.9.cloned.1.call-start = ((), (), s32[]{:S(2)}) async-start(), calls=%async_computation.19 | async-start | bytes 24281088 | tf_op jit(solution)/shard_map/psum | solution.py:296
  3042.8 48.8 %copy-start.80 = (f32[2,6656]{1,0:T(2,128)S(1)}, f32[2,6656]{1,0:T(2,128)}, u32[]{:S(2)}) copy-start(f32[2,6656]{1,0:T(2,128)} %param.38) | copy-start | bytes 159748
  3042.8 51.1 %copy-start.34 = (f32[64,512]{1,0:T(8,128)S(1)}, f32[64,512]{1,0:T(8,128)}, u32[]{:S(2)}) copy-start(f32[64,512]{1,0:T(8,128)} %get-tuple-element.76) | copy-start | bytes 393220
  3047.3 47.3 %copy-start.123 = (f32[2,64]{1,0:T(2,128)}, f32[2,64]{1,0:T(2,128)S(1)}, u32[]{:S(2)}) copy-start(f32[2,64]{1,0:T(2,128)S(1)} %get-tuple-element.46) | copy-start | bytes 1540
  3047.9 46.7 %copy-start.134 = (f32[64]{0:T(128)}, f32[64]{0:T(128)S(1)}, u32[]{:S(2)}) copy-start(f32[64]{0:T(128)S(1)} %get-tuple-element.92) | copy-start | bytes 772
  (139 other events, 887.9 us)
Sparse Core Ops, SparseCore 0:
  13.0 612.1 all-gather.6
  628.0 60.4 all-gather.8
  691.2 38.8 all-gather.10
  732.7 123.6 all-gather.12
  859.0 71.5 all-gather.14
  1097.8 59.5 reduce-scatter.11
  1161.3 66.8 reduce-scatter.15
  1232.8 116.8 reduce-scatter.13
  1353.8 148.0 reduce-scatter.19
  1505.6 281.0 reduce-scatter.17
  1791.2 964.2 reduce-scatter.23
  2759.3 60.3 reduce-scatter.21
  2822.8 214.8 all-reduce.8
where the time goes:
time: 3170 us; the launch traced here: 3160 us
  waiting for transfers between devices  2470 us (78%)
  blocking collectives  231 us (7%)
  matrix products  180 us (6%)
  other arithmetic  170 us (5%)
  local copies, waits for them, and re-layouts  81.2 us (3%)
    unnamed x15, waiting for transfers between devices  1030 us
    all_gather x1, waiting for transfers between devices, shards(): lax.all_gather(embed_master.astype(jnp.bfloat16), 'dp', axis=0, tiled=True)  454 us
    reduce_scatter x1, waiting for transfers between devices, shards(): lax.psum_scatter(grad_gate_up, 'dp', scatter_dimension=1, tiled=True)  285 us
    psum x1, waiting for transfers between devices, shards(): lax.psum((owned[0], owned[1], owned[2], owned[3], owned[4], owned[5], emb...  211 us
    reduce_scatter x1, waiting for transfers between devices, shards(): lax.psum_scatter(grad_down, 'dp', scatter_dimension=1, tiled=True)  152 us
    all_gather x1, waiting for transfers between devices, shards(): lax.all_gather(ffn_in.astype(jnp.bfloat16), 'dp', axis=1, tiled=True)  125 us
    all_gather x1, blocking collectives, shards(): lax.all_gather(norm_master.astype(jnp.bfloat16), 'dp', axis=2, tiled=True)  80.8 us
    reduce_scatter x1, waiting for transfers between devices, shards(): lax.psum_scatter(grad_qkv, 'dp', scatter_dimension=1, tiled=True)  64.3 us
  transfers between devices with their start and end apart: 13, of which 11 were waited for; matrix products, arithmetic and copies ran while one was open for 8% of the time, Pallas kernels for 0%

commit v1 on v0

--- a/solution.py
+++ b/solution.py
@@ -1,6 +1,10 @@
+import functools
+
 import jax
 import jax.numpy as jnp
 from jax import lax
+from jax.experimental import pallas as pl
+from jax.experimental.pallas import tpu as pltpu
 from jax.sharding import PartitionSpec as P
 
 D = 512
@@ -416,6 +420,692 @@
     )
 
 
+MESH = pl.DeviceIdType.MESH
+BF=jnp.bfloat16
+
+def place():
+    dp = lax.axis_index("dp"); g = lax.axis_index("group")
+    return dp // 2, dp % 2, g // 2, g % 2
+
+def dev(z, x, y, c):
+    return (z * 2 + x, y * 2 + c)
+
+def entry_barrier(peers):
+    bar = pltpu.get_barrier_semaphore()
+    for p in peers:
+        pl.semaphore_signal(bar, inc=1, device_id=p, device_id_type=MESH)
+    pl.semaphore_wait(bar, len(peers))
+
+def mult(v, m=16):
+    return pl.multiple_of(v, m)
+
+def gather_kernel(chunks, w_ref, rows_ref, ag_ref, got_ref, zs, zr, xs, xr, ys, yr, cs, cr, ls, es, er):
+    z, x, y, c = place()
+    me = z * 2 + x
+    ep = [(lax.rem(me + k, 8), y * 2 + c) for k in range(8)]
+    zp = [dev((z + k) % 4, x, y, c) for k in range(4)]
+    xp, yp, cp = dev(z, 1 - x, y, c), dev(z, x, 1 - y, c), dev(z, x, y, 1 - c)
+    entry_barrier(ep[1:] + [yp, cp])
+    Q = len(chunks)
+    hs = [mult(b + c * h + y * nb) for b, h, nb in chunks]
+    nh = [h - nb for b, h, nb in chunks]
+    bs = [mult(b + c * h + y * (h - nb)) for b, h, nb in chunks]
+    nbs = [nb for b, h, nb in chunks]
+    cb = [mult(b + c * h) for b, h, nb in chunks]
+    nc = [h for b, h, nb in chunks]
+    def rc(src, dst, s, r, d):
+        return pltpu.make_async_remote_copy(src, dst, s, r, device_id=d, device_id_type=MESH)
+    def shard(k, f):
+        return ((z + 4 - k) % 4) * 2 + (x if f == 0 else 1 - x)
+    own = pltpu.make_async_copy(w_ref, ag_ref.at[me], ls.at[0])
+    own.start()
+    kept = pltpu.make_async_copy(rows_ref.at[me], got_ref.at[me], ls.at[1])
+    kept.start()
+    ec = [rc(rows_ref.at[ep[k][0]], got_ref.at[me], es.at[k], er.at[k], ep[k]) for k in range(1, 8)]
+    for copy in ec:
+        copy.start()
+    zc = {}; xc = {}; yc = {}; cc = {}
+    for q in range(Q):
+        for k in range(1, 4):
+            zc[q, k] = rc(w_ref.at[pl.ds(hs[q], nh[q])], ag_ref.at[me, pl.ds(hs[q], nh[q])], zs.at[q, k], zr.at[q, k], zp[k])
+        for k in range(4):
+            src = w_ref.at[pl.ds(hs[q], nh[q])] if k == 0 else ag_ref.at[shard(k, 0), pl.ds(hs[q], nh[q])]
+            xc[q, k] = rc(src, ag_ref.at[shard(k, 0), pl.ds(hs[q], nh[q])], xs.at[q, k], xr.at[q, k], xp)
+        for k in range(4):
+            for f in range(2):
+                if k == 0 and f == 0: continue
+                s = shard(k, f)
+                yc[q, k, f] = rc(ag_ref.at[s, pl.ds(bs[q], nbs[q])], ag_ref.at[s, pl.ds(bs[q], nbs[q])], ys.at[q, 2 * k + f], yr.at[q, 2 * k + f], yp)
+                cc[q, k, f] = rc(ag_ref.at[s, pl.ds(cb[q], nc[q])], ag_ref.at[s, pl.ds(cb[q], nc[q])], cs.at[q, 2 * k + f], cr.at[q, 2 * k + f], cp)
+    def s0(q):
+        for k in (2, 1, 3):
+            zc[q, k].start()
+        xc[q, 0].start()
+    def s1(q):
+        for k in (1, 3, 2):
+            zc[q, k].wait_recv()
+            xc[q, k].start()
+            yc[q, k, 0].start()
+    def s2(q):
+        for k in (0, 1, 3, 2):
+            xc[q, k].wait_recv()
+            yc[q, k, 1].start()
+    def s3(q):
+        for k, f in ((1, 0), (3, 0), (2, 0), (0, 1), (1, 1), (3, 1), (2, 1)):
+            yc[q, k, f].wait_recv()
+            cc[q, k, f].start()
+    st = [s0, s1, s2, s3]
+    for t in range(Q + 3):
+        for i in reversed(range(4)):
+            q = t - i
+            if 0 <= q < Q:
+                st[i](q)
+    for q in range(Q):
+        for k in range(4):
+            for f in range(2):
+                if k or f: cc[q, k, f].wait_recv()
+    for d in (zc, xc, cc) + (yc,):
+        for v in d.values(): v.wait_send()
+    for copy in ec:
+        copy.wait()
+    own.wait()
+    kept.wait()
+
+def gather_weights(w, rows, chunks, cid=1):
+    Q = len(chunks)
+    D = pltpu.SemaphoreType.DMA
+    return pl.pallas_call(
+        functools.partial(gather_kernel, chunks),
+        out_shape=(jax.ShapeDtypeStruct((8,) + w.shape, w.dtype), jax.ShapeDtypeStruct(rows.shape, rows.dtype)),
+        in_specs=[pl.BlockSpec(memory_space=pl.ANY)] * 2, out_specs=[pl.BlockSpec(memory_space=pl.ANY)] * 2,
+        scratch_shapes=[D((Q, 4)), D((Q, 4)), D((Q, 4)), D((Q, 4)), D((Q, 8)), D((Q, 8)), D((Q, 8)), D((Q, 8)), D((2,)), D((8,)), D((8,))],
+        compiler_params=pltpu.CompilerParams(collective_id=cid, has_side_effects=True),
+    )(w, rows)
+
+def spread_kernel(v_ref, o_ref, ss, rs, ls):
+    lin = lax.axis_index("dp") * 4 + lax.axis_index("group")
+    peers = [lax.rem(lin + k, 32) for k in range(32)]
+    peers = [(p // 4, p % 4) for p in peers]
+    entry_barrier(peers[1:])
+    copies = [pltpu.make_async_remote_copy(v_ref, o_ref.at[lin], ss.at[k], rs.at[k], device_id=peers[k], device_id_type=MESH) for k in range(1, 32)]
+    for copy in copies:
+        copy.start()
+    own = pltpu.make_async_copy(v_ref, o_ref.at[lin], ls)
+    own.start()
+    for copy in copies:
+        copy.wait()
+    own.wait()
+
+def spread(v, cid):
+    D = pltpu.SemaphoreType.DMA
+    return pl.pallas_call(
+        spread_kernel,
+        out_shape=jax.ShapeDtypeStruct((32,) + v.shape, v.dtype),
+        in_specs=[pl.BlockSpec(memory_space=pltpu.VMEM)], out_specs=pl.BlockSpec(memory_space=pltpu.VMEM),
+        scratch_shapes=[D((32,)), D((32,)), D],
+        compiler_params=pltpu.CompilerParams(collective_id=cid, has_side_effects=True),
+    )(v)
+
+def scatter_kernel(chunks, g_ref, e_ref, out_ref, t_ref, acc, b1, b2, b3, b4, b5, fin,
+                   cs, cr, ys, yr, xs, xr, zs, zr, as_, ar, fs, fr, ls, os_, es, er, el):
+    z, x, y, c = place()
+    me = z * 2 + x
+    g = y * 2 + c
+    ep = [(lax.rem(me + k, 8), g) for k in range(8)]
+    zp = [dev((z + k) % 4, x, y, c) for k in range(4)]
+    xp, yp, cp = dev(z, 1 - x, y, c), dev(z, x, 1 - y, c), dev(z, x, y, 1 - c)
+    entry_barrier(ep[1:] + [yp, cp])
+    Q = len(chunks)
+    lo = []; o = 0; lb = []; ob = 0; lh = []; oh = 0; la = []; oa = 0
+    for b, h, nb in chunks:
+        lo.append(o); o += h
+        lb.append(ob); ob += nb
+        lh.append(oh); oh += h - nb
+        la.append(oa); oa += h - 2 * nb
+    nh = [h - nb for b, h, nb in chunks]
+    nbs = [nb for b, h, nb in chunks]
+    na = [h - 2 * nb for b, h, nb in chunks]
+    hs = [mult(lo[q] + y * nbs[q]) for q in range(Q)]
+    mb = [mult(lo[q] + y * nh[q]) for q in range(Q)]
+    ob_ = [mult(lo[q] + (1 - y) * nh[q]) for q in range(Q)]
+    aa = [lo[q] + nbs[q] for q in range(Q)]
+    def rc(src, dst, s, r, d):
+        return pltpu.make_async_remote_copy(src, dst, s, r, device_id=d, device_id_type=MESH)
+    def add(dst, src, n, blk=16):
+        def body(i, _):
+            a = mult(i * blk)
+            d = dst(a, blk); s = src(a, blk)
+            d[...] = (d[...].astype(jnp.float32) + s[...].astype(jnp.float32)).astype(BF)
+            return _
+        lax.fori_loop(0, n // blk, body, 0)
+    order = []
+    for k in (2, 1, 3, 0):
+        for f in (1, 0):
+            order.append((k, f))
+    def owner(k, f):
+        return ((z + k) % 4) * 2 + (x if f == 0 else 1 - x)
+    C1 = {}; Y = {}; X = {}; Z = {}; A = {}; F = {}; L = {}; O = {}; BX = {}
+    for q, (b, h, nb) in enumerate(chunks):
+        for i, (k, f) in enumerate(order):
+            s = owner(k, f)
+            L[q, i] = pltpu.make_async_copy(g_ref.at[s, pl.ds(mult(b + c * h), h)], acc.at[s, pl.ds(lo[q], h)], ls.at[q, i])
+            C1[q, i] = rc(g_ref.at[s, pl.ds(mult(b + (1 - c) * h), h)], b1.at[s, pl.ds(lo[q], h)], cs.at[q, i], cr.at[q, i], cp)
+            Y[q, i] = rc(acc.at[s, pl.ds(ob_[q], nb)], b2.at[s, pl.ds(lb[q], nb)], ys.at[q, i], yr.at[q, i], yp)
+        for k in range(4):
+            X[q, k] = rc(acc.at[owner(k, 1), pl.ds(hs[q], nh[q])], b3.at[k, pl.ds(lh[q], nh[q])], xs.at[q, k], xr.at[q, k], xp)
+            if k:
+                Z[q, k] = rc(acc.at[owner(k, 0), pl.ds(hs[q], nh[q])], b4.at[k - 1, pl.ds(lh[q], nh[q])], zs.at[q, k], zr.at[q, k], zp[k])
+        A[q] = rc(fin.at[pl.ds(aa[q], na[q])], b5.at[pl.ds(la[q], na[q])], as_.at[q, 0], ar.at[q, 0], yp)
+        BX[q] = rc(fin.at[pl.ds(mb[q], nb)], fin.at[pl.ds(mb[q], nb)], as_.at[q, 1], ar.at[q, 1], yp)
+        F[q] = rc(fin.at[pl.ds(lo[q], h)], out_ref.at[pl.ds(mult(b + c * h), h)], fs.at[q], fr.at[q], cp)
+        O[q] = pltpu.make_async_copy(fin.at[pl.ds(lo[q], h)], out_ref.at[pl.ds(mult(b + c * h), h)], os_.at[q])
+    g2 = (1 - y) * 2 + c
+    kept = pltpu.make_async_copy(e_ref.at[me], t_ref.at[g, me], el)
+    E = [rc(e_ref.at[ep[k][0]], t_ref.at[g, me], es.at[k], er.at[k], ep[k]) for k in range(1, 8)]
+    EY = rc(t_ref.at[g], t_ref.at[g], es.at[8], er.at[8], yp)
+    EC = rc(t_ref.at[g], t_ref.at[g], es.at[9], er.at[9], cp)
+    ED = rc(t_ref.at[g2], t_ref.at[g2], es.at[10], er.at[10], cp)
+    def e0():
+        kept.start()
+        for v in E: v.start()
+    def e1():
+        kept.wait()
+        for v in E: v.wait_recv()
+        EY.start(); EC.start()
+    def e2():
+        EY.wait_recv()
+        ED.start()
+    def e3():
+        EC.wait_recv(); ED.wait_recv()
+        for v in E + [EY, EC, ED]: v.wait_send()
+    ev = {0: e0, 3: e1, 5: e2}
+    def s0(q):
+        for i in range(8):
+            L[q, i].start(); C1[q, i].start()
+    def s1(q):
+        h = chunks[q][1]
+        for i, (k, f) in enumerate(order):
+            s = owner(k, f)
+            L[q, i].wait(); C1[q, i].wait_recv()
+            add(lambda a, n: acc.at[s, pl.ds(lo[q] + a, n)], lambda a, n: b1.at[s, pl.ds(lo[q] + a, n)], h)
+            Y[q, i].start()
+    def s2(q):
+        for i, (k, f) in enumerate(order):
+            s = owner(k, f)
+            if nbs[q]:
+                Y[q, i].wait_recv()
+                add(lambda a, n: acc.at[s, pl.ds(mb[q] + a, n)], lambda a, n: b2.at[s, pl.ds(lb[q] + a, n)], nbs[q])
+            if f == 1:
+                X[q, k].start()
+    def s3(q):
+        for k in (2, 1, 3, 0):
+            s = owner(k, 0)
+            X[q, k].wait_recv()
+            add(lambda a, n: acc.at[s, pl.ds(hs[q] + a, n)], lambda a, n: b3.at[k, pl.ds(lh[q] + a, n)], nh[q])
+            if k: Z[q, k].start()
+    def s4(q):
+        for k in range(1, 4):
+            Z[q, k].wait_recv()
+        def body(i, _):
+            a = mult(i * 16)
+            t = acc[me, pl.ds(hs[q] + a, 16)].astype(jnp.float32)
+            for k in range(3):
+                t += b4[k, pl.ds(lh[q] + a, 16)].astype(jnp.float32)
+            fin[pl.ds(hs[q] + a, 16)] = t.astype(BF)
+            return _
+        lax.fori_loop(0, nh[q] // 16, body, 0)
+        A[q].start()
+        BX[q].start()
+    def s5(q):
+        A[q].wait_recv()
+        A[q].wait_send()
+        add(lambda a, n: fin.at[pl.ds(aa[q] + a, n)], lambda a, n: b5.at[pl.ds(la[q] + a, n)], na[q])
+        BX[q].wait_recv()
+        F[q].start(); O[q].start()
+    st = [s0, s1, s2, s3, s4, s5]
+    for t in range(Q + 5):
+        if t in ev: ev[t]()
+        for i in reversed(range(6)):
+            q = t - i
+            if 0 <= q < Q:
+                st[i](q)
+    for q in range(Q):
+        F[q].wait(); O[q].wait()
+        BX[q].wait_send()
+    for d in (C1, Y, X, Z):
+        for v in d.values(): v.wait_send()
+    e3()
+
+def scatter_grads(g, e, chunks, cid=2):
+    Q = len(chunks)
+    D = pltpu.SemaphoreType.DMA
+    H = sum(h for _, h, _ in chunks); NB = sum(nb for _, _, nb in chunks); NH = H - NB
+    V = lambda *s: pltpu.VMEM(s, BF)
+    return pl.pallas_call(
+        functools.partial(scatter_kernel, chunks),
+        out_shape=(jax.ShapeDtypeStruct(g.shape[1:], g.dtype), jax.ShapeDtypeStruct((4,) + e.shape, e.dtype)),
+        in_specs=[pl.BlockSpec(memory_space=pl.ANY)] * 2, out_specs=[pl.BlockSpec(memory_space=pl.ANY)] * 2,
+        scratch_shapes=[V(8, H, 512), V(8, H, 512), V(8, NB, 512), V(4, NH, 512), V(3, NH, 512), V(H - 2 * NB, 512), V(H, 512),
+            D((Q, 8)), D((Q, 8)), D((Q, 8)), D((Q, 8)), D((Q, 4)), D((Q, 4)), D((Q, 4)), D((Q, 4)), D((Q, 2)), D((Q, 2)), D((Q,)), D((Q,)), D((Q, 8)), D((Q,)),
+            D((11,)), D((11,)), D],
+        compiler_params=pltpu.CompilerParams(collective_id=cid, has_side_effects=True, vmem_limit_bytes=60 * 2**20),
+    )(g, e)
+
+def plan(rows, count, share):
+    units = rows // 32
+    chunks = []
+    base = 0
+    for i in range(count):
+        size = units // count + (1 if i < units % count else 0)
+        chunks.append((base, 16 * size, 16 * int(round(size * share))))
+        base += 32 * size
+    return chunks
+
+
+SLOTS = 96
+PART = 1024
+HEAD_AT = 2 * PART
+NORM_AT = HEAD_AT + 64
+PACKED = NORM_AT + 32
+
+
+def slot_plan(token_ids, shard_rows):
+    tokens = token_ids.shape[0]
+    owner = token_ids // shard_rows
+    local = token_ids - owner * shard_rows
+    index = jnp.arange(tokens, dtype=jnp.int32)
+    same_id = token_ids[:, None] == token_ids[None, :]
+    first = jnp.min(jnp.where(same_id, index[None, :], tokens), axis=1)
+    leads = first == index
+    same_owner = owner[:, None] == owner[None, :]
+    slot = jnp.sum(
+        (same_owner & leads[None, :] & (index[None, :] < first[:, None])).astype(jnp.int32), axis=1
+    )
+    key = jnp.where(slot < SLOTS, owner * SLOTS + slot, 8 * SLOTS)
+    wanted = jnp.max(
+        jnp.where(
+            key[:, None] == jnp.arange(8 * SLOTS, dtype=jnp.int32)[None, :], local[:, None], -1
+        ),
+        axis=0,
+    )
+    return key, wanted, jnp.max(slot)
+
+
+def column_blocks(rows):
+    lead, count, width = rows.shape
+    return (
+        rows.reshape(lead, count, width // D, D).transpose(0, 2, 1, 3).reshape(lead, -1, D)
+    )
+
+
+def pack_weights(attn_in, attn_out, ffn_in, ffn_out, head_master, norm_master):
+    layers = jnp.concatenate(
+        [column_blocks(attn_in), attn_out, column_blocks(ffn_in), ffn_out], axis=1
+    ).astype(jnp.bfloat16)
+    norm_rows = jnp.pad(
+        norm_master.reshape(10, -1).astype(jnp.bfloat16), ((0, 22), (0, D - norm_master.shape[2]))
+    )
+    return jnp.concatenate(
+        [layers.reshape(-1, D), head_master.astype(jnp.bfloat16), norm_rows], axis=0
+    )
+
+
+def whole_columns(part, blocks):
+    return (
+        part.reshape(8, blocks, -1, D).transpose(0, 2, 1, 3).reshape(-1, blocks * D)
+    )
+
+
+def shard_columns(part, blocks):
+    return part.reshape(blocks, -1, D).transpose(1, 0, 2).reshape(-1, blocks * D)
+
+
+def owned_columns(grad):
+    rows, width = grad.shape
+    return (
+        grad.reshape(8, rows // 8, width // D, D).transpose(0, 2, 1, 3).reshape(8, -1, D)
+    )
+
+
+def place_kernel(slot_ref, rows_ref, out_ref):
+    start = pl.program_id(0) * out_ref.shape[0]
+    rows = lax.broadcasted_iota(jnp.int32, (out_ref.shape[0], slot_ref.shape[1]), 0) + start
+    picks = jnp.where(rows == slot_ref[...], 1.0, 0.0).astype(jnp.bfloat16)
+    out_ref[...] = jnp.dot(picks, rows_ref[...], preferred_element_type=jnp.float32)
+
+
+def place_rows(slots, rows, row_count):
+    tile = row_count // 9
+    return pl.pallas_call(
+        place_kernel,
+        grid=(9,),
+        in_specs=[
+            pl.BlockSpec((1, slots.shape[1]), lambda i: (0, 0)),
+            pl.BlockSpec(rows.shape, lambda i: (0, 0)),
+        ],
+        out_specs=pl.BlockSpec((tile, D), lambda i: (i, 0)),
+        out_shape=jax.ShapeDtypeStruct((row_count, D), jnp.float32),
+        compiler_params=pltpu.CompilerParams(vmem_limit_bytes=48 * 2**20),
+    )(slots, rows)
+
+
+def fast_shards(
+    token_ids,
+    seq_lengths,
+    valid_mask,
+    deal_order,
+    log_scale,
+    embed_master,
+    attn_in,
+    attn_out,
+    ffn_in,
+    ffn_out,
+    head_master,
+    norm_master,
+    embed_rows,
+    head_rows,
+    layer_rows,
+    ffn_out_rows,
+    layer_cols,
+    embed_head_cols,
+    norm_state,
+    scale_state,
+):
+    tokens = token_ids.shape[0]
+    seq_count = seq_lengths.shape[1]
+    head_count = HEADS
+    shard_rows = embed_master.shape[0]
+    my_dp = lax.axis_index("dp")
+    my_group = lax.axis_index("group")
+    position = jnp.arange(tokens, dtype=jnp.int32)
+    bounds = jnp.cumsum(seq_lengths[0])
+    segment = jnp.sum((position[:, None] >= bounds[None, :]).astype(jnp.int32), axis=1)
+
+    key, wanted, most = slot_plan(token_ids, shard_rows)
+    request = jnp.concatenate(
+        [wanted.reshape(-1, 128), jnp.broadcast_to(most, (2, 128))], axis=0
+    ).astype(jnp.int32)
+    requests = spread(request, 0)
+    crowded = jnp.max(requests[:, 6]) >= SLOTS
+    asked = requests[:, :6].reshape(32, 8, SLOTS)
+    asked_here = lax.dynamic_index_in_dim(asked, my_dp, 1, keepdims=False)
+    group_asks = asked_here.reshape(8, 4, SLOTS)
+    to_send = lax.dynamic_index_in_dim(group_asks, my_group, 1, keepdims=False)
+    sent_rows = jnp.take(
+        embed_master, jnp.clip(to_send.reshape(-1), 0, shard_rows - 1), axis=0
+    ).astype(jnp.bfloat16)
+    packed = pack_weights(attn_in, attn_out, ffn_in, ffn_out, head_master, norm_master)
+    weights, got_rows = gather_weights(
+        packed, sent_rows.reshape(8, SLOTS, D), plan(PACKED, 4, 0.36)
+    )
+
+    def dense_rows():
+        table = lax.all_gather(embed_master.astype(jnp.bfloat16), "dp", axis=0, tiled=True)
+        return jnp.take(table, token_ids, axis=0)
+
+    def slot_rows():
+        return jnp.take(got_rows.reshape(-1, D), jnp.minimum(key, 8 * SLOTS - 1), axis=0)
+
+    stream = lax.cond(crowded, dense_rows, slot_rows).astype(jnp.float32)
+    w_qkv = [whole_columns(weights[:, l * PART : l * PART + 192], 3) for l in range(LAYERS)]
+    w_attn = [weights[:, l * PART + 192 : l * PART + 256].reshape(D, D) for l in range(LAYERS)]
+    w_gate_up = [whole_columns(weights[:, l * PART + 256 : l * PART + 768], 8) for l in range(LAYERS)]
+    w_down = [weights[:, l * PART + 768 : l * PART + 1024].reshape(FF, D) for l in range(LAYERS)]
+    w_head = weights[:, HEAD_AT : HEAD_AT + 64].reshape(D, D)
+    norms = (
+        weights[:, NORM_AT : NORM_AT + 10, :64]
+        .transpose(1, 0, 2)
+        .reshape(5, 2, D)
+        .astype(jnp.float32)
+    )
+    kept_list = []
+    for layer_idx in range(LAYERS):
+        stream_low = stream.astype(jnp.bfloat16)
+        qkv_low = jnp.dot(stream_low, w_qkv[layer_idx], preferred_element_type=jnp.float32).astype(
+            jnp.bfloat16
+        )
+        mixed_heads, lse_all = attend(qkv_low, segment, head_count)
+        mixed_low = mixed_heads.astype(jnp.bfloat16)
+        resid_one = stream + jnp.dot(
+            mixed_low, w_attn[layer_idx], preferred_element_type=jnp.float32
+        )
+        normed = layer_norm(resid_one, norms[2 * layer_idx, 0], norms[2 * layer_idx, 1])
+        normed_low = normed.astype(jnp.bfloat16)
+        joined = jnp.dot(normed_low, w_gate_up[layer_idx], preferred_element_type=jnp.float32)
+        hidden_low = geglu(joined).astype(jnp.bfloat16)
+        resid_two = normed + jnp.dot(
+            hidden_low, w_down[layer_idx], preferred_element_type=jnp.float32
+        )
+        kept_list.append(
+            (
+                stream_low,
+                qkv_low,
+                lse_all,
+                mixed_low,
+                resid_one,
+                normed_low,
+                joined,
+                hidden_low,
+                resid_two,
+            )
+        )
+        stream = layer_norm(resid_two, norms[2 * layer_idx + 1, 0], norms[2 * layer_idx + 1, 1])
+    final = layer_norm(stream, norms[2 * LAYERS, 0], norms[2 * LAYERS, 1])
+    member = (
+        (segment[None, :] == jnp.arange(seq_count, dtype=jnp.int32)[:, None])
+        & (valid_mask[None, :] > 0)
+    ).astype(jnp.float32)
+    counts = jnp.maximum(jnp.sum(member, axis=1), 1.0)
+    pooled = jnp.matmul(member, final, precision=lax.Precision.HIGHEST) / counts[:, None]
+    pooled_low = pooled.astype(jnp.bfloat16)
+    head_out = jnp.dot(pooled_low, w_head, preferred_element_type=jnp.float32)
+    unit_vecs, unit_back = jax.vjp(normalize, head_out)
+    unit_every = spread(unit_vecs, 3).reshape(-1, D)
+    loss_value, loss_back = jax.vjp(
+        lambda unit_all, scale_arg: contrast(unit_all, scale_arg, deal_order), unit_every, log_scale
+    )
+    grad_units, grad_scale = loss_back(jnp.ones_like(loss_value))
+    own_rows = lax.dynamic_slice_in_dim(
+        grad_units, lax.axis_index(("dp", "group")) * seq_count, seq_count, 0
+    )
+    grad_head_out = unit_back(own_rows)[0].astype(jnp.bfloat16)
+    grad_head = jnp.dot(pooled_low.T, grad_head_out, preferred_element_type=jnp.float32)
+    grad_pooled = jnp.dot(grad_head_out, w_head.T, preferred_element_type=jnp.float32)
+    grad_final = jnp.matmul(
+        member.T, grad_pooled / counts[:, None], precision=lax.Precision.HIGHEST
+    )
+    final_back = jax.vjp(layer_norm, stream, norms[2 * LAYERS, 0], norms[2 * LAYERS, 1])[1]
+    grad_stream, gain_last, shift_last = final_back(grad_final)
+    norm_grads = [None] * (2 * LAYERS + 1)
+    norm_grads[2 * LAYERS] = jnp.stack([gain_last, shift_last])
+    packed_grads = [None] * LAYERS
+    for layer_idx in reversed(range(LAYERS)):
+        (
+            stream_low,
+            qkv_low,
+            lse_all,
+            mixed_low,
+            resid_one,
+            normed_low,
+            joined,
+            hidden_low,
+            resid_two,
+        ) = kept_list[layer_idx]
+        norm_two_back = jax.vjp(
+            layer_norm, resid_two, norms[2 * layer_idx + 1, 0], norms[2 * layer_idx + 1, 1]
+        )[1]
+        grad_two, gain_two, shift_two = norm_two_back(grad_stream)
+        norm_grads[2 * layer_idx + 1] = jnp.stack([gain_two, shift_two])
+        grad_branch = grad_two.astype(jnp.bfloat16)
+        down_grad = jnp.dot(hidden_low.T, grad_branch, preferred_element_type=jnp.float32)
+        grad_hidden = jnp.dot(grad_branch, w_down[layer_idx].T, preferred_element_type=jnp.float32)
+        grad_joined = jax.vjp(geglu, joined)[1](grad_hidden)[0].astype(jnp.bfloat16)
+        gate_grad = jnp.dot(normed_low.T, grad_joined, preferred_element_type=jnp.float32)
+        grad_normed = grad_two + jnp.dot(
+            grad_joined, w_gate_up[layer_idx].T, preferred_element_type=jnp.float32
+        )
+        norm_one_back = jax.vjp(
+            layer_norm, resid_one, norms[2 * layer_idx, 0], norms[2 * layer_idx, 1]
+        )[1]
+        grad_one, gain_one, shift_one = norm_one_back(grad_normed)
+        norm_grads[2 * layer_idx] = jnp.stack([gain_one, shift_one])
+        grad_attended = grad_one.astype(jnp.bfloat16)
+        attn_grad = jnp.dot(mixed_low.T, grad_attended, preferred_element_type=jnp.float32)
+        grad_mixed = jnp.dot(
+            grad_attended, w_attn[layer_idx].T, preferred_element_type=jnp.float32
+        ).astype(jnp.bfloat16)
+        grad_qkv_low = attend_back(qkv_low, segment, head_count, lse_all, grad_mixed)
+        qkv_grad = jnp.dot(stream_low.T, grad_qkv_low, preferred_element_type=jnp.float32)
+        grad_stream = grad_one + jnp.dot(
+            grad_qkv_low, w_qkv[layer_idx].T, preferred_element_type=jnp.float32
+        )
+        packed_grads[layer_idx] = jnp.concatenate(
+            [
+                owned_columns(qkv_grad),
+                owned_columns(attn_grad),
+                owned_columns(gate_grad),
+                down_grad.reshape(8, -1, D),
+            ],
+            axis=1,
+        ).astype(jnp.bfloat16)
+    head_part = owned_columns(grad_head).astype(jnp.bfloat16)
+    all_grads = jnp.concatenate(
+        packed_grads + [head_part, jnp.zeros((8, PACKED - NORM_AT, D), jnp.bfloat16)], axis=1
+    )
+    slot_grads = jnp.dot(
+        (jnp.arange(8 * SLOTS, dtype=jnp.int32)[:, None] == key[None, :]).astype(jnp.bfloat16),
+        grad_stream.astype(jnp.bfloat16),
+        preferred_element_type=jnp.float32,
+    ).astype(jnp.bfloat16)
+    shard_grads, table_rows = scatter_grads(
+        all_grads, slot_grads.reshape(8, SLOTS, D), plan(PACKED, 4, 0.29)
+    )
+    table_slots = asked_here.reshape(8, 4, SLOTS).transpose(1, 0, 2).reshape(1, -1)
+
+    def dense_grad():
+        total = jnp.zeros((shard_rows * 8, D), jnp.float32).at[token_ids].add(grad_stream)
+        return lax.psum(
+            lax.psum_scatter(total, "dp", scatter_dimension=0, tiled=True), "group"
+        )
+
+    def slot_grad():
+        return place_rows(table_slots, table_rows.reshape(-1, D), shard_rows)
+
+    shard_embed = lax.cond(crowded, dense_grad, slot_grad)
+    shard_full = shard_grads.astype(jnp.float32)
+    shard_layers = shard_full[:HEAD_AT].reshape(LAYERS, PART, D)
+    shard_qkv = jnp.stack([shard_columns(shard_layers[l, :192], 3) for l in range(LAYERS)])
+    shard_attn = shard_layers[:, 192:256]
+    shard_gate_up = jnp.stack([shard_columns(shard_layers[l, 256:768], 8) for l in range(LAYERS)])
+    shard_down = shard_layers[:, 768:]
+    shard_head = shard_full[HEAD_AT : HEAD_AT + 64]
+    grad_list = [
+        shard_embed[None],
+        shard_head[None],
+        shard_qkv,
+        shard_attn,
+        shard_gate_up,
+        shard_down,
+    ]
+    master_list = [embed_master[None], head_master[None], attn_in, attn_out, ffn_in, ffn_out]
+    state_list = [
+        embed_rows[None],
+        head_rows[None],
+        layer_rows[:, 0],
+        layer_rows[:, 1],
+        layer_rows[:, 2],
+        ffn_out_rows,
+    ]
+    col_list = [
+        embed_head_cols[0:1],
+        embed_head_cols[1:2],
+        layer_cols[:, : 3 * D],
+        layer_cols[:, 3 * D : 4 * D],
+        layer_cols[:, 4 * D : 4 * D + 2 * FF],
+        layer_cols[:, 4 * D + 2 * FF :],
+    ]
+    total_rows = [VOCAB, D, D, D, D, FF]
+    wide_rate = RATE_SCALE / D**0.5
+    rates = [
+        RATE_SCALE,
+        wide_rate,
+        wide_rate,
+        RATE_SCALE / (D // 8) ** 0.5,
+        wide_rate,
+        RATE_SCALE / FF**0.5,
+    ]
+    square_list = [grad_part * grad_part for grad_part in grad_list]
+    rows_new = [
+        DECAY_RATE * state_list[i]
+        + (1.0 - DECAY_RATE) * (jnp.mean(square_list[i], axis=-1) + STATE_EPS)
+        for i in range(6)
+    ]
+    col_parts = jnp.concatenate([jnp.sum(part, axis=1).reshape(-1) for part in square_list])
+    step_parts = jnp.concatenate(
+        [
+            jnp.sum(square_list[i] * (1.0 / rows_new[i])[:, :, None], axis=1).reshape(-1)
+            for i in range(6)
+        ]
+    )
+    row_parts = jnp.concatenate([jnp.sum(part, axis=-1) for part in rows_new])
+    col_sum, step_sum, row_sum, norm_grad = lax.psum(
+        (0.25 * col_parts, 0.25 * step_parts, 0.25 * row_parts, jnp.stack(norm_grads)),
+        ("dp", "group"),
+    )
+    shard_norm = lax.dynamic_slice_in_dim(norm_grad, my_dp * 64, 64, 2)
+    cols_new = []
+    new_weights = []
+    rms_list = []
+    lead_start = 0
+    col_start = 0
+    for i in range(6):
+        lead_count, _, col_width = grad_list[i].shape
+        span = slice(col_start, col_start + lead_count * col_width)
+        row_mean = row_sum[lead_start : lead_start + lead_count] / total_rows[i]
+        col_state_new = DECAY_RATE * col_list[i] + (1.0 - DECAY_RATE) * (
+            col_sum[span].reshape(lead_count, col_width) / total_rows[i] + STATE_EPS
+        )
+        cols_new.append(col_state_new)
+        step_total = jnp.sum(
+            step_sum[span].reshape(lead_count, col_width) * row_mean[:, None] / col_state_new,
+            axis=1,
+        )
+        step_rms = jnp.sqrt(step_total / (total_rows[i] * col_width))
+        rms_list.append(step_rms)
+        row_factor = lax.rsqrt(rows_new[i] / row_mean[:, None]) * (
+            -rates[i] / jnp.maximum(1.0, step_rms / CLIP_LEVEL)[:, None]
+        )
+        new_weights.append(
+            master_list[i]
+            + grad_list[i] * row_factor[:, :, None] * lax.rsqrt(col_state_new)[:, None, :]
+        )
+        lead_start = lead_start + lead_count
+        col_start = col_start + lead_count * col_width
+    norm_delta, norm_second = unfactored(shard_norm, norm_state)
+    scale_delta, scale_state_new = unfactored(grad_scale, scale_state)
+    return (
+        loss_value,
+        new_weights[0][0],
+        new_weights[2],
+        new_weights[3],
+        new_weights[4],
+        new_weights[5],
+        new_weights[1][0],
+        norm_master + norm_delta,
+        log_scale + scale_delta,
+        rows_new[0][0],
+        rows_new[1][0],
+        jnp.stack([rows_new[2], rows_new[3], rows_new[4]], axis=1),
+        rows_new[5],
+        jnp.concatenate([cols_new[2], cols_new[3], cols_new[4], cols_new[5]], axis=1),
+        cols_new[0][0],
+        cols_new[1][0],
+        norm_second,
+        scale_state_new,
+        jnp.concatenate(rms_list),
+    )
+
+
 def solution(mesh):
     in_specs = (
         P(("dp", "group")),
@@ -460,4 +1150,5 @@
         P(),
         P(),
     )
-    return jax.shard_map(shards, mesh=mesh, in_specs=in_specs, out_specs=out_specs, check_vma=False)
+    body = fast_shards if dict(mesh.shape) == {"dp": 8, "group": 4} else shards
+    return jax.shard_map(body, mesh=mesh, in_specs=in_specs, out_specs=out_specs, check_vma=False)

time: 3170 us -> 802 us (0.25)
  waiting for transfers between devices: 2470 us -> 120 us
  Pallas kernels: 0 us -> 265 us
  blocking collectives: 231 us -> 0 us
  other arithmetic: 170 us -> 96.2 us
  local copies, waits for them, and re-layouts: 81.2 us -> 116 us
    unnamed x15 -> x1, waiting for transfers between devices: 1030 us -> 0.02 us
    all_gather x5 -> x0, waiting for transfers between devices: 728 us -> none  [the longest x1 454 us: shards(): lax.all_gather(embed_master.astype(jnp.bfloat16), 'dp', axis=0, tiled=True)]
    reduce_scatter x5 -> x0, waiting for transfers between devices: 501 us -> none  [the longest x1 285 us: shards(): lax.psum_scatter(grad_gate_up, 'dp', scatter_dimension=1, tiled=True)]
    pallas_call x0 -> x5, Pallas kernels: none -> 265 us  [the longest x1 116 us: scatter_grads(): pl.pallas_call(functools.partial(scatter_kernel, chunks), out_shape=(jax....]
    all_gather x3 -> x0, blocking collectives: 170 us -> none  [the longest x1 80.8 us: shards(): lax.all_gather(norm_master.astype(jnp.bfloat16), 'dp', axis=2, tiled=True)]
    psum x1, waiting for transfers between devices: 211 us -> 120 us  [fast_shards(): lax.psum((0.25 * col_parts, 0.25 * step_parts, 0.25 * row_parts, jnp.stac...]
    psum x3 -> x0, blocking collectives: 61.2 us -> none  [the longest x1 37.6 us: shards(): col_sum, row_sum = lax.psum((col_parts, row_parts), 'dp')]
    scatter-add x1 -> x0, other arithmetic: 61.1 us -> none  [shards(): jnp.zeros((row_count, model_width), jnp.float32).at[slot_idx]]
  transfers between devices with their start and end apart: 13 -> 1, of which waited for: 11 -> 1; matrix products, arithmetic and copies ran while one was open for 8% -> 0% of each run, Pallas kernels for 0% -> 0%
where the time goes in v1:
time: 802 us; the launch traced here: 792 us
  Pallas kernels  265 us (33%)
  matrix products  169 us (21%)
  waiting for transfers between devices  120 us (15%)
  local copies, waits for them, and re-layouts  116 us (14%)
  other arithmetic  96.2 us (12%)
  between operations  26.3 us (3%)
    psum x1, waiting for transfers between devices, fast_shards(): lax.psum((0.25 * col_parts, 0.25 * step_parts, 0.25 * row_parts, jnp.stac...  120 us
    pallas_call x1, Pallas kernels, scatter_grads(): pl.pallas_call(functools.partial(scatter_kernel, chunks), out_shape=(jax....  116 us
    pallas_call x1, Pallas kernels, gather_weights(): pl.pallas_call(functools.partial(gather_kernel, chunks), out_shape=(jax.S...  102 us
    unnamed x354, local copies, waits for them, and re-layouts  46 us
    dot_general x2, matrix products, attend_back(): jnp.einsum('hts,shc->thc', grad_raw, key_all, preferred_element_type=jnp....  31.5 us
    dot_general x2, matrix products, attend_back(): jnp.einsum('hts,thc->shc', grad_raw, query_all, preferred_element_type=jn...  31 us
    pallas_call x2, Pallas kernels, spread(): pl.pallas_call(spread_kernel, out_shape=jax.ShapeDtypeStruct((32,) + v.sh...  29.9 us
    add x6, other arithmetic, fast_shards(): master_list[i]  18 us
  transfers between devices with their start and end apart: 1, of which 1 were waited for; matrix products, arithmetic and copies ran while one was open for 0% of the time, Pallas kernels for 0%

profile of v1, /device:TPU:0, one launch (start us, length us, event | category | flops | bytes accessed | tf_op | source)
XLA Modules:
  0.0 792.5 jit_solution(7444935341980874132)
XLA Ops:
  18.5 11.9 %shard_map.339 = s32[32,8,128]{2,1,0:T(8,128)} custom-call(s32[8,128]{1,0:T(8,128)} %concatenate.37.v_ref), custom_call_target="tpu_custom_call" | custom-call | tf_op jit(solution)/shard_map/pallas_call | solution.py:541
  32.7 5.9 gather_fusion.2
  41.4 102.4 %shard_map.340 = (bf16[8,2144,512]{2,1,0:T(8,128)(2,1)}, bf16[8,96,512]{2,1,0:T(8,128)(2,1)S(1)}) custom-call(bf16[2144,512]{1,0:T(8,128)(2,1)} %fusion.49.w_ref, bf16[8,96,512]{2,1,0:T(8,128)(2,1)} %select_convert_fusion.rows_ref), custom_call_target="tpu_custom_call" | custom-call | tf_op jit(solution)/shard_map/pallas_call | solution.py:517
  144.7 7.0 fusion.211
  162.7 4.7 copy.187
  167.5 4.2 copy.235
  171.7 2.6 copy.183
  174.3 4.2 copy.233
  181.6 4.2 conditional.4
  187.9 3.2 convolution_convert_fusion.3
  193.3 3.8 fusion.218
  204.5 2.5 fusion.189
  218.2 2.6 copy.185
  220.8 3.7 fusion.221
  227.8 2.6 fusion.74
  233.0 2.5 fusion.186
  244.8 18.0 %shard_map.341 = f32[32,4,512]{2,1,0:T(4,128)} custom-call(f32[4,512]{1,0:T(4,128)} %broadcast_multiply_fusion.3.v_ref), custom_call_target="tpu_custom_call" | custom-call | tf_op jit(solution)/shard_map/pallas_call | solution.py:541
  271.1 3.8 scatter_fusion.1
  284.1 2.9 fusion.224
  287.0 2.6 copy.189
  295.5 6.9 fusion.52
  302.5 3.3 multiply_reduce_fusion.10
  307.3 5.5 fusion.100
  315.1 15.5 %fusion.63 = bf16[512,1,8,64]{0,3,2,1:T(8,128)(2,1)} fusion(f32[8,512,512]{1,2,0:T(8,128)} %fusion.100, f32[8,512,512]{1,2,0:T(8,128)} %copy-done.3, f32[8,512]{1,0:T(8,128)S(1)} %log_add_fusion, bf16[512,3,8,64]{0,3,2,1:T(8,128)(2,1)} %bitcast.404), kind=kOutput, calls=%fused_computation.113 | convolution fusion | flops 283120128 | bytes 34635776 | tf_op jit(solution)/shard_map/hts,thc->shc/dot_general | solution.py:111
  330.6 15.9 %fusion.60 = bf16[512,1,8,64]{0,3,2,1:T(8,128)(2,1)} fusion(f32[8,512,512]{1,2,0:T(8,128)} %fusion.100, f32[8,512,512]{1,2,0:T(8,128)} %copy-done.3, f32[8,512]{1,0:T(8,128)S(1)} %log_add_fusion, bf16[512,3,8,64]{0,3,2,1:T(8,128)(2,1)} %bitcast.405), kind=kOutput, calls=%fused_computation.112 | convolution fusion | flops 283120128 | bytes 34635776 | tf_op jit(solution)/shard_map/hts,shc->thc/dot_general | solution.py:110
  348.1 3.9 multiply_reduce_fusion.11
  352.4 6.8 fusion.51
  359.3 3.3 multiply_reduce_fusion.12
  364.1 5.6 fusion.99
  371.9 15.5 %fusion.57 = bf16[512,1,8,64]{0,3,2,1:T(8,128)(2,1)} fusion(f32[8,512,512]{1,2,0:T(8,128)} %fusion.99, f32[8,512,512]{1,2,0:T(8,128)} %copy-done.1, f32[8,512]{1,0:T(8,128)S(1)} %log_add_fusion.1, bf16[512,3,8,64]{0,3,2,1:T(8,128)(2,1)} %bitcast.399), kind=kOutput, calls=%fused_computation.111 | convolution fusion | flops 283120128 | bytes 34635776 | tf_op jit(solution)/shard_map/hts,thc->shc/dot_general | solution.py:111
  387.4 15.7 %fusion.54 = bf16[512,1,8,64]{0,3,2,1:T(8,128)(2,1)} fusion(f32[8,512,512]{1,2,0:T(8,128)} %fusion.99, f32[8,512,512]{1,2,0:T(8,128)} %copy-done.1, f32[8,512]{1,0:T(8,128)S(1)} %log_add_fusion.1, bf16[512,3,8,64]{0,3,2,1:T(8,128)(2,1)} %bitcast.400), kind=kOutput, calls=%fused_computation.110 | convolution fusion | flops 283120128 | bytes 34635776 | tf_op jit(solution)/shard_map/hts,shc->thc/dot_general | solution.py:110
  403.1 8.0 %convolution_convert_fusion.1 = bf16[512,4096]{1,0:T(8,128)(2,1)} fusion(f32[512,2048]{1,0:T(8,128)} %copy-done.156, f32[512,2048]{1,0:T(8,128)} %copy-done.155, f32[512,512]{0,1:T(8,128)S(1)} %get-tuple-element.251, f32[512]{0:T(512)S(1)} %bitcast.470, f32[512]{0:T(512)S(1)} %bitcast.459, f32[512]{0:T(512)S(1)} %copy-done.86, f32[512]{0:T(512)S(1)} %copy-done.74), kind=kOutput, calls=%fused_computation.50 | convolution fusion | flops 2155085824 | bytes 13639680 | tf_op jit(solution)/shard_map/dot_general | solution.py:943
  411.2 2.6 convolution_convert_fusion.5
  414.2 4.2 convolution_convert_fusion
  418.4 2.7 convolution_convert_fusion.4
  425.9 2.7 convolution_convert_fusion.7
  435.0 2.4 constant_dynamic-update-slice_fusion.5
  443.3 2.4 copy.237
  447.4 2.4 constant_dynamic-update-slice_fusion.2
  453.0 116.2 %shard_map.342 = (bf16[2144,512]{1,0:T(8,128)(2,1)}, bf16[4,8,96,512]{3,2,1,0:T(8,128)(2,1)}) custom-call(bf16[8,2144,512]{2,1,0:T(8,128)(2,1)} %broadcast_dynamic-update-slice_fusion.g_ref, bf16[8,96,512]{2,1,0:T(8,128)(2,1)} %bitcast.433), custom_call_target="tpu_custom_call" | custom-call | tf_op jit(solution)/shard_map/pallas_call | solution.py:684
  569.3 4.4 convert_element_type.266
  576.8 16.8 %conditional.10 = (f32[3816,512]{1,0:T(8,128)}) conditional(s32[]{:T(128)} %convert_element_type.216, (s32[4,8,96]{2,0,1:T(4,128)S(1)}, bf16[4,8,96,512]{3,2,1,0:T(8,128)(2,1)}) %tuple.175, (s32[512]{0:T(512)S(1)}, f32[512,512]{0,1:T(8,128)}) %tuple.177), branch_computations={%region_46.48_spmd, %region_47.52_spmd} | conditional | flops 2217472 | bytes 325671040 | solution.py:994
  576.9 16.7 %branch_0_fun.1 = f32[3816,512]{1,0:T(8,128)} custom-call(s32[1,3072]{1,0:T(1,128)S(1)} %reshape.940.slot_ref, bf16[3072,512]{1,0:T(8,128)(2,1)} %bitcast.395), custom_call_target="tpu_custom_call" | custom-call | tf_op jit(solution)/shard_map/cond/branch_0_fun/pallas_call | solution.py:779
  593.6 4.0 multiply_reduce_fusion.4
  607.9 2.8 copy.209
  610.8 2.4 stack_reshape.15
  628.5 119.8 %all-reduce.13.cloned.1.call-done = (f32[14336]{0:T(1024)}, f32[14336]{0:T(1024)}, f32[10]{0:T(128)}, f32[5,2,512]{2,1,0:T(2,128)}) async-done(((f32[14336]{0:T(1024)}, f32[14336]{0:T(1024)}, f32[10]{0:T(128)}, f32[5,2,512]{2,1,0:T(2,128)}), (f32[14336]{0:T(1024)}, f32[14336]{0:T(1024)}, f32[10]{0:T(128)}, f32[5,2,512]{2,1,0:T(2,128)})) %all-reduce.13.cloned.1.call-update) | async-done | bytes 135224 | tf_op jit(solution)/shard_map/psum | solution.py:1051
  762.3 9.2 %multiply_add_fusion.2 = f32[3816,512]{1,0:T(8,128)} fusion(f32[3816,512]{1,0:T(8,128)} %param.31, f32[3816,512]{1,0:T(8,128)} %get-tuple-element.280, f32[512]{0:T(512)S(1)} %bitcast.487, f32[3816]{0:T(1024)S(1)} %rsqrt_multiply_fusion), kind=kLoop, calls=%fused_computation.39 | loop fusion | flops 5861376 | bytes 23462816 | tf_op jit(solution)/shard_map/add | solution.py:1079
  (592 shorter events, 174.0 us)
Async XLA Ops:
  16.9 164.6 %copy-start.103 = (s32[512]{0:T(512)}, s32[512]{0:T(512)S(1)}, u32[]{:S(2)}) copy-start(s32[512]{0:T(512)S(1)} %get-tuple-element.228) | copy-start | bytes 6148
  144.7 11.8 %copy-start.7 = (bf16[8,2144,512]{2,1,0:T(8,128)(2,1)S(1)}, bf16[8,2144,512]{2,1,0:T(8,128)(2,1)}, u32[]{:S(2)}) copy-start(bf16[8,2144,512]{2,1,0:T(8,128)(2,1)} %get-tuple-element.75) | copy-start | bytes 52690948
  162.7 48.0 %copy-start.83 = (f32[1,1,512]{2,1,0:T(1,128)}, f32[1,1,512]{2,1,0:T(1,128)S(1)}, u32[]{:S(2)}) copy-start(f32[1,1,512]{2,1,0:T(1,128)S(1)} %get-tuple-element.217) | copy-start | bytes 6148
  162.7 48.0 %copy-start.101 = (f32[1,1,512]{2,1,0:T(1,128)}, f32[1,1,512]{2,1,0:T(1,128)S(1)}, u32[]{:S(2)}) copy-start(f32[1,1,512]{2,1,0:T(1,128)S(1)} %get-tuple-element.216) | copy-start | bytes 6148
  162.7 67.8 %copy-start.122 = (f32[1,1,512]{2,1,0:T(1,128)}, f32[1,1,512]{2,1,0:T(1,128)S(1)}, u32[]{:S(2)}) copy-start(f32[1,1,512]{2,1,0:T(1,128)S(1)} %get-tuple-element.215) | copy-start | bytes 6148
  162.7 76.5 %copy-start.81 = (f32[1,1,512]{2,1,0:T(1,128)}, f32[1,1,512]{2,1,0:T(1,128)S(1)}, u32[]{:S(2)}) copy-start(f32[1,1,512]{2,1,0:T(1,128)S(1)} %get-tuple-element.213) | copy-start | bytes 6148
  162.7 76.5 %copy-start.99 = (f32[1,1,512]{2,1,0:T(1,128)}, f32[1,1,512]{2,1,0:T(1,128)S(1)}, u32[]{:S(2)}) copy-start(f32[1,1,512]{2,1,0:T(1,128)S(1)} %get-tuple-element.212) | copy-start | bytes 6148
  162.7 79.4 %copy-start.69 = (f32[1,1,512]{2,1,0:T(1,128)}, f32[1,1,512]{2,1,0:T(1,128)S(1)}, u32[]{:S(2)}) copy-start(f32[1,1,512]{2,1,0:T(1,128)S(1)} %get-tuple-element.208) | copy-start | bytes 6148
  162.7 79.4 %copy-start.97 = (f32[1,1,512]{2,1,0:T(1,128)}, f32[1,1,512]{2,1,0:T(1,128)S(1)}, u32[]{:S(2)}) copy-start(f32[1,1,512]{2,1,0:T(1,128)S(1)} %get-tuple-element.211) | copy-start | bytes 6148
  193.1 49.0 %copy-start.96 = (s32[512]{0:T(512)}, s32[512]{0:T(512)S(1)}, u32[]{:S(2)}) copy-start(s32[512]{0:T(512)S(1)} %convert_reduce_fusion.2) | copy-start | bytes 6148
  212.1 18.4 %copy-start.105 = (f32[512]{0:T(512)}, f32[512]{0:T(512)S(1)}, u32[]{:S(2)}) copy-start(f32[512]{0:T(512)S(1)} %broadcast_multiply_fusion.7) | copy-start | bytes 6148
  212.3 18.2 %copy-start.124 = (f32[512]{0:T(512)}, f32[512]{0:T(512)S(1)}, u32[]{:S(2)}) copy-start(f32[512]{0:T(512)S(1)} %fusion.146) | copy-start | bytes 6148
  240.6 23.3 %copy-start.140 = (s32[128]{0:T(128)S(1)}, s32[128]{0:T(128)}, u32[]{:S(2)}) copy-start(s32[128]{0:T(128)} %param.29) | copy-start | bytes 1540
  241.6 23.5 %copy-start.107 = (f32[512]{0:T(512)}, f32[512]{0:T(512)S(1)}, u32[]{:S(2)}) copy-start(f32[512]{0:T(512)S(1)} %broadcast_multiply_fusion.4) | copy-start | bytes 6148
  241.9 23.2 %copy-start.119 = (f32[512]{0:T(512)}, f32[512]{0:T(512)S(1)}, u32[]{:S(2)}) copy-start(f32[512]{0:T(512)S(1)} %multiply_reduce_fusion.19) | copy-start | bytes 6148
  242.1 23.0 %copy-start.150 = (f32[4]{0:T(128)}, f32[4]{0:T(128)S(1)}, u32[]{:S(2)}) copy-start(f32[4]{0:T(128)S(1)} %broadcast_maximum_fusion) | copy-start | bytes 52
  243.7 21.3 %copy-start.128 = (bf16[4,512]{1,0:T(4,128)(2,1)}, bf16[4,512]{1,0:T(4,128)(2,1)S(1)}, u32[]{:S(2)}) copy-start(bf16[4,512]{1,0:T(4,128)(2,1)S(1)} %fusion.78) | copy-start | bytes 12292
  244.0 18.7 %copy-start.147 = (f32[4]{0:T(128)}, f32[4]{0:T(128)S(1)}, u32[]{:S(2)}) copy-start(f32[4]{0:T(128)S(1)} %get-tuple-element.260) | copy-start | bytes 52
  244.1 21.0 %copy-start.138 = (f32[4]{0:T(128)}, f32[4]{0:T(128)S(1)}, u32[]{:S(2)}) copy-start(f32[4]{0:T(128)S(1)} %add_rsqrt_fusion) | copy-start | bytes 52
  270.1 21.8 %copy-start.120 = (f32[512]{0:T(512)S(1)}, f32[512]{0:T(512)}, u32[]{:S(2)}) copy-start(f32[512]{0:T(512)} %copy-done.119) | copy-start | bytes 6148
  270.1 21.8 %copy-start.68 = (f32[512]{0:T(512)S(1)}, f32[512]{0:T(512)}, u32[]{:S(2)}) copy-start(f32[512]{0:T(512)} %copy-done.67) | copy-start | bytes 6148
  270.1 21.9 %copy-start.70 = (f32[1,1,512]{2,1,0:T(1,128)S(1)}, f32[1,1,512]{2,1,0:T(1,128)}, u32[]{:S(2)}) copy-start(f32[1,1,512]{2,1,0:T(1,128)} %copy-done.69) | copy-start | bytes 6148
  270.1 21.9 %copy-start.72 = (f32[512]{0:T(512)S(1)}, f32[512]{0:T(512)}, u32[]{:S(2)}) copy-start(f32[512]{0:T(512)} %copy-done.71) | copy-start | bytes 6148
  270.1 21.9 %copy-start.98 = (f32[1,1,512]{2,1,0:T(1,128)S(1)}, f32[1,1,512]{2,1,0:T(1,128)}, u32[]{:S(2)}) copy-start(f32[1,1,512]{2,1,0:T(1,128)} %copy-done.97) | copy-start | bytes 6148
  270.1 21.9 %copy-start.108 = (f32[512]{0:T(512)S(1)}, f32[512]{0:T(512)}, u32[]{:S(2)}) copy-start(f32[512]{0:T(512)} %copy-done.107) | copy-start | bytes 6148
  270.1 21.9 %copy-start.127 = (f32[512]{0:T(512)S(1)}, f32[512]{0:T(512)}, u32[]{:S(2)}) copy-start(f32[512]{0:T(512)} %copy-done.126) | copy-start | bytes 6148
  274.9 19.0 %copy-start.13 = (f32[64,64]{1,0:T(8,128)}, f32[64,64]{1,0:T(8,128)S(1)}, u32[]{:S(2)}) copy-start(f32[64,64]{1,0:T(8,128)S(1)} %scatter_fusion.1) | copy-start | bytes 49156
  295.4 17.4 %slice-start.2 = ((s8[8388608]{0:T(1024)(128)(4,1)}), s8[4194304]{0:T(1024)(128)(4,1)S(1)}, s32[]{:S(2)}) async-start(s8[8388608]{0:T(1024)(128)(4,1)} %bitcast.355), calls=%async_computation.7 | async-start | bytes 8388608
  302.5 10.4 %slice-start.3 = ((s8[8388608]{0:T(1024)(128)(4,1)}), s8[4194304]{0:T(1024)(128)(4,1)S(1)}, s32[]{:S(2)}) async-start(s8[8388608]{0:T(1024)(128)(4,1)} %bitcast.355), calls=%async_computation.8 | async-start | bytes 8388608
  330.6 15.9 %copy-start.90 = (f32[8,512]{1,0:T(8,128)S(1)}, f32[8,512]{1,0:T(8,128)}, u32[]{:S(2)}) copy-start(f32[8,512]{1,0:T(8,128)} %copy-done.89) | copy-start | bytes 49156
  330.6 15.9 %copy-start.92 = (f32[8,512]{1,0:T(8,128)S(1)}, f32[8,512]{1,0:T(8,128)}, u32[]{:S(2)}) copy-start(f32[8,512]{1,0:T(8,128)} %copy-done.91) | copy-start | bytes 49156
  330.6 17.5 %copy-start.106 = (f32[512]{0:T(512)S(1)}, f32[512]{0:T(512)}, u32[]{:S(2)}) copy-start(f32[512]{0:T(512)} %copy-done.105) | copy-start | bytes 6148
  330.6 17.5 %copy-start.123 = (f32[1,1,512]{2,1,0:T(1,128)S(1)}, f32[1,1,512]{2,1,0:T(1,128)}, u32[]{:S(2)}) copy-start(f32[1,1,512]{2,1,0:T(1,128)} %copy-done.122) | copy-start | bytes 6148
  330.6 17.5 %copy-start.125 = (f32[512]{0:T(512)S(1)}, f32[512]{0:T(512)}, u32[]{:S(2)}) copy-start(f32[512]{0:T(512)} %copy-done.124) | copy-start | bytes 6148
  352.4 17.3 %slice-start = ((s8[8388608]{0:T(1024)(128)(4,1)}), s8[4194304]{0:T(1024)(128)(4,1)S(1)}, s32[]{:S(2)}) async-start(s8[8388608]{0:T(1024)(128)(4,1)} %bitcast.353), calls=%async_computation.5 | async-start | bytes 8388608
  359.3 10.4 %slice-start.1 = ((s8[8388608]{0:T(1024)(128)(4,1)}), s8[4194304]{0:T(1024)(128)(4,1)S(1)}, s32[]{:S(2)}) async-start(s8[8388608]{0:T(1024)(128)(4,1)} %bitcast.353), calls=%async_computation.6 | async-start | bytes 8388608
  387.4 15.7 %copy-start.102 = (f32[1,1,512]{2,1,0:T(1,128)S(1)}, f32[1,1,512]{2,1,0:T(1,128)}, u32[]{:S(2)}) copy-start(f32[1,1,512]{2,1,0:T(1,128)} %copy-done.101) | copy-start | bytes 6148
  403.1 10.7 %copy-start.154 = (f32[512,2048]{1,0:T(8,128)S(1)}, f32[512,2048]{1,0:T(8,128)}, u32[]{:S(2)}) copy-start(f32[512,2048]{1,0:T(8,128)} %copy-done.153) | copy-start | bytes 12582916
  593.5 154.7 %all-reduce.13.cloned.1.call-start = ((), (), s32[]{:S(2)}) async-start(), calls=%async_computation.4 | async-start | bytes 271360 | tf_op jit(solution)/shard_map/psum | solution.py:1051
  598.1 162.9 %copy-start.65 = (f32[3816]{0:T(1024)}, f32[3816]{0:T(1024)S(1)}, u32[]{:S(2)}) copy-start(f32[3816]{0:T(1024)S(1)} %get-tuple-element.161) | copy-start | bytes 45796
  614.5 11.4 %copy-start.14 = (f32[64,64]{1,0:T(8,128)S(1)}, f32[64,64]{1,0:T(8,128)}, u32[]{:S(2)}) copy-start(f32[64,64]{1,0:T(8,128)} %copy-done.13) | copy-start | bytes 49156
  614.5 11.4 %copy-start.66 = (f32[64,64]{1,0:T(8,128)S(1)}, f32[64,64]{1,0:T(8,128)}, u32[]{:S(2)}) copy-start(f32[64,64]{1,0:T(8,128)} %get-tuple-element.262) | copy-start | bytes 49156
  614.8 141.6 %copy-start.95 = (f32[2,6656]{1,0:T(2,128)S(1)}, f32[2,6656]{1,0:T(2,128)}, u32[]{:S(2)}) copy-start(f32[2,6656]{1,0:T(2,128)} %param.42) | copy-start | bytes 159748
  614.8 144.9 %copy-start.137 = (f32[2,512]{1,0:T(2,128)S(1)}, f32[2,512]{1,0:T(2,128)}, u32[]{:S(2)}) copy-start(f32[2,512]{1,0:T(2,128)} %param.43) | copy-start | bytes 12292
  614.8 147.4 %copy-start.146 = (f32[64]{0:T(128)S(1)}, f32[64]{0:T(128)}, u32[]{:S(2)}) copy-start(f32[64]{0:T(128)} %copy-done.145) | copy-start | bytes 772
  617.0 154.6 %copy-start.121 = (f32[2,256]{1,0:T(2,128)}, f32[2,256]{1,0:T(2,128)S(1)}, u32[]{:S(2)}) copy-start(f32[2,256]{1,0:T(2,128)S(1)} %get-tuple-element.151) | copy-start | bytes 6148
  760.3 11.2 %copy-start.133 = (f32[1,512]{1,0:T(1,128)}, f32[1,512]{1,0:T(1,128)S(1)}, u32[]{:S(2)}) copy-start(f32[1,512]{1,0:T(1,128)S(1)} %get-tuple-element.139) | copy-start | bytes 6148
  760.3 11.2 %copy-start.134 = (f32[1,512]{1,0:T(1,128)}, f32[1,512]{1,0:T(1,128)S(1)}, u32[]{:S(2)}) copy-start(f32[1,512]{1,0:T(1,128)S(1)} %get-tuple-element.219) | copy-start | bytes 6148
  (114 other events, 467.2 us)
Sparse Core Ops, SparseCore 1:
  626.0 122.2 all-reduce.12

commit v2 on v1

--- a/solution.py
+++ b/solution.py
@@ -789,6 +789,491 @@
     )(slots, rows)
 
 
+def dot_nn(left, right):
+    return lax.dot_general(left, right, (((1,), (0,)), ((), ())), preferred_element_type=jnp.float32)
+
+
+def dot_nt(left, right):
+    return lax.dot_general(left, right, (((1,), (1,)), ((), ())), preferred_element_type=jnp.float32)
+
+
+def dot_tn(left, right):
+    return lax.dot_general(left, right, (((0,), (0,)), ((), ())), preferred_element_type=jnp.float32)
+
+
+def exact_dot(left, right, dims=((1,), (0,))):
+    return lax.dot_general(
+        left, right, (dims, ((), ())), precision=lax.Precision.HIGHEST, preferred_element_type=jnp.float32
+    )
+
+
+GELU_SCALE = (2.0 / 3.141592653589793) ** 0.5
+GELU_CUBE = 0.044715
+TILE = 256
+
+
+def norm_parts(values):
+    center = values - jnp.mean(values, axis=-1, keepdims=True)
+    inverse = lax.rsqrt(jnp.mean(center * center, axis=-1, keepdims=True) + NORM_EPS)
+    return center * inverse, inverse
+
+
+def norm_back(scaled, inverse, grad_out, gain):
+    grad_scaled = grad_out * gain
+    mean_grad = jnp.mean(grad_scaled, axis=-1, keepdims=True)
+    mean_both = jnp.mean(grad_scaled * scaled, axis=-1, keepdims=True)
+    return inverse * (grad_scaled - mean_grad - scaled * mean_both)
+
+
+def gelu_parts(value):
+    bend = jnp.tanh(GELU_SCALE * (value + GELU_CUBE * value * value * value))
+    half = 0.5 * (1.0 + bend)
+    slope = half + 0.5 * value * (1.0 - bend * bend) * GELU_SCALE * (1.0 + 3.0 * GELU_CUBE * value * value)
+    return value * half, slope
+
+
+def block(w_ref, start):
+    return w_ref[:, start : start + 64, :].reshape(D, D)
+
+
+def down_block(w_ref, j):
+    return w_ref[2 * j : 2 * j + 2, 768:1024, :].reshape(D, D)
+
+
+def fill_distance(far, seg_col_ref, seg_row_ref):
+    tokens = far.shape[0]
+    def body(i, carry):
+        start = pl.multiple_of(i * 64, 64)
+        rows = lax.broadcasted_iota(jnp.int32, (64, tokens), 0) + start
+        cols = lax.broadcasted_iota(jnp.int32, (64, tokens), 1)
+        gap = jnp.abs(rows - cols).astype(jnp.float32)
+        same = seg_col_ref[pl.ds(start, 64), :] == seg_row_ref[...]
+        far[pl.ds(start, 64), :] = jnp.where(same, gap, jnp.inf)
+        return carry
+    lax.fori_loop(0, tokens // 64, body, 0)
+
+
+def forward_kernel(
+    first_ref, seg_col_ref, seg_row_ref, valid_ref, w_ref, head_ref, norm_ref,
+    low_ref, qkv_ref, lse_ref, mix_ref, one_ref, two_ref, unit_ref, pool_ref, zed_ref,
+    x_s, far, acc,
+):
+    layer = pl.program_id(0)
+    tokens = x_s.shape[0]
+    tiles = tokens // TILE
+
+    @pl.when(layer == 0)
+    def _():
+        x_s[...] = first_ref[...].astype(jnp.float32)
+        fill_distance(far, seg_col_ref, seg_row_ref)
+
+    def project(i, carry):
+        rows = pl.ds(pl.multiple_of(i * TILE, TILE), TILE)
+        low = x_s[rows, :].astype(jnp.bfloat16)
+        low_ref[0, rows, :] = low
+        for j in range(3):
+            qkv_ref[0, rows, j * D : (j + 1) * D] = dot_nn(low, block(w_ref, j * 64)).astype(jnp.bfloat16)
+        return carry
+
+    lax.fori_loop(0, tiles, project, 0)
+    for head in range(HEADS):
+        lanes = slice(head * HEAD_DIM, (head + 1) * HEAD_DIM)
+        keys = qkv_ref[0, :, D + head * HEAD_DIM : D + (head + 1) * HEAD_DIM]
+        vals_t = qkv_ref[0, :, 2 * D + head * HEAD_DIM : 2 * D + (head + 1) * HEAD_DIM].T
+        slope = 2.0 ** (-8.0 * (head + 1) / HEADS)
+        for i in range(tiles):
+            cols = slice(i * TILE, (i + 1) * TILE)
+            scores = dot_nt(keys, qkv_ref[0, cols, lanes]) * HEAD_DIM**-0.5 - slope * far[:, cols]
+            top = jnp.max(scores, axis=0, keepdims=True)
+            raised = jnp.exp(scores - top)
+            total = jnp.sum(raised, axis=0, keepdims=True)
+            lse_ref[0, head, :, cols] = top + jnp.log(total)
+            prob = (raised * (1.0 / total)).astype(jnp.bfloat16)
+            mix_ref[0, lanes, cols] = dot_nn(vals_t, prob).astype(jnp.bfloat16)
+
+    acc[...] = dot_tn(mix_ref[0], block(w_ref, 192))
+
+    def feed(i, carry):
+        rows = pl.ds(pl.multiple_of(i * TILE, TILE), TILE)
+        resid = x_s[rows, :] + acc[rows, :]
+        one_ref[0, rows, :] = resid
+        at = 4 * layer
+        scaled, _ = norm_parts(resid)
+        hidden = scaled * norm_ref[pl.ds(at, 1), :] + norm_ref[pl.ds(at + 1, 1), :]
+        low = hidden.astype(jnp.bfloat16)
+        total = hidden
+        for j in range(4):
+            gate = dot_nn(low, block(w_ref, 256 + j * 64))
+            up = dot_nn(low, block(w_ref, 512 + j * 64))
+            bend = jnp.tanh(GELU_SCALE * (gate + GELU_CUBE * gate * gate * gate))
+            mid = (0.5 * gate * (1.0 + bend) * up).astype(jnp.bfloat16)
+            total = total + dot_nn(mid, down_block(w_ref, j))
+        two_ref[0, rows, :] = total
+        scaled, _ = norm_parts(total)
+        x_s[rows, :] = scaled * norm_ref[pl.ds(at + 2, 1), :] + norm_ref[pl.ds(at + 3, 1), :]
+        return carry
+
+    lax.fori_loop(0, tiles, feed, 0)
+
+    @pl.when(layer == LAYERS - 1)
+    def _():
+        scaled, _ = norm_parts(x_s[...])
+        final = scaled * norm_ref[8:9, :] + norm_ref[9:10, :]
+        member = members(seg_row_ref, valid_ref)
+        counts = jnp.maximum(jnp.sum(member, axis=1, keepdims=True), 1.0)
+        pooled = (exact_dot(member, final) / counts).astype(jnp.bfloat16)
+        pool_ref[...] = pooled
+        zed = dot_nn(pooled, head_ref[...].reshape(D, D))
+        zed_ref[...] = zed
+        unit = zed * lax.rsqrt(jnp.sum(zed * zed, axis=-1, keepdims=True) + UNIT_EPS)
+        for s in range(4):
+            for part in range(4):
+                unit_ref[4 * s + part : 4 * s + part + 1, :] = unit[s : s + 1, part * 128 : (part + 1) * 128]
+
+
+def members(seg_row_ref, valid_ref):
+    tokens = seg_row_ref.shape[1]
+    slot = lax.broadcasted_iota(jnp.int32, (8, tokens), 0)
+    return jnp.where((seg_row_ref[...] == slot) & (valid_ref[...] > 0), 1.0, 0.0)
+
+
+def whole(shape):
+    return pl.BlockSpec(shape, lambda i: (0,) * len(shape))
+
+
+def run_forward(first, seg_col, seg_row, valid, weights, norms):
+    tokens = first.shape[0]
+    low = jnp.bfloat16
+    layered = lambda *s: pl.BlockSpec((1,) + s, lambda i: (i,) + (0,) * len(s))
+    return pl.pallas_call(
+        forward_kernel,
+        grid=(LAYERS,),
+        in_specs=[
+            whole((tokens, D)), whole((tokens, 1)), whole((1, tokens)), whole((1, tokens)),
+            pl.BlockSpec((8, PART, D), lambda i: (0, i, 0)),
+            pl.BlockSpec((8, 64, D), lambda i: (0, HEAD_AT // 64, 0)),
+            whole(norms.shape),
+        ],
+        out_specs=[
+            layered(tokens, D), layered(tokens, 3 * D), layered(HEADS, 1, tokens), layered(D, tokens),
+            layered(tokens, D), layered(tokens, D), whole((16, 128)), whole((8, D)), whole((8, D)),
+        ],
+        out_shape=[
+            jax.ShapeDtypeStruct((LAYERS, tokens, D), low),
+            jax.ShapeDtypeStruct((LAYERS, tokens, 3 * D), low),
+            jax.ShapeDtypeStruct((LAYERS, HEADS, 1, tokens), jnp.float32),
+            jax.ShapeDtypeStruct((LAYERS, D, tokens), low),
+            jax.ShapeDtypeStruct((LAYERS, tokens, D), jnp.float32),
+            jax.ShapeDtypeStruct((LAYERS, tokens, D), jnp.float32),
+            jax.ShapeDtypeStruct((16, 128), jnp.float32),
+            jax.ShapeDtypeStruct((8, D), low),
+            jax.ShapeDtypeStruct((8, D), jnp.float32),
+        ],
+        scratch_shapes=[
+            pltpu.VMEM((tokens, D), jnp.float32), pltpu.VMEM((tokens, tokens), jnp.float32),
+            pltpu.VMEM((tokens, D), jnp.float32),
+        ],
+        compiler_params=pltpu.CompilerParams(vmem_limit_bytes=60 * 2**20),
+    )(first, seg_col, seg_row, valid, weights, weights, norms)
+
+
+def contrast_kernel(unit_ref, deal_col_ref, deal_row_ref, scale_ref, loss_ref, own_ref, slope_ref, every, ss, rs, ls):
+    lin = lax.axis_index("dp") * 4 + lax.axis_index("group")
+    peers = [lax.rem(lin + k, 32) for k in range(32)]
+    peers = [(p // 4, p % 4) for p in peers]
+    entry_barrier(peers[1:])
+    copies = [
+        pltpu.make_async_remote_copy(
+            unit_ref, every.at[lin], ss.at[k], rs.at[k], device_id=peers[k], device_id_type=MESH
+        )
+        for k in range(1, 32)
+    ]
+    for copy in copies:
+        copy.start()
+    own = pltpu.make_async_copy(unit_ref, every.at[lin], ls)
+    own.start()
+    for copy in copies:
+        copy.wait()
+    own.wait()
+    units = every[...].reshape(512, 128)
+    place_at = lax.broadcasted_iota(jnp.int32, (128, 512), 1)
+    sorted_units = jnp.concatenate(
+        [
+            exact_dot(jnp.where(deal_col_ref[...] * 4 + part == place_at, 1.0, 0.0), units)
+            for part in range(4)
+        ],
+        axis=1,
+    )
+    queries, documents = sorted_units[:64], sorted_units[64:]
+    scale = jnp.exp(scale_ref[...])
+    logits = scale * exact_dot(queries, documents, ((1,), (1,)))
+    row_top = jnp.max(logits, axis=1, keepdims=True)
+    row_lse = row_top + jnp.log(jnp.sum(jnp.exp(logits - row_top), axis=1, keepdims=True))
+    col_top = jnp.max(logits, axis=0, keepdims=True)
+    col_lse = col_top + jnp.log(jnp.sum(jnp.exp(logits - col_top), axis=0, keepdims=True))
+    diagonal = jnp.where(
+        lax.broadcasted_iota(jnp.int32, (64, 64), 0) == lax.broadcasted_iota(jnp.int32, (64, 64), 1), 1.0, 0.0
+    )
+    on_diagonal = jnp.sum(logits * diagonal, axis=1, keepdims=True)
+    col_sum = jnp.sum(col_lse, axis=1, keepdims=True)
+    row_sum = jnp.sum(row_lse, axis=0, keepdims=True)
+    loss_ref[...] = 0.5 * (row_sum + col_sum) - jnp.sum(on_diagonal, axis=0, keepdims=True)
+    grad_logits = 0.5 * (jnp.exp(logits - row_lse) + jnp.exp(logits - col_lse)) - diagonal
+    slope = jnp.sum(grad_logits * logits, axis=1, keepdims=True)
+    slope_ref[...] = jnp.sum(slope, axis=0, keepdims=True)
+    grad_raw = scale * grad_logits
+    grad_queries = exact_dot(grad_raw, documents)
+    grad_documents = exact_dot(grad_raw, queries, ((0,), (0,)))
+    mine = lax.broadcasted_iota(jnp.int32, (8, 128), 0)
+    picks = jnp.where((deal_row_ref[...] == mine + lin * 4) & (mine < 4), 1.0, 0.0)
+    own_ref[...] = exact_dot(picks, jnp.concatenate([grad_queries, grad_documents], axis=0))
+
+
+def run_contrast(unit, deal_order, log_scale, cid):
+    sems = pltpu.SemaphoreType.DMA
+    one = jax.ShapeDtypeStruct((1, 1), jnp.float32)
+    return pl.pallas_call(
+        contrast_kernel,
+        out_shape=[one, jax.ShapeDtypeStruct((8, D), jnp.float32), one],
+        in_specs=[pl.BlockSpec(memory_space=pltpu.VMEM)] * 4,
+        out_specs=[pl.BlockSpec(memory_space=pltpu.VMEM)] * 3,
+        scratch_shapes=[pltpu.VMEM((32, 16, 128), jnp.float32), sems((32,)), sems((32,)), sems],
+        compiler_params=pltpu.CompilerParams(collective_id=cid, has_side_effects=True),
+    )(unit, deal_order.reshape(128, 1), deal_order.reshape(1, 128), log_scale.reshape(1, 1))
+
+
+def backward_kernel(
+    own_ref, zed_ref, pool_ref, seg_col_ref, seg_row_ref, valid_ref, w_ref, head_ref, norm_ref,
+    low_ref, qkv_ref, lse_ref, mix_ref, one_ref, two_ref, last_ref,
+    grad_ref, norm_out_ref, first_ref,
+    dx, far, acc, two_s, low_s, mid_s, ups, gates, back,
+):
+    step = pl.program_id(0)
+    tokens = dx.shape[0]
+    tiles = tokens // TILE
+    low_type = jnp.bfloat16
+
+    @pl.when(step == 0)
+    def _():
+        fill_distance(far, seg_col_ref, seg_row_ref)
+        zed = zed_ref[...]
+        square = jnp.sum(zed * zed, axis=-1, keepdims=True) + UNIT_EPS
+        inverse = lax.rsqrt(square)
+        own = own_ref[...]
+        inner = jnp.sum(own * zed, axis=-1, keepdims=True)
+        grad_zed = (inverse * (own - zed * (inner / square))).astype(low_type)
+        head = head_ref[...].reshape(D, D)
+        grad_head = dot_tn(pool_ref[...], grad_zed)
+        grad_ref[:, 0:64, :] = grad_head.reshape(8, 64, D).astype(low_type)
+        grad_ref[:, 64:96, :] = jnp.zeros((8, 32, D), low_type)
+        member = members(seg_row_ref, valid_ref)
+        counts = jnp.maximum(jnp.sum(member, axis=1, keepdims=True), 1.0)
+        grad_pooled = dot_nt(grad_zed, head) / counts
+        grad_final = exact_dot(member, grad_pooled, ((0,), (0,)))
+        gain_last = norm_ref[6:7, :]
+        stream_scaled, _ = norm_parts(last_ref[0])
+        stream = stream_scaled * gain_last + norm_ref[7:8, :]
+        scaled, inverse = norm_parts(stream)
+        norm_out_ref[0, 0:1, :] = jnp.sum(grad_final * scaled, axis=0, keepdims=True)
+        norm_out_ref[0, 1:2, :] = jnp.sum(grad_final, axis=0, keepdims=True)
+        dx[...] = norm_back(scaled, inverse, grad_final, norm_ref[8:9, :])
+
+    @pl.when(step > 0)
+    def _():
+        at = 4 * (LAYERS - step)
+        norm_out_ref[0] = jnp.zeros((8, D), jnp.float32)
+
+        def enter(i, carry):
+            rows = pl.ds(pl.multiple_of(i * TILE, TILE), TILE)
+            scaled, inverse = norm_parts(two_ref[0, rows, :])
+            grad = dx[rows, :]
+            norm_out_ref[0, 2:3, :] += jnp.sum(grad * scaled, axis=0, keepdims=True)
+            norm_out_ref[0, 3:4, :] += jnp.sum(grad, axis=0, keepdims=True)
+            grad = norm_back(scaled, inverse, grad, norm_ref[pl.ds(at + 2, 1), :])
+            acc[rows, :] = grad
+            two_s[rows, :] = grad.astype(low_type)
+            scaled, _ = norm_parts(one_ref[0, rows, :])
+            hidden = scaled * norm_ref[pl.ds(at, 1), :] + norm_ref[pl.ds(at + 1, 1), :]
+            low_s[rows, :] = hidden.astype(low_type)
+            return carry
+
+        lax.fori_loop(0, tiles, enter, 0)
+        for j in range(4):
+            def feed(i, carry):
+                rows = pl.ds(pl.multiple_of(i * TILE, TILE), TILE)
+                low = low_s[rows, :]
+                gate = dot_nn(low, block(w_ref, 256 + j * 64))
+                up = dot_nn(low, block(w_ref, 512 + j * 64))
+                grad_mid = dot_nt(two_s[rows, :], down_block(w_ref, j))
+                value, slope = gelu_parts(gate)
+                mid_s[rows, :] = (value * up).astype(low_type)
+                grad_gate = (grad_mid * up * slope).astype(low_type)
+                grad_up = (grad_mid * value).astype(low_type)
+                gates[rows, :] = grad_gate
+                ups[rows, :] = grad_up
+                acc[rows, :] += dot_nt(grad_gate, block(w_ref, 256 + j * 64)) + dot_nt(
+                    grad_up, block(w_ref, 512 + j * 64)
+                )
+                return carry
+
+            lax.fori_loop(0, tiles, feed, 0)
+            grad_ref[2 * j : 2 * j + 2, 768:1024, :] = (
+                dot_tn(mid_s[...], two_s[...]).reshape(2, 256, D).astype(low_type)
+            )
+            grad_ref[:, 256 + j * 64 : 320 + j * 64, :] = (
+                dot_tn(low_s[...], gates[...]).reshape(8, 64, D).astype(low_type)
+            )
+            grad_ref[:, 512 + j * 64 : 576 + j * 64, :] = (
+                dot_tn(low_s[...], ups[...]).reshape(8, 64, D).astype(low_type)
+            )
+
+        def middle(i, carry):
+            rows = pl.ds(pl.multiple_of(i * TILE, TILE), TILE)
+            scaled, inverse = norm_parts(one_ref[0, rows, :])
+            grad = acc[rows, :]
+            norm_out_ref[0, 0:1, :] += jnp.sum(grad * scaled, axis=0, keepdims=True)
+            norm_out_ref[0, 1:2, :] += jnp.sum(grad, axis=0, keepdims=True)
+            grad = norm_back(scaled, inverse, grad, norm_ref[pl.ds(at, 1), :])
+            dx[rows, :] = grad
+            low = grad.astype(low_type)
+            two_s[rows, :] = low
+            mid_s[rows, :] = dot_nt(low, block(w_ref, 192)).astype(low_type)
+            return carry
+
+        lax.fori_loop(0, tiles, middle, 0)
+        grad_ref[:, 192:256, :] = dot_nn(mix_ref[0], two_s[...]).reshape(8, 64, D).astype(low_type)
+        for head in range(HEADS):
+            lanes = slice(head * HEAD_DIM, (head + 1) * HEAD_DIM)
+            key_lanes = slice(D + head * HEAD_DIM, D + (head + 1) * HEAD_DIM)
+            val_lanes = slice(2 * D + head * HEAD_DIM, 2 * D + (head + 1) * HEAD_DIM)
+            keys = qkv_ref[0, :, key_lanes]
+            keys_t = keys.T
+            vals = qkv_ref[0, :, val_lanes]
+            slope = 2.0 ** (-8.0 * (head + 1) / HEADS)
+            grad_vals = None
+            grad_keys = None
+            for i in range(tiles):
+                cols = slice(i * TILE, (i + 1) * TILE)
+                query = qkv_ref[0, cols, lanes]
+                grad_mix = mid_s[cols, lanes]
+                scores = dot_nt(keys, query) * HEAD_DIM**-0.5 - slope * far[:, cols]
+                prob = jnp.exp(scores - lse_ref[0, head, :, cols])
+                grad_prob = dot_nt(vals, grad_mix)
+                inner = jnp.sum(prob * grad_prob, axis=0, keepdims=True)
+                grad_raw = (prob * (grad_prob - inner) * HEAD_DIM**-0.5).astype(low_type)
+                back[cols, lanes] = dot_nn(keys_t, grad_raw).T.astype(low_type)
+                value_part = dot_nn(prob.astype(low_type), grad_mix)
+                key_part = dot_nn(grad_raw, query)
+                grad_vals = value_part if grad_vals is None else grad_vals + value_part
+                grad_keys = key_part if grad_keys is None else grad_keys + key_part
+            back[:, key_lanes] = grad_keys.astype(low_type)
+            back[:, val_lanes] = grad_vals.astype(low_type)
+
+        def leave(i, carry):
+            rows = pl.ds(pl.multiple_of(i * TILE, TILE), TILE)
+            total = dx[rows, :]
+            for j in range(3):
+                total = total + dot_nt(back[rows, j * D : (j + 1) * D], block(w_ref, j * 64))
+            dx[rows, :] = total
+            return carry
+
+        lax.fori_loop(0, tiles, leave, 0)
+        for j in range(3):
+            grad_ref[:, j * 64 : (j + 1) * 64, :] = (
+                dot_tn(low_ref[0], back[:, j * D : (j + 1) * D]).reshape(8, 64, D).astype(low_type)
+            )
+
+        @pl.when(step == LAYERS)
+        def _():
+            first_ref[...] = dx[...].astype(low_type)
+
+
+def run_backward(own, zed, pool, seg_col, seg_row, valid, weights, norms, saved):
+    low_x, qkv, lse, mix, one, two = saved
+    tokens = low_x.shape[1]
+    low = jnp.bfloat16
+    pick = lambda i: jnp.minimum(LAYERS - i, LAYERS - 1)
+    layered = lambda *s: pl.BlockSpec((1,) + s, lambda i: (pick(i),) + (0,) * len(s))
+    return pl.pallas_call(
+        backward_kernel,
+        grid=(LAYERS + 1,),
+        in_specs=[
+            whole((8, D)), whole((8, D)), whole((8, D)), whole((tokens, 1)), whole((1, tokens)), whole((1, tokens)),
+            pl.BlockSpec((8, PART, D), lambda i: (0, pick(i), 0)),
+            pl.BlockSpec((8, 64, D), lambda i: (0, HEAD_AT // 64, 0)),
+            whole(norms.shape),
+            layered(tokens, D), layered(tokens, 3 * D), layered(HEADS, 1, tokens), layered(D, tokens),
+            layered(tokens, D), layered(tokens, D),
+            pl.BlockSpec((1, tokens, D), lambda i: (LAYERS - 1, 0, 0)),
+        ],
+        out_specs=[
+            pl.BlockSpec((8, PART, D), lambda i: (0, LAYERS - i, 0)),
+            pl.BlockSpec((1, 8, D), lambda i: (LAYERS - i, 0, 0)),
+            whole((tokens, D)),
+        ],
+        out_shape=[
+            jax.ShapeDtypeStruct((8, PACKED, D), low),
+            jax.ShapeDtypeStruct((LAYERS + 1, 8, D), jnp.float32),
+            jax.ShapeDtypeStruct((tokens, D), low),
+        ],
+        scratch_shapes=[
+            pltpu.VMEM((tokens, D), jnp.float32), pltpu.VMEM((tokens, tokens), jnp.float32),
+            pltpu.VMEM((tokens, D), jnp.float32), pltpu.VMEM((tokens, D), low), pltpu.VMEM((tokens, D), low),
+            pltpu.VMEM((tokens, D), low), pltpu.VMEM((tokens, D), low), pltpu.VMEM((tokens, D), low),
+            pltpu.VMEM((tokens, 3 * D), low),
+        ],
+        compiler_params=pltpu.CompilerParams(vmem_limit_bytes=62 * 2**20),
+    )(own, zed, pool, seg_col, seg_row, valid, weights, weights, norms, low_x, qkv, lse, mix, one, two, two)
+
+
+def total_kernel(v_ref, o_ref, got, mine, ss, rs, ts, us, ls):
+    lin = lax.axis_index("dp") * 4 + lax.axis_index("group")
+    to = [lax.rem(lin + k, 32) for k in range(32)]
+    peers = [(p // 4, p % 4) for p in to]
+    entry_barrier(peers[1:])
+    first = [
+        pltpu.make_async_remote_copy(
+            v_ref.at[to[k]], got.at[k], ss.at[k], rs.at[k], device_id=peers[k], device_id_type=MESH
+        )
+        for k in range(1, 32)
+    ]
+    for copy in first:
+        copy.start()
+    own = pltpu.make_async_copy(v_ref.at[lin], got.at[0], ls.at[0])
+    own.start()
+    for copy in first:
+        copy.wait()
+    own.wait()
+    mine[...] = jnp.sum(got[...], axis=0)
+    second = [
+        pltpu.make_async_remote_copy(
+            mine, o_ref.at[lin], ts.at[k], us.at[k], device_id=peers[k], device_id_type=MESH
+        )
+        for k in range(1, 32)
+    ]
+    for copy in second:
+        copy.start()
+    own = pltpu.make_async_copy(mine, o_ref.at[lin], ls.at[1])
+    own.start()
+    for copy in second:
+        copy.wait()
+    own.wait()
+
+
+def total(v, cid):
+    sems = pltpu.SemaphoreType.DMA
+    return pl.pallas_call(
+        total_kernel,
+        out_shape=jax.ShapeDtypeStruct(v.shape, v.dtype),
+        in_specs=[pl.BlockSpec(memory_space=pltpu.VMEM)], out_specs=pl.BlockSpec(memory_space=pltpu.VMEM),
+        scratch_shapes=[
+            pltpu.VMEM(v.shape, v.dtype), pltpu.VMEM(v.shape[1:], v.dtype),
+            sems((32,)), sems((32,)), sems((32,)), sems((32,)), sems((2,)),
+        ],
+        compiler_params=pltpu.CompilerParams(collective_id=cid, has_side_effects=True),
+    )(v)
+
+
 def fast_shards(
     token_ids,
     seq_lengths,
@@ -846,135 +1331,27 @@
     def slot_rows():
         return jnp.take(got_rows.reshape(-1, D), jnp.minimum(key, 8 * SLOTS - 1), axis=0)
 
-    stream = lax.cond(crowded, dense_rows, slot_rows).astype(jnp.float32)
-    w_qkv = [whole_columns(weights[:, l * PART : l * PART + 192], 3) for l in range(LAYERS)]
-    w_attn = [weights[:, l * PART + 192 : l * PART + 256].reshape(D, D) for l in range(LAYERS)]
-    w_gate_up = [whole_columns(weights[:, l * PART + 256 : l * PART + 768], 8) for l in range(LAYERS)]
-    w_down = [weights[:, l * PART + 768 : l * PART + 1024].reshape(FF, D) for l in range(LAYERS)]
-    w_head = weights[:, HEAD_AT : HEAD_AT + 64].reshape(D, D)
-    norms = (
-        weights[:, NORM_AT : NORM_AT + 10, :64]
-        .transpose(1, 0, 2)
-        .reshape(5, 2, D)
-        .astype(jnp.float32)
-    )
-    kept_list = []
-    for layer_idx in range(LAYERS):
-        stream_low = stream.astype(jnp.bfloat16)
-        qkv_low = jnp.dot(stream_low, w_qkv[layer_idx], preferred_element_type=jnp.float32).astype(
-            jnp.bfloat16
-        )
-        mixed_heads, lse_all = attend(qkv_low, segment, head_count)
-        mixed_low = mixed_heads.astype(jnp.bfloat16)
-        resid_one = stream + jnp.dot(
-            mixed_low, w_attn[layer_idx], preferred_element_type=jnp.float32
-        )
-        normed = layer_norm(resid_one, norms[2 * layer_idx, 0], norms[2 * layer_idx, 1])
-        normed_low = normed.astype(jnp.bfloat16)
-        joined = jnp.dot(normed_low, w_gate_up[layer_idx], preferred_element_type=jnp.float32)
-        hidden_low = geglu(joined).astype(jnp.bfloat16)
-        resid_two = normed + jnp.dot(
-            hidden_low, w_down[layer_idx], preferred_element_type=jnp.float32
-        )
-        kept_list.append(
-            (
-                stream_low,
-                qkv_low,
-                lse_all,
-                mixed_low,
-                resid_one,
-                normed_low,
-                joined,
-                hidden_low,
-                resid_two,
-            )
-        )
-        stream = layer_norm(resid_two, norms[2 * layer_idx + 1, 0], norms[2 * layer_idx + 1, 1])
-    final = layer_norm(stream, norms[2 * LAYERS, 0], norms[2 * LAYERS, 1])
-    member = (
-        (segment[None, :] == jnp.arange(seq_count, dtype=jnp.int32)[:, None])
-        & (valid_mask[None, :] > 0)
-    ).astype(jnp.float32)
-    counts = jnp.maximum(jnp.sum(member, axis=1), 1.0)
-    pooled = jnp.matmul(member, final, precision=lax.Precision.HIGHEST) / counts[:, None]
-    pooled_low = pooled.astype(jnp.bfloat16)
-    head_out = jnp.dot(pooled_low, w_head, preferred_element_type=jnp.float32)
-    unit_vecs, unit_back = jax.vjp(normalize, head_out)
-    unit_every = spread(unit_vecs, 3).reshape(-1, D)
-    loss_value, loss_back = jax.vjp(
-        lambda unit_all, scale_arg: contrast(unit_all, scale_arg, deal_order), unit_every, log_scale
-    )
-    grad_units, grad_scale = loss_back(jnp.ones_like(loss_value))
-    own_rows = lax.dynamic_slice_in_dim(
-        grad_units, lax.axis_index(("dp", "group")) * seq_count, seq_count, 0
-    )
-    grad_head_out = unit_back(own_rows)[0].astype(jnp.bfloat16)
-    grad_head = jnp.dot(pooled_low.T, grad_head_out, preferred_element_type=jnp.float32)
-    grad_pooled = jnp.dot(grad_head_out, w_head.T, preferred_element_type=jnp.float32)
-    grad_final = jnp.matmul(
-        member.T, grad_pooled / counts[:, None], precision=lax.Precision.HIGHEST
-    )
-    final_back = jax.vjp(layer_norm, stream, norms[2 * LAYERS, 0], norms[2 * LAYERS, 1])[1]
-    grad_stream, gain_last, shift_last = final_back(grad_final)
-    norm_grads = [None] * (2 * LAYERS + 1)
-    norm_grads[2 * LAYERS] = jnp.stack([gain_last, shift_last])
-    packed_grads = [None] * LAYERS
-    for layer_idx in reversed(range(LAYERS)):
-        (
-            stream_low,
-            qkv_low,
-            lse_all,
-            mixed_low,
-            resid_one,
-            normed_low,
-            joined,
-            hidden_low,
-            resid_two,
-        ) = kept_list[layer_idx]
-        norm_two_back = jax.vjp(
-            layer_norm, resid_two, norms[2 * layer_idx + 1, 0], norms[2 * layer_idx + 1, 1]
-        )[1]
-        grad_two, gain_two, shift_two = norm_two_back(grad_stream)
-        norm_grads[2 * layer_idx + 1] = jnp.stack([gain_two, shift_two])
-        grad_branch = grad_two.astype(jnp.bfloat16)
-        down_grad = jnp.dot(hidden_low.T, grad_branch, preferred_element_type=jnp.float32)
-        grad_hidden = jnp.dot(grad_branch, w_down[layer_idx].T, preferred_element_type=jnp.float32)
-        grad_joined = jax.vjp(geglu, joined)[1](grad_hidden)[0].astype(jnp.bfloat16)
-        gate_grad = jnp.dot(normed_low.T, grad_joined, preferred_element_type=jnp.float32)
-        grad_normed = grad_two + jnp.dot(
-            grad_joined, w_gate_up[layer_idx].T, preferred_element_type=jnp.float32
-        )
-        norm_one_back = jax.vjp(
-            layer_norm, resid_one, norms[2 * layer_idx, 0], norms[2 * layer_idx, 1]
-        )[1]
-        grad_one, gain_one, shift_one = norm_one_back(grad_normed)
-        norm_grads[2 * layer_idx] = jnp.stack([gain_one, shift_one])
-        grad_attended = grad_one.astype(jnp.bfloat16)
-        attn_grad = jnp.dot(mixed_low.T, grad_attended, preferred_element_type=jnp.float32)
-        grad_mixed = jnp.dot(
-            grad_attended, w_attn[layer_idx].T, preferred_element_type=jnp.float32
-        ).astype(jnp.bfloat16)
-        grad_qkv_low = attend_back(qkv_low, segment, head_count, lse_all, grad_mixed)
-        qkv_grad = jnp.dot(stream_low.T, grad_qkv_low, preferred_element_type=jnp.float32)
-        grad_stream = grad_one + jnp.dot(
-            grad_qkv_low, w_qkv[layer_idx].T, preferred_element_type=jnp.float32
-        )
-        packed_grads[layer_idx] = jnp.concatenate(
-            [
-                owned_columns(qkv_grad),
-                owned_columns(attn_grad),
-                owned_columns(gate_grad),
-                down_grad.reshape(8, -1, D),
-            ],
-            axis=1,
-        ).astype(jnp.bfloat16)
-    head_part = owned_columns(grad_head).astype(jnp.bfloat16)
-    all_grads = jnp.concatenate(
-        packed_grads + [head_part, jnp.zeros((8, PACKED - NORM_AT, D), jnp.bfloat16)], axis=1
+    stream = lax.cond(crowded, dense_rows, slot_rows)
+    norms = jnp.pad(
+        weights[:, NORM_AT : NORM_AT + 10, :64].transpose(1, 0, 2).reshape(10, D).astype(jnp.float32),
+        ((0, 6), (0, 0)),
+    )
+    seg_col, seg_row = segment.reshape(-1, 1), segment.reshape(1, -1)
+    valid_row = valid_mask.reshape(1, -1)
+    *saved, unit_parts, pooled_low, head_out = run_forward(
+        stream, seg_col, seg_row, valid_row, weights, norms
+    )
+    loss_value, own_rows, grad_scale = run_contrast(unit_parts, deal_order, log_scale, 3)
+    loss_value, grad_scale = loss_value[0, 0], grad_scale[0]
+    all_grads, norm_parts_out, grad_first = run_backward(
+        own_rows, head_out, pooled_low, seg_col, seg_row, valid_row, weights, norms, saved
+    )
+    norm_grads = jnp.concatenate(
+        [norm_parts_out[:LAYERS, :4].reshape(-1, D), norm_parts_out[LAYERS, :2]], axis=0
     )
     slot_grads = jnp.dot(
         (jnp.arange(8 * SLOTS, dtype=jnp.int32)[:, None] == key[None, :]).astype(jnp.bfloat16),
-        grad_stream.astype(jnp.bfloat16),
+        grad_first,
         preferred_element_type=jnp.float32,
     ).astype(jnp.bfloat16)
     shard_grads, table_rows = scatter_grads(
@@ -983,7 +1360,7 @@
     table_slots = asked_here.reshape(8, 4, SLOTS).transpose(1, 0, 2).reshape(1, -1)
 
     def dense_grad():
-        total = jnp.zeros((shard_rows * 8, D), jnp.float32).at[token_ids].add(grad_stream)
+        total = jnp.zeros((shard_rows * 8, D), jnp.float32).at[token_ids].add(grad_first.astype(jnp.float32))
         return lax.psum(
             lax.psum_scatter(total, "dp", scatter_dimension=0, tiled=True), "group"
         )
@@ -1048,10 +1425,13 @@
         ]
     )
     row_parts = jnp.concatenate([jnp.sum(part, axis=-1) for part in rows_new])
-    col_sum, step_sum, row_sum, norm_grad = lax.psum(
-        (0.25 * col_parts, 0.25 * step_parts, 0.25 * row_parts, jnp.stack(norm_grads)),
-        ("dp", "group"),
-    )
+    width = col_parts.shape[0]
+    pieces = jnp.concatenate([0.25 * col_parts, 0.25 * step_parts, 0.25 * row_parts, norm_grads.reshape(-1)])
+    size = pieces.shape[0]
+    pieces = jnp.pad(pieces, (0, 32 * 1152 - size)).reshape(32, 9, 128)
+    sums = total(pieces, 4).reshape(-1)
+    col_sum, step_sum, row_sum = sums[:width], sums[width : 2 * width], sums[2 * width : 2 * width + 10]
+    norm_grad = sums[2 * width + 10 : size].reshape(2 * LAYERS + 1, 2, D)
     shard_norm = lax.dynamic_slice_in_dim(norm_grad, my_dp * 64, 64, 2)
     cols_new = []
     new_weights = []

time: 802 us -> 536 us (0.67)
  matrix products: 169 us -> 1.46 us
  Pallas kernels: 265 us -> 399 us
  waiting for transfers between devices: 120 us -> 0 us
  local copies, waits for them, and re-layouts: 116 us -> 39.7 us
  other arithmetic: 96.2 us -> 61.1 us
    dot_general x44 -> x0, matrix products: 168 us -> none  [the longest x2 31.5 us: attend_back(): jnp.einsum('hts,shc->thc', grad_raw, key_all, preferred_element_type=jnp....]
    pallas_call x0 -> x4, Pallas kernels: none -> 153 us  [the longest x1 77.5 us: run_backward(): pl.pallas_call(backward_kernel, grid=(LAYERS + 1,), in_specs=[whole((8, D...]
    psum x1 -> x0, waiting for transfers between devices: 120 us -> none  [fast_shards(): lax.psum((0.25 * col_parts, 0.25 * step_parts, 0.25 * row_parts, jnp.stac...]
    unnamed x354 -> x114, local copies, waits for them, and re-layouts: 46 us -> 6.4 us
    pallas_call x2 -> x1, Pallas kernels: 29.9 us -> 11.9 us  [spread(): pl.pallas_call(spread_kernel, out_shape=jax.ShapeDtypeStruct((32,) + v.sh...]
    reduce_sum x19 -> x0, other arithmetic: 12 us -> none  [the longest x2 3.48 us: layer_norm(): return center * lax.rsqrt(spread + NORM_EPS) * gain_vec + shift_vec]
    slice x5 -> x2, local copies, waits for them, and re-layouts: 12.4 us -> 0.83 us  [the longest x1 0.76 us: fast_shards(): norm_parts_out[:LAYERS, :4].reshape(-1, D)]
    reshape x7, local copies, waits for them, and re-layouts: 14.7 us -> 3.32 us  [the longest x1 0.97 us: fast_shards(): sums = total(pieces, 4).reshape(-1)]
  transfers between devices with their start and end apart: 1 -> 0, of which waited for: 1 -> 0; matrix products, arithmetic and copies ran while one was open for 0% -> 0% of each run, Pallas kernels for 0% -> 0%
where the time goes in v2:
time: 536 us; the launch traced here: 527 us
  Pallas kernels  399 us (74%)
  other arithmetic  61.1 us (11%)
  local copies, waits for them, and re-layouts  39.7 us (7%)
  between operations  26.1 us (5%)
    pallas_call x1, Pallas kernels, scatter_grads(): pl.pallas_call(functools.partial(scatter_kernel, chunks), out_shape=(jax....  116 us
    pallas_call x1, Pallas kernels, gather_weights(): pl.pallas_call(functools.partial(gather_kernel, chunks), out_shape=(jax.S...  102 us
    pallas_call x1, Pallas kernels, run_backward(): pl.pallas_call(backward_kernel, grid=(LAYERS + 1,), in_specs=[whole((8, D...  77.5 us
    pallas_call x1, Pallas kernels, run_forward(): pl.pallas_call(forward_kernel, grid=(LAYERS,), in_specs=[whole((tokens, D...  36.9 us
    add x6, other arithmetic, fast_shards(): master_list[i]  20.5 us
    pallas_call x1, Pallas kernels, run_contrast(): pl.pallas_call(contrast_kernel, out_shape=[one, jax.ShapeDtypeStruct((8,...  20.1 us
    pallas_call x1, Pallas kernels, total(): pl.pallas_call(total_kernel, out_shape=jax.ShapeDtypeStruct(v.shape, v.dt...  19 us
    pallas_call x1, Pallas kernels, place_rows(): pl.pallas_call(place_kernel, grid=(9,), in_specs=[pl.BlockSpec((1, slots....  14.8 us

profile of v2, /device:TPU:0, one launch (start us, length us, event | category | flops | bytes accessed | tf_op | source)
XLA Modules:
  0.0 527.5 jit_solution(10756138132511524712)
XLA Ops:
  7.9 1.0 select_reduce_fusion.1
  10.4 1.2 concatenate.31.v_ref
  11.6 11.9 %shard_map.339 = s32[32,8,128]{2,1,0:T(8,128)} custom-call(s32[8,128]{1,0:T(8,128)} %concatenate.31.v_ref), custom_call_target="tpu_custom_call" | custom-call | tf_op jit(solution)/shard_map/pallas_call | solution.py:541
  23.5 1.6 slice_reduce_fusion
  26.5 0.9 convert_element_type.57
  27.4 1.3 convert.25
  28.7 1.8 convert.24
  31.9 1.5 fusion.1.w_ref
  34.9 5.9 %gather_fusion.2 = bf16[768,512]{1,0:T(8,128)(2,1)S(1)} fusion(f32[3816,512]{1,0:T(8,128)} %param.29, s32[1024]{0:T(1024)S(1)} %pad_clamp_fusion.2), kind=kCustom, calls=%fused_computation.2 | custom fusion | bytes 1575936 | tf_op jit(solution)/shard_map/jit(_take)/gather | solution.py:1319
  40.8 1.1 select_convert_fusion.rows_ref
  41.9 102.4 %shard_map.340 = (bf16[8,2144,512]{2,1,0:T(8,128)(2,1)}, bf16[8,96,512]{2,1,0:T(8,128)(2,1)S(1)}) custom-call(bf16[2144,512]{1,0:T(8,128)(2,1)} %fusion.1.w_ref, bf16[8,96,512]{2,1,0:T(8,128)(2,1)} %select_convert_fusion.rows_ref), custom_call_target="tpu_custom_call" | custom-call | tf_op jit(solution)/shard_map/pallas_call | solution.py:517
  144.4 2.4 conditional.2
  144.5 2.0 gather_fusion
  149.5 36.9 %shard_map.341 = (bf16[2,512,512]{2,1,0:T(8,128)(2,1)}, bf16[2,512,1536]{2,1,0:T(8,128)(2,1)}, f32[2,8,1,512]{3,2,1,0:T(1,128)}, bf16[2,512,512]{2,1,0:T(8,128)(...) custom-call(bf16[512,512]{1,0:T(8,128)(2,1)S(1)} %get-tuple-element., ...), custom_call_target="tpu_custom_call" | custom-call | tf_op jit(solution)/shard_map/pallas_call | solution.py:948
  187.8 20.1 %shard_map.342 = (f32[1,1]{1,0:T(1,128)}, f32[8,512]{1,0:T(8,128)}, f32[1,1]{1,0:T(1,128)}) custom-call(f32[16,128]{1,0:T(8,128)} %get-tuple-element.71.unit_ref, s32[128,1]{1,0:T(8,128)} %copy.83.deal_col_ref, s32[1,128]{1,0:T(1,128)} %bitcast.164, f32[1,1]{1,0:T(1,128)} %bitcast.109.scale_ref), custom_call_target="tpu_custom_call" | custom-call | tf_op jit(solution)/shard_map/pallas_call | solution.py:1035
  207.9 77.5 %shard_map.343 = (bf16[8,2144,512]{2,1,0:T(8,128)(2,1)}, f32[3,8,512]{2,1,0:T(8,128)}, bf16[512,512]{1,0:T(8,128)(2,1)S(1)}) custom-call(f32[8,512]{1,0:T(8,128)} %get-tuple-element.73.own_ref, f32[8,512]{1,0:T(8,128)} %get-tuple-element.74.zed_ref, bf16[8,512]{1,0:T(8,128)(2,1)} %get-tuple-element.75.pool_ref, s32[512,1]{1,0:T(8,128)} %copy.82.seg_col_ref, ...), custom_call_target="tpu_custom_call" | custom-call | tf_op jit(solution)/shard_map/pallas_call | solution.py:1197
  285.4 1.5 fusion.3
  286.8 116.3 %shard_map.344 = (bf16[2144,512]{1,0:T(8,128)(2,1)}, bf16[4,8,96,512]{3,2,1,0:T(8,128)(2,1)S(1)}) custom-call(bf16[8,2144,512]{2,1,0:T(8,128)(2,1)} %get-tuple-element.82.g_ref, bf16[8,96,512]{2,1,0:T(8,128)(2,1)} %bitcast.133), custom_call_target="tpu_custom_call" | custom-call | tf_op jit(solution)/shard_map/pallas_call | solution.py:684
  403.1 14.9 %conditional.3 = (f32[3816,512]{1,0:T(8,128)}) conditional(s32[]{:T(128)} %convert_element_type.55, (s32[4,8,96]{2,0,1:T(4,128)S(1)}, bf16[4,8,96,512]{3,2,1,0:T(8,128)(2,1)S(1)}) %tuple.89, (s32[512]{0:T(512)S(1)}, bf16[512,512]{1,0:T(8,128)(2,1)}) %tuple.91), branch_computations={%region_9.10_spmd, %region_10.14_spmd} | conditional | flops 2479616 | bytes 325146752 | solution.py:1371
  403.3 14.8 %branch_0_fun.1 = f32[3816,512]{1,0:T(8,128)} custom-call(s32[1,3072]{1,0:T(1,128)S(1)} %reshape.567.slot_ref, bf16[3072,512]{1,0:T(8,128)(2,1)S(1)} %bitcast.126), custom_call_target="tpu_custom_call" | custom-call | tf_op jit(solution)/shard_map/cond/branch_0_fun/pallas_call | solution.py:779
  418.0 4.0 multiply_reduce_fusion.2
  423.5 1.8 multiply_reduce_fusion
  426.9 1.1 copy-done.3
  428.6 1.9 copy-done.1
  431.8 2.7 fusion.50
  435.1 1.2 stack_reshape.14
  436.3 1.3 constant_dynamic-update-slice_fusion.3
  437.6 2.8 copy.89
  440.4 2.4 stack_reshape.15
  442.8 1.3 constant_dynamic-update-slice_fusion.2
  444.5 1.1 fusion.8
  446.5 1.1 multiply_reduce_fusion.10
  448.1 1.4 fusion.5
  449.6 1.4 multiply_reduce_fusion.6
  451.2 1.4 concatenate.36
  454.9 19.0 %shard_map.345 = f32[32,9,128]{2,1,0:T(8,128)} custom-call(f32[32,9,128]{2,1,0:T(8,128)} %reshape.627.v_ref), custom_call_target="tpu_custom_call" | custom-call | tf_op jit(solution)/shard_map/pallas_call | solution.py:1265
  473.9 1.0 reshape.628
  476.8 1.2 divide_reduce_fusion
  478.8 9.2 %multiply_add_fusion = f32[3816,512]{1,0:T(8,128)} fusion(f32[3816,512]{1,0:T(8,128)} %param.29, f32[3816,512]{1,0:T(8,128)} %get-tuple-element.217, f32[512]{0:T(512)S(1)} %bitcast.157, f32[3816]{0:T(1024)S(1)} %rsqrt_multiply_fusion), kind=kLoop, calls=%fused_computation.13 | loop fusion | flops 5861376 | bytes 23462816 | tf_op jit(solution)/shard_map/add | solution.py:1459
  490.2 2.2 multiply_add_fusion.3
  493.0 1.3 fusion.37
  494.4 1.5 fusion.26
  497.1 1.8 multiply_add_fusion.4
  499.1 1.0 fusion.13
  501.5 3.3 multiply_add_fusion.1
  504.9 2.4 multiply_add_fusion.2
  508.7 1.7 multiply_add_fusion.5
  515.0 1.2 concatenate.40
  (220 shorter events, 28.1 us)
Async XLA Ops:
  28.7 2.6 copy-start.7
  28.7 2.7 copy-start.6
  31.8 1.7 copy-start.8
  34.8 109.6 %copy-start.14 = (s32[512]{0:T(512)S(1)}, s32[512]{0:T(512)}, u32[]{:S(2)}) copy-start(s32[512]{0:T(512)} %param.24) | copy-start | bytes 6148
  144.4 2.5 copy-start.47
  147.1 2.4 copy-start.19
  149.5 36.9 %copy-start.42 = (s32[128]{0:T(128)S(1)}, s32[128]{0:T(128)}, u32[]{:S(2)}) copy-start(s32[128]{0:T(128)} %param.27) | copy-start | bytes 1540
  285.4 1.5 copy-start.9
  418.0 4.0 copy-start.24
  418.0 5.5 %copy-start = (f32[3816,512]{1,0:T(8,128)S(1)}, f32[3816,512]{1,0:T(8,128)}, u32[]{:S(2)}) copy-start(f32[3816,512]{1,0:T(8,128)} %get-tuple-element.217) | copy-start | bytes 23445508
  422.0 3.3 copy-start.2
  422.6 56.1 %copy-start.11 = (f32[3816]{0:T(1024)}, f32[3816]{0:T(1024)S(1)}, u32[]{:S(2)}) copy-start(f32[3816]{0:T(1024)S(1)} %get-tuple-element.206) | copy-start | bytes 45796
  425.2 0.8 copy-start.45
  425.9 2.1 copy-start.3
  426.8 1.8 copy-start.44
  428.6 2.0 copy-start.1
  440.4 5.2 copy-start.25
  444.1 5.4 %copy-start.43 = (f32[2,256]{1,0:T(2,128)S(1)}, f32[2,256]{1,0:T(2,128)}, u32[]{:S(2)}) copy-start(f32[2,256]{1,0:T(2,128)} %param.39) | copy-start | bytes 6148
  444.3 2.1 copy-start.27
  444.5 2.0 copy-start.29
  444.5 32.3 %copy-start.41 = (f32[2,512]{1,0:T(2,128)S(1)}, f32[2,512]{1,0:T(2,128)}, u32[]{:S(2)}) copy-start(f32[2,512]{1,0:T(2,128)} %param.41) | copy-start | bytes 12292
  445.6 0.6 copy-start.31
  445.7 0.6 copy-start.33
  445.7 8.3 %copy-start.35 = (f32[2,64]{1,0:T(2,128)}, f32[2,64]{1,0:T(2,128)S(1)}, u32[]{:S(2)}) copy-start(f32[2,64]{1,0:T(2,128)S(1)} %get-tuple-element.126) | copy-start | bytes 1540
  445.7 8.3 %copy-start.36 = (f32[2,64]{1,0:T(2,128)}, f32[2,64]{1,0:T(2,128)S(1)}, u32[]{:S(2)}) copy-start(f32[2,64]{1,0:T(2,128)S(1)} %get-tuple-element.163) | copy-start | bytes 1540
  449.6 1.5 copy-start.21
  478.0 10.0 %copy-start.38 = (f32[1,512]{1,0:T(1,128)}, f32[1,512]{1,0:T(1,128)S(1)}, u32[]{:S(2)}) copy-start(f32[1,512]{1,0:T(1,128)S(1)} %get-tuple-element.156) | copy-start | bytes 6148
  478.7 9.2 %copy-start.5 = (f32[32,9,128]{2,1,0:T(8,128)S(1)}, f32[32,9,128]{2,1,0:T(8,128)}, u32[]{:S(2)}) copy-start(f32[32,9,128]{2,1,0:T(8,128)} %shard_map.345) | copy-start | bytes 442372
  478.8 11.3 %copy-start.34 = (f32[2,64]{1,0:T(2,128)S(1)}, f32[2,64]{1,0:T(2,128)}, u32[]{:S(2)}) copy-start(f32[2,64]{1,0:T(2,128)} %copy-done.33) | copy-start | bytes 1540
  489.5 0.7 copy-start.12
  492.3 12.6 %copy-start.4 = (f32[2,256,512]{2,1,0:T(8,128)S(1)}, f32[2,256,512]{2,1,0:T(8,128)}, u32[]{:S(2)}) copy-start(f32[2,256,512]{2,1,0:T(8,128)} %param.33) | copy-start | bytes 3145732
  494.4 6.3 %copy-start.17 = (f32[2,512]{1,0:T(2,128)}, f32[2,512]{1,0:T(2,128)S(1)}, u32[]{:S(2)}) copy-start(f32[2,512]{1,0:T(2,128)S(1)} %get-tuple-element.115) | copy-start | bytes 12292
  495.8 4.8 copy-start.15
  499.0 5.8 %copy-start.46 = (f32[2]{0:T(128)S(1)}, f32[2]{0:T(128)}, u32[]{:S(2)}) copy-start(f32[2]{0:T(128)} %get-tuple-element.108) | copy-start | bytes 28
  499.0 5.8 %copy-start.22 = (f32[2,256]{1,0:T(2,128)S(1)}, f32[2,256]{1,0:T(2,128)}, u32[]{:S(2)}) copy-start(f32[2,256]{1,0:T(2,128)} %copy-done.21) | copy-start | bytes 6148
  499.0 5.8 %copy-start.40 = (f32[2]{0:T(128)S(1)}, f32[2]{0:T(128)}, u32[]{:S(2)}) copy-start(f32[2]{0:T(128)} %get-tuple-element.152) | copy-start | bytes 28
  499.1 5.9 %copy-start.23 = (f32[2,512]{1,0:T(2,128)S(1)}, f32[2,512]{1,0:T(2,128)}, u32[]{:S(2)}) copy-start(f32[2,512]{1,0:T(2,128)} %get-tuple-element.114) | copy-start | bytes 12292
  501.4 5.9 %copy-start.37 = (f32[1,512]{1,0:T(1,128)S(1)}, f32[1,512]{1,0:T(1,128)}, u32[]{:S(2)}) copy-start(f32[1,512]{1,0:T(1,128)} %get-tuple-element.113) | copy-start | bytes 6148
  501.4 7.3 %copy-start.10 = (f32[64,512]{1,0:T(8,128)S(1)}, f32[64,512]{1,0:T(8,128)}, u32[]{:S(2)}) copy-start(f32[64,512]{1,0:T(8,128)} %param.34) | copy-start | bytes 393220
  501.4 9.1 %copy-start.20 = (f32[5,2,64]{2,1,0:T(2,128)S(1)}, f32[5,2,64]{2,1,0:T(2,128)}, u32[]{:S(2)}) copy-start(f32[5,2,64]{2,1,0:T(2,128)} %param.35) | copy-start | bytes 7684
  501.4 9.1 %copy-start.39 = (f32[5,2,64]{2,1,0:T(2,128)S(1)}, f32[5,2,64]{2,1,0:T(2,128)}, u32[]{:S(2)}) copy-start(f32[5,2,64]{2,1,0:T(2,128)} %param.42) | copy-start | bytes 7684
  501.4 12.3 %copy-start.26 = (f32[2,3,64]{2,0,1:T(2,128)S(1)}, f32[2,3,64]{2,0,1:T(2,128)}, u32[]{:S(2)}) copy-start(f32[2,3,64]{2,0,1:T(2,128)} %param.38) | copy-start | bytes 4612
  501.4 12.3 %copy-start.28 = (f32[2,64]{1,0:T(2,128)S(1)}, f32[2,64]{1,0:T(2,128)}, u32[]{:S(2)}) copy-start(f32[2,64]{1,0:T(2,128)} %copy-done.27) | copy-start | bytes 1540
  501.5 12.3 %copy-start.30 = (f32[2,64]{1,0:T(2,128)S(1)}, f32[2,64]{1,0:T(2,128)}, u32[]{:S(2)}) copy-start(f32[2,64]{1,0:T(2,128)} %copy-done.29) | copy-start | bytes 1540
  501.5 12.3 %copy-start.32 = (f32[2,64]{1,0:T(2,128)S(1)}, f32[2,64]{1,0:T(2,128)}, u32[]{:S(2)}) copy-start(f32[2,64]{1,0:T(2,128)} %copy-done.31) | copy-start | bytes 1540
  501.5 12.9 %copy-start.13 = (f32[2,1536]{1,0:T(2,128)S(1)}, f32[2,1536]{1,0:T(2,128)}, u32[]{:S(2)}) copy-start(f32[2,1536]{1,0:T(2,128)} %copy-done.12) | copy-start | bytes 36868
  501.5 12.9 %copy-start.16 = (f32[2,512]{1,0:T(2,128)S(1)}, f32[2,512]{1,0:T(2,128)}, u32[]{:S(2)}) copy-start(f32[2,512]{1,0:T(2,128)} %copy-done.15) | copy-start | bytes 12292
  501.5 12.9 %copy-start.18 = (f32[2,512]{1,0:T(2,128)S(1)}, f32[2,512]{1,0:T(2,128)}, u32[]{:S(2)}) copy-start(f32[2,512]{1,0:T(2,128)} %copy-done.17) | copy-start | bytes 12292

commit v3 on v2

--- a/solution.py
+++ b/solution.py
@@ -420,6 +420,13 @@
     )
 
 
+SLOTS = 96
+PART = 1024
+HEAD_AT = 2 * PART
+NORM_AT = HEAD_AT + 64
+PACKED = NORM_AT + 32
+
+
 MESH = pl.DeviceIdType.MESH
 BF=jnp.bfloat16
 
@@ -439,10 +446,13 @@
 def mult(v, m=16):
     return pl.multiple_of(v, m)
 
-def gather_kernel(chunks, w_ref, rows_ref, ag_ref, got_ref, zs, zr, xs, xr, ys, yr, cs, cr, ls, es, er):
+def gather_kernel(chunks, w_ref, ask_ref, table_ref, ag_ref, got_ref, asks_ref, table, picked, rows_s,
+                  zs, zr, xs, xr, ys, yr, cs, cr, ls, es, er, qs, qr):
     z, x, y, c = place()
     me = z * 2 + x
-    ep = [(lax.rem(me + k, 8), y * 2 + c) for k in range(8)]
+    g = y * 2 + c
+    g2 = (1 - y) * 2 + c
+    ep = [(lax.rem(me + k, 8), g) for k in range(8)]
     zp = [dev((z + k) % 4, x, y, c) for k in range(4)]
     xp, yp, cp = dev(z, 1 - x, y, c), dev(z, x, 1 - y, c), dev(z, x, y, 1 - c)
     entry_barrier(ep[1:] + [yp, cp])
@@ -457,13 +467,47 @@
         return pltpu.make_async_remote_copy(src, dst, s, r, device_id=d, device_id_type=MESH)
     def shard(k, f):
         return ((z + 4 - k) % 4) * 2 + (x if f == 0 else 1 - x)
-    own = pltpu.make_async_copy(w_ref, ag_ref.at[me], ls.at[0])
+    qc = [rc(ask_ref.at[ep[k][0]], asks_ref.at[g, me], qs.at[k], qr.at[k], ep[k]) for k in range(1, 8)]
+    for copy in qc:
+        copy.start()
+    mine = pltpu.make_async_copy(ask_ref.at[me], asks_ref.at[g, me], ls.at[0])
+    mine.start()
+    near = pltpu.make_async_copy(table_ref, table.at[pl.ds(0, table_ref.shape[0])], ls.at[1])
+    near.start()
+    qy = rc(asks_ref.at[g], asks_ref.at[g], qs.at[8], qr.at[8], yp)
+    qcc = rc(asks_ref.at[g], asks_ref.at[g], qs.at[9], qr.at[9], cp)
+    qd = rc(asks_ref.at[g2], asks_ref.at[g2], qs.at[10], qr.at[10], cp)
+    own = pltpu.make_async_copy(w_ref, ag_ref.at[me], ls.at[2])
     own.start()
-    kept = pltpu.make_async_copy(rows_ref.at[me], got_ref.at[me], ls.at[1])
-    kept.start()
-    ec = [rc(rows_ref.at[ep[k][0]], got_ref.at[me], es.at[k], er.at[k], ep[k]) for k in range(1, 8)]
-    for copy in ec:
-        copy.start()
+    kept = pltpu.make_async_copy(rows_s.at[me], got_ref.at[me], ls.at[3])
+    ec = [rc(rows_s.at[ep[k][0]], got_ref.at[me], es.at[k], er.at[k], ep[k]) for k in range(1, 8)]
+    def pick_rows():
+        mine.wait()
+        for copy in qc:
+            copy.wait_recv()
+        qy.start()
+        qcc.start()
+        wanted = asks_ref[pl.ds(g, 1)].reshape(8, 128).astype(jnp.float32).T
+        near.wait()
+        depth = table.shape[0] // 5
+        table[pl.ds(table_ref.shape[0], table.shape[0] - table_ref.shape[0]), :] = jnp.zeros(
+            (table.shape[0] - table_ref.shape[0], 512), jnp.float32
+        )
+        picked[...] = jnp.zeros(picked.shape, jnp.float32)
+        ramp = lax.broadcasted_iota(jnp.int32, (SLOTS, depth), 1).astype(jnp.float32)
+        def body(i, carry):
+            start = pl.multiple_of(i * depth, depth)
+            low = table[pl.ds(start, depth), :].astype(BF)
+            shifted = ramp + (i * depth).astype(jnp.float32)
+            for r in range(8):
+                hot = jnp.where(wanted[:SLOTS, r : r + 1] == shifted, 1.0, 0.0).astype(BF)
+                picked[r] += jnp.dot(hot, low, preferred_element_type=jnp.float32)
+            return carry
+        lax.fori_loop(0, 5, body, 0)
+        rows_s[...] = picked[...].astype(BF)
+        kept.start()
+        for copy in ec:
+            copy.start()
     zc = {}; xc = {}; yc = {}; cc = {}
     for q in range(Q):
         for k in range(1, 4):
@@ -500,6 +544,11 @@
             q = t - i
             if 0 <= q < Q:
                 st[i](q)
+        if t == 0:
+            pick_rows()
+        if t == 2:
+            qy.wait_recv()
+            qd.start()
     for q in range(Q):
         for k in range(4):
             for f in range(2):
@@ -508,46 +557,30 @@
         for v in d.values(): v.wait_send()
     for copy in ec:
         copy.wait()
+    qcc.wait_recv()
+    qd.wait_recv()
+    for copy in qc + [qy, qcc, qd]:
+        copy.wait_send()
     own.wait()
     kept.wait()
 
-def gather_weights(w, rows, chunks, cid=1):
+def gather_weights(w, asks, table, chunks, cid):
     Q = len(chunks)
     D = pltpu.SemaphoreType.DMA
+    anywhere = pl.BlockSpec(memory_space=pl.ANY)
+    near = pl.BlockSpec(memory_space=pltpu.VMEM)
+    padded = -(-table.shape[0] // 640) * 640
     return pl.pallas_call(
         functools.partial(gather_kernel, chunks),
-        out_shape=(jax.ShapeDtypeStruct((8,) + w.shape, w.dtype), jax.ShapeDtypeStruct(rows.shape, rows.dtype)),
-        in_specs=[pl.BlockSpec(memory_space=pl.ANY)] * 2, out_specs=[pl.BlockSpec(memory_space=pl.ANY)] * 2,
-        scratch_shapes=[D((Q, 4)), D((Q, 4)), D((Q, 4)), D((Q, 4)), D((Q, 8)), D((Q, 8)), D((Q, 8)), D((Q, 8)), D((2,)), D((8,)), D((8,))],
-        compiler_params=pltpu.CompilerParams(collective_id=cid, has_side_effects=True),
-    )(w, rows)
-
-def spread_kernel(v_ref, o_ref, ss, rs, ls):
-    lin = lax.axis_index("dp") * 4 + lax.axis_index("group")
-    peers = [lax.rem(lin + k, 32) for k in range(32)]
-    peers = [(p // 4, p % 4) for p in peers]
-    entry_barrier(peers[1:])
-    copies = [pltpu.make_async_remote_copy(v_ref, o_ref.at[lin], ss.at[k], rs.at[k], device_id=peers[k], device_id_type=MESH) for k in range(1, 32)]
-    for copy in copies:
-        copy.start()
-    own = pltpu.make_async_copy(v_ref, o_ref.at[lin], ls)
-    own.start()
-    for copy in copies:
-        copy.wait()
-    own.wait()
-
-def spread(v, cid):
-    D = pltpu.SemaphoreType.DMA
-    return pl.pallas_call(
-        spread_kernel,
-        out_shape=jax.ShapeDtypeStruct((32,) + v.shape, v.dtype),
-        in_specs=[pl.BlockSpec(memory_space=pltpu.VMEM)], out_specs=pl.BlockSpec(memory_space=pltpu.VMEM),
-        scratch_shapes=[D((32,)), D((32,)), D],
-        compiler_params=pltpu.CompilerParams(collective_id=cid, has_side_effects=True),
-    )(v)
-
-def scatter_kernel(chunks, g_ref, e_ref, out_ref, t_ref, acc, b1, b2, b3, b4, b5, fin,
-                   cs, cr, ys, yr, xs, xr, zs, zr, as_, ar, fs, fr, ls, os_, es, er, el):
+        out_shape=(jax.ShapeDtypeStruct((8,) + w.shape, w.dtype), jax.ShapeDtypeStruct((8, SLOTS, 512), BF), jax.ShapeDtypeStruct((4,) + asks.shape, asks.dtype)),
+        in_specs=[anywhere, near, anywhere], out_specs=[anywhere, anywhere, near],
+        scratch_shapes=[pltpu.VMEM((padded, 512), jnp.float32), pltpu.VMEM((8, SLOTS, 512), jnp.float32), pltpu.VMEM((8, SLOTS, 512), BF),
+            D((Q, 4)), D((Q, 4)), D((Q, 4)), D((Q, 4)), D((Q, 8)), D((Q, 8)), D((Q, 8)), D((Q, 8)), D((4,)), D((8,)), D((8,)), D((11,)), D((11,))],
+        compiler_params=pltpu.CompilerParams(collective_id=cid, has_side_effects=True, vmem_limit_bytes=48 * 2**20),
+    )(w, asks, table)
+
+def scatter_kernel(chunks, g_ref, e_ref, n_ref, out_ref, t_ref, n_out, nbuf, acc, b1, b2, b3, b4, b5, fin,
+                   cs, cr, ys, yr, xs, xr, zs, zr, as_, ar, fs, fr, ls, os_, es, er, el, ns, nr):
     z, x, y, c = place()
     me = z * 2 + x
     g = y * 2 + c
@@ -605,19 +638,27 @@
     EY = rc(t_ref.at[g], t_ref.at[g], es.at[8], er.at[8], yp)
     EC = rc(t_ref.at[g], t_ref.at[g], es.at[9], er.at[9], cp)
     ED = rc(t_ref.at[g2], t_ref.at[g2], es.at[10], er.at[10], cp)
+    NC = rc(n_ref, nbuf.at[0], ns.at[0], nr.at[0], cp)
+    NY = rc(nbuf.at[1], nbuf.at[2], ns.at[1], nr.at[1], yp)
     def e0():
+        NC.start()
         kept.start()
         for v in E: v.start()
     def e1():
+        NC.wait_recv()
+        nbuf[1] = nbuf[0] + n_ref[...]
+        NY.start()
         kept.wait()
         for v in E: v.wait_recv()
         EY.start(); EC.start()
     def e2():
+        NY.wait_recv()
+        n_out[...] = nbuf[1] + nbuf[2]
         EY.wait_recv()
         ED.start()
     def e3():
         EC.wait_recv(); ED.wait_recv()
-        for v in E + [EY, EC, ED]: v.wait_send()
+        for v in E + [EY, EC, ED, NC, NY]: v.wait_send()
     ev = {0: e0, 3: e1, 5: e2}
     def s0(q):
         for i in range(8):
@@ -676,20 +717,22 @@
         for v in d.values(): v.wait_send()
     e3()
 
-def scatter_grads(g, e, chunks, cid=2):
+def scatter_grads(g, e, n, chunks, cid):
     Q = len(chunks)
     D = pltpu.SemaphoreType.DMA
     H = sum(h for _, h, _ in chunks); NB = sum(nb for _, _, nb in chunks); NH = H - NB
     V = lambda *s: pltpu.VMEM(s, BF)
+    anywhere = pl.BlockSpec(memory_space=pl.ANY)
+    near = pl.BlockSpec(memory_space=pltpu.VMEM)
     return pl.pallas_call(
         functools.partial(scatter_kernel, chunks),
-        out_shape=(jax.ShapeDtypeStruct(g.shape[1:], g.dtype), jax.ShapeDtypeStruct((4,) + e.shape, e.dtype)),
-        in_specs=[pl.BlockSpec(memory_space=pl.ANY)] * 2, out_specs=[pl.BlockSpec(memory_space=pl.ANY)] * 2,
-        scratch_shapes=[V(8, H, 512), V(8, H, 512), V(8, NB, 512), V(4, NH, 512), V(3, NH, 512), V(H - 2 * NB, 512), V(H, 512),
+        out_shape=(jax.ShapeDtypeStruct(g.shape[1:], g.dtype), jax.ShapeDtypeStruct((4,) + e.shape, e.dtype), jax.ShapeDtypeStruct(n.shape, n.dtype)),
+        in_specs=[anywhere, anywhere, near], out_specs=[anywhere, anywhere, near],
+        scratch_shapes=[pltpu.VMEM((3,) + n.shape, n.dtype), V(8, H, 512), V(8, H, 512), V(8, NB, 512), V(4, NH, 512), V(3, NH, 512), V(H - 2 * NB, 512), V(H, 512),
             D((Q, 8)), D((Q, 8)), D((Q, 8)), D((Q, 8)), D((Q, 4)), D((Q, 4)), D((Q, 4)), D((Q, 4)), D((Q, 2)), D((Q, 2)), D((Q,)), D((Q,)), D((Q, 8)), D((Q,)),
-            D((11,)), D((11,)), D],
+            D((11,)), D((11,)), D, D((2,)), D((2,))],
         compiler_params=pltpu.CompilerParams(collective_id=cid, has_side_effects=True, vmem_limit_bytes=60 * 2**20),
-    )(g, e)
+    )(g, e, n)
 
 def plan(rows, count, share):
     units = rows // 32
@@ -700,13 +743,6 @@
         chunks.append((base, 16 * size, 16 * int(round(size * share))))
         base += 32 * size
     return chunks
-
-
-SLOTS = 96
-PART = 1024
-HEAD_AT = 2 * PART
-NORM_AT = HEAD_AT + 64
-PACKED = NORM_AT + 32
 
 
 def slot_plan(token_ids, shard_rows):
@@ -748,45 +784,6 @@
     return jnp.concatenate(
         [layers.reshape(-1, D), head_master.astype(jnp.bfloat16), norm_rows], axis=0
     )
-
-
-def whole_columns(part, blocks):
-    return (
-        part.reshape(8, blocks, -1, D).transpose(0, 2, 1, 3).reshape(-1, blocks * D)
-    )
-
-
-def shard_columns(part, blocks):
-    return part.reshape(blocks, -1, D).transpose(1, 0, 2).reshape(-1, blocks * D)
-
-
-def owned_columns(grad):
-    rows, width = grad.shape
-    return (
-        grad.reshape(8, rows // 8, width // D, D).transpose(0, 2, 1, 3).reshape(8, -1, D)
-    )
-
-
-def place_kernel(slot_ref, rows_ref, out_ref):
-    start = pl.program_id(0) * out_ref.shape[0]
-    rows = lax.broadcasted_iota(jnp.int32, (out_ref.shape[0], slot_ref.shape[1]), 0) + start
-    picks = jnp.where(rows == slot_ref[...], 1.0, 0.0).astype(jnp.bfloat16)
-    out_ref[...] = jnp.dot(picks, rows_ref[...], preferred_element_type=jnp.float32)
-
-
-def place_rows(slots, rows, row_count):
-    tile = row_count // 9
-    return pl.pallas_call(
-        place_kernel,
-        grid=(9,),
-        in_specs=[
-            pl.BlockSpec((1, slots.shape[1]), lambda i: (0, 0)),
-            pl.BlockSpec(rows.shape, lambda i: (0, 0)),
-        ],
-        out_specs=pl.BlockSpec((tile, D), lambda i: (i, 0)),
-        out_shape=jax.ShapeDtypeStruct((row_count, D), jnp.float32),
-        compiler_params=pltpu.CompilerParams(vmem_limit_bytes=48 * 2**20),
-    )(slots, rows)
 
 
 def dot_nn(left, right):
@@ -1227,15 +1224,18 @@
 
 
 def total_kernel(v_ref, o_ref, got, mine, ss, rs, ts, us, ls):
-    lin = lax.axis_index("dp") * 4 + lax.axis_index("group")
+    me = lax.axis_index("dp")
+    g = lax.axis_index("group")
+    lin = me * 4 + g
     to = [lax.rem(lin + k, 32) for k in range(32)]
     peers = [(p // 4, p % 4) for p in to]
+    owners = [(lax.rem(me + k, 8), g) for k in range(8)]
     entry_barrier(peers[1:])
     first = [
         pltpu.make_async_remote_copy(
-            v_ref.at[to[k]], got.at[k], ss.at[k], rs.at[k], device_id=peers[k], device_id_type=MESH
-        )
-        for k in range(1, 32)
+            v_ref.at[owners[k][0] * 4 + g], got.at[k], ss.at[k], rs.at[k], device_id=owners[k], device_id_type=MESH
+        )
+        for k in range(1, 8)
     ]
     for copy in first:
         copy.start()
@@ -1267,11 +1267,207 @@
         out_shape=jax.ShapeDtypeStruct(v.shape, v.dtype),
         in_specs=[pl.BlockSpec(memory_space=pltpu.VMEM)], out_specs=pl.BlockSpec(memory_space=pltpu.VMEM),
         scratch_shapes=[
-            pltpu.VMEM(v.shape, v.dtype), pltpu.VMEM(v.shape[1:], v.dtype),
-            sems((32,)), sems((32,)), sems((32,)), sems((32,)), sems((2,)),
+            pltpu.VMEM((8,) + v.shape[1:], v.dtype), pltpu.VMEM(v.shape[1:], v.dtype),
+            sems((8,)), sems((8,)), sems((32,)), sems((32,)), sems((2,)),
         ],
         compiler_params=pltpu.CompilerParams(collective_id=cid, has_side_effects=True),
     )(v)
+
+
+BLOCKS = 28
+STEP_AT = 28
+SUM_AT = 56
+NORM_ROW = 57
+ROW_TILE = 512
+RATES = (
+    RATE_SCALE, RATE_SCALE / D**0.5, RATE_SCALE / D**0.5, RATE_SCALE / (D // 8) ** 0.5,
+    RATE_SCALE / D**0.5, RATE_SCALE / FF**0.5,
+)
+
+
+def matrices(layer):
+    at = layer * PART
+    first = 2 + 13 * layer
+    return (
+        (2, at, 64, 3, first), (3, at + 192, 64, 1, first + 3),
+        (4, at + 256, 64, 8, first + 4), (5, at + 768, 256, 1, first + 12),
+    )
+
+
+def turn(row):
+    return jnp.broadcast_to(row, (8, row.shape[1])).T[:, 0:1]
+
+
+def lane_pick(value, lane):
+    return jnp.where(lax.broadcasted_iota(jnp.int32, (1, D), 1) == lane, value, 0.0)
+
+
+def stats_kernel(dense, row_count, *refs):
+    if dense:
+        full_ref, grads_ref, norm_ref, table_row_ref, rows_ref, down_ref, *outs = refs
+    else:
+        slot_ref, slot_rows_ref, grads_ref, norm_ref, table_row_ref, rows_ref, down_ref, *outs = refs
+    table_ref, table_row_out, stat_ref, rows_out, down_out = outs
+    step = pl.program_id(0)
+
+    def put(at, value):
+        stat_ref[at // 3, at % 3 : at % 3 + 1, :] = value
+
+    def add(at, value):
+        stat_ref[at // 3, at % 3 : at % 3 + 1, :] += value
+
+    @pl.when(step == 0)
+    def _():
+        stat_ref[...] = jnp.zeros(stat_ref.shape, jnp.float32)
+        for row in range(10):
+            put(NORM_ROW + row, norm_ref[row // 4, row % 4 : row % 4 + 1, :])
+        sums = jnp.zeros((1, D), jnp.float32)
+        rows_out[...] = jnp.zeros(rows_out.shape, jnp.float32)
+
+        def part(first, count, blocks, block_at, old):
+            squares = [
+                grads_ref[first + j * count : first + (j + 1) * count, :].astype(jnp.float32) ** 2 for j in range(blocks)
+            ]
+            mean = jnp.sum(functools.reduce(jnp.add, squares), axis=-1, keepdims=True) / (blocks * D)
+            new = DECAY_RATE * old + (1.0 - DECAY_RATE) * (mean + STATE_EPS)
+            inverse = 1.0 / new
+            for j in range(blocks):
+                put(block_at + j, jnp.sum(squares[j], axis=0, keepdims=True))
+                put(STEP_AT + block_at + j, jnp.sum(squares[j] * inverse, axis=0, keepdims=True))
+            return new, jnp.sum(new, axis=0, keepdims=True)
+
+        new, count = part(HEAD_AT, 64, 1, 1, rows_ref[:, 6:7])
+        rows_out[:, 6:7] = new
+        sums += lane_pick(count, 1)
+        for layer in range(LAYERS):
+            for name, first, rows, blocks, block_at in matrices(layer):
+                if name == 5:
+                    new, count = part(first, rows, blocks, block_at, down_ref[:, layer : layer + 1])
+                    down_out[:, layer : layer + 1] = new
+                else:
+                    lane = 3 * layer + name - 2
+                    new, count = part(first, rows, blocks, block_at, rows_ref[:, lane : lane + 1])
+                    rows_out[:, lane : lane + 1] = new
+                sums += lane_pick(count, 2 * name - 2 + layer)
+        put(SUM_AT, sums)
+
+    index = lax.broadcasted_iota(jnp.int32, (ROW_TILE, 1), 0) + step * ROW_TILE
+    if dense:
+        grad = jnp.where(index < row_count, full_ref[...], 0.0)
+    else:
+        picks = jnp.where(index == slot_ref[...], 1.0, 0.0).astype(jnp.bfloat16)
+        grad = jnp.dot(picks, slot_rows_ref[...], preferred_element_type=jnp.float32)
+    low = grad.astype(jnp.bfloat16)
+    table_ref[...] = low
+    squares = low.astype(jnp.float32) ** 2
+    mean = jnp.mean(squares, axis=-1, keepdims=True)
+    mean_row = jnp.broadcast_to(mean, (ROW_TILE, 128)).T[0:1, :]
+    new = DECAY_RATE * table_row_ref[...] + (1.0 - DECAY_RATE) * (mean_row + STATE_EPS)
+    real = lax.broadcasted_iota(jnp.int32, (1, ROW_TILE), 1) + step * ROW_TILE < row_count
+    new = jnp.where(real, new, 1.0)
+    table_row_out[...] = new
+    add(0, jnp.sum(squares, axis=0, keepdims=True))
+    add(STEP_AT, jnp.sum(squares * (1.0 / turn(new)), axis=0, keepdims=True))
+    add(SUM_AT, lane_pick(jnp.sum(jnp.where(real, new, 0.0), axis=1, keepdims=True), 0))
+
+
+def run_stats(dense, heads, grads, norm, table_row, rows, down):
+    row_count = table_row.shape[1]
+    tile = pl.BlockSpec((ROW_TILE, D), lambda i: (i, 0))
+    lane = pl.BlockSpec((1, ROW_TILE), lambda i: (0, i))
+    head_specs = [tile] if dense else [whole(v.shape) for v in heads]
+    stat = (32, 3, D)
+    return pl.pallas_call(
+        functools.partial(stats_kernel, dense, row_count),
+        grid=(-(-row_count // ROW_TILE),),
+        in_specs=head_specs + [whole(grads.shape), whole(norm.shape), lane, whole(rows.shape), whole(down.shape)],
+        out_specs=[tile, lane, whole(stat), whole(rows.shape), whole(down.shape)],
+        out_shape=[
+            jax.ShapeDtypeStruct((row_count, D), jnp.bfloat16), jax.ShapeDtypeStruct(table_row.shape, jnp.float32),
+            jax.ShapeDtypeStruct(stat, jnp.float32), jax.ShapeDtypeStruct(rows.shape, jnp.float32),
+            jax.ShapeDtypeStruct(down.shape, jnp.float32),
+        ],
+        compiler_params=pltpu.CompilerParams(vmem_limit_bytes=48 * 2**20),
+    )(*heads, grads, norm, table_row, rows, down)
+
+
+def update_kernel(
+    totals, stat_ref, table_ref, embed_ref, table_row_ref, grads_ref, rows_ref, down_ref, top_cols_ref, cols_ref,
+    in_ref, mix_ref, gate_ref, low_ref, head_ref,
+    embed_out, table_cols_out, head_cols_out, cols_out, in_out, mix_out, gate_out, low_out, head_out, rms_out, factors,
+):
+    step = pl.program_id(0)
+
+    def stat(at):
+        return stat_ref[at // 3, at % 3 : at % 3 + 1, :]
+
+    def mean_of(lane, name):
+        return jnp.sum(jnp.where(lax.broadcasted_iota(jnp.int32, (1, D), 1) == lane, stat(SUM_AT), 0.0), axis=1, keepdims=True) / totals[name]
+
+    def columns(block_at, blocks, old, lane, name):
+        row_mean = mean_of(lane, name)
+        news = []
+        steps = 0.0
+        for j in range(blocks):
+            new = DECAY_RATE * old(j) + (1.0 - DECAY_RATE) * (stat(block_at + j) / totals[name] + STATE_EPS)
+            news.append(new)
+            steps += jnp.sum(row_mean * stat(STEP_AT + block_at + j) / new, axis=1, keepdims=True)
+        rms = jnp.sqrt(steps / (totals[name] * blocks * D))
+        scale = -RATES[name] / jnp.maximum(1.0, rms / CLIP_LEVEL)
+        return news, row_mean, rms, scale
+
+    @pl.when(step == 0)
+    def _():
+        news, row_mean, rms, scale = columns(0, 1, lambda j: top_cols_ref[0:1, :], 0, 0)
+        table_cols_out[...] = news[0]
+        factors[0:1, :] = lax.rsqrt(news[0])
+        factors[1:2, :] = jnp.broadcast_to(row_mean, (1, D))
+        factors[2:3, :] = jnp.broadcast_to(scale, (1, D))
+        all_rms = lane_pick(rms, 0)
+        news, row_mean, rms, scale = columns(1, 1, lambda j: top_cols_ref[1:2, :], 1, 1)
+        head_cols_out[...] = news[0]
+        all_rms += lane_pick(rms, 1)
+        row = lax.rsqrt(rows_ref[:, 6:7] / row_mean) * scale
+        head_out[...] = head_ref[...] + grads_ref[HEAD_AT : HEAD_AT + 64, :].astype(jnp.float32) * row * lax.rsqrt(news[0])
+        for layer in range(LAYERS):
+            for name, first, rows, blocks, block_at in matrices(layer):
+                col_at = (block_at - 2 - 13 * layer) * D
+                old = lambda j: cols_ref[layer : layer + 1, col_at + j * D : col_at + (j + 1) * D]
+                news, row_mean, rms, scale = columns(block_at, blocks, old, 2 * name - 2 + layer, name)
+                all_rms += lane_pick(rms, 2 * name - 2 + layer)
+                lane = 3 * layer + name - 2
+                state = down_ref[:, layer : layer + 1] if name == 5 else rows_ref[:, lane : lane + 1]
+                row = lax.rsqrt(state / row_mean) * scale
+                source, target = ((in_ref, in_out), (mix_ref, mix_out), (gate_ref, gate_out), (low_ref, low_out))[name - 2]
+                for j in range(blocks):
+                    cols_out[layer : layer + 1, col_at + j * D : col_at + (j + 1) * D] = news[j]
+                    span = slice(j * D, (j + 1) * D)
+                    grad = grads_ref[first + j * rows : first + (j + 1) * rows, :].astype(jnp.float32)
+                    target[layer, :, span] = source[layer, :, span] + grad * row * lax.rsqrt(news[j])
+        rms_out[...] = all_rms
+
+    row = lax.rsqrt(turn(table_row_ref[...] / factors[1:2, :ROW_TILE])) * factors[2:3, 0:1]
+    embed_out[...] = embed_ref[...] + table_ref[...].astype(jnp.float32) * row * factors[0:1, :]
+
+
+def run_update(totals, stat, table, embed, table_row, grads, rows, down, top_cols, cols, others):
+    row_count = embed.shape[0]
+    tile = pl.BlockSpec((ROW_TILE, D), lambda i: (i, 0))
+    lane = pl.BlockSpec((1, ROW_TILE), lambda i: (0, i))
+    shape = lambda v: jax.ShapeDtypeStruct(v.shape, jnp.float32)
+    one = jax.ShapeDtypeStruct((1, D), jnp.float32)
+    outs = [shape(embed), one, one, shape(cols)] + [shape(v) for v in others] + [one]
+    return pl.pallas_call(
+        functools.partial(update_kernel, totals),
+        grid=(-(-row_count // ROW_TILE),),
+        in_specs=[whole(stat.shape), tile, tile, lane]
+        + [whole(v.shape) for v in (grads, rows, down, top_cols, cols)]
+        + [whole(v.shape) for v in others],
+        out_specs=[tile] + [whole(v.shape) for v in outs[1:]],
+        out_shape=outs,
+        scratch_shapes=[pltpu.VMEM((8, D), jnp.float32)],
+        compiler_params=pltpu.CompilerParams(vmem_limit_bytes=48 * 2**20),
+    )(stat, table, embed, table_row, grads, rows, down, top_cols, cols, *others)
 
 
 def fast_shards(
@@ -1297,32 +1493,19 @@
     scale_state,
 ):
     tokens = token_ids.shape[0]
-    seq_count = seq_lengths.shape[1]
-    head_count = HEADS
     shard_rows = embed_master.shape[0]
     my_dp = lax.axis_index("dp")
-    my_group = lax.axis_index("group")
     position = jnp.arange(tokens, dtype=jnp.int32)
     bounds = jnp.cumsum(seq_lengths[0])
     segment = jnp.sum((position[:, None] >= bounds[None, :]).astype(jnp.int32), axis=1)
 
     key, wanted, most = slot_plan(token_ids, shard_rows)
-    request = jnp.concatenate(
-        [wanted.reshape(-1, 128), jnp.broadcast_to(most, (2, 128))], axis=0
+    asks = jnp.concatenate(
+        [wanted.reshape(8, 1, SLOTS), jnp.broadcast_to(most, (8, 1, 128 - SLOTS))], axis=2
     ).astype(jnp.int32)
-    requests = spread(request, 0)
-    crowded = jnp.max(requests[:, 6]) >= SLOTS
-    asked = requests[:, :6].reshape(32, 8, SLOTS)
-    asked_here = lax.dynamic_index_in_dim(asked, my_dp, 1, keepdims=False)
-    group_asks = asked_here.reshape(8, 4, SLOTS)
-    to_send = lax.dynamic_index_in_dim(group_asks, my_group, 1, keepdims=False)
-    sent_rows = jnp.take(
-        embed_master, jnp.clip(to_send.reshape(-1), 0, shard_rows - 1), axis=0
-    ).astype(jnp.bfloat16)
     packed = pack_weights(attn_in, attn_out, ffn_in, ffn_out, head_master, norm_master)
-    weights, got_rows = gather_weights(
-        packed, sent_rows.reshape(8, SLOTS, D), plan(PACKED, 4, 0.36)
-    )
+    weights, got_rows, asked = gather_weights(packed, asks, embed_master, plan(PACKED, 4, 0.36), 0)
+    crowded = jnp.max(asked[:, :, 0, SLOTS:]) >= SLOTS
 
     def dense_rows():
         table = lax.all_gather(embed_master.astype(jnp.bfloat16), "dp", axis=0, tiled=True)
@@ -1341,148 +1524,72 @@
     *saved, unit_parts, pooled_low, head_out = run_forward(
         stream, seg_col, seg_row, valid_row, weights, norms
     )
-    loss_value, own_rows, grad_scale = run_contrast(unit_parts, deal_order, log_scale, 3)
+    loss_value, own_rows, grad_scale = run_contrast(unit_parts, deal_order, log_scale, 1)
     loss_value, grad_scale = loss_value[0, 0], grad_scale[0]
     all_grads, norm_parts_out, grad_first = run_backward(
         own_rows, head_out, pooled_low, seg_col, seg_row, valid_row, weights, norms, saved
-    )
-    norm_grads = jnp.concatenate(
-        [norm_parts_out[:LAYERS, :4].reshape(-1, D), norm_parts_out[LAYERS, :2]], axis=0
     )
     slot_grads = jnp.dot(
         (jnp.arange(8 * SLOTS, dtype=jnp.int32)[:, None] == key[None, :]).astype(jnp.bfloat16),
         grad_first,
         preferred_element_type=jnp.float32,
     ).astype(jnp.bfloat16)
-    shard_grads, table_rows = scatter_grads(
-        all_grads, slot_grads.reshape(8, SLOTS, D), plan(PACKED, 4, 0.29)
-    )
-    table_slots = asked_here.reshape(8, 4, SLOTS).transpose(1, 0, 2).reshape(1, -1)
-
-    def dense_grad():
-        total = jnp.zeros((shard_rows * 8, D), jnp.float32).at[token_ids].add(grad_first.astype(jnp.float32))
-        return lax.psum(
-            lax.psum_scatter(total, "dp", scatter_dimension=0, tiled=True), "group"
-        )
-
-    def slot_grad():
-        return place_rows(table_slots, table_rows.reshape(-1, D), shard_rows)
-
-    shard_embed = lax.cond(crowded, dense_grad, slot_grad)
-    shard_full = shard_grads.astype(jnp.float32)
-    shard_layers = shard_full[:HEAD_AT].reshape(LAYERS, PART, D)
-    shard_qkv = jnp.stack([shard_columns(shard_layers[l, :192], 3) for l in range(LAYERS)])
-    shard_attn = shard_layers[:, 192:256]
-    shard_gate_up = jnp.stack([shard_columns(shard_layers[l, 256:768], 8) for l in range(LAYERS)])
-    shard_down = shard_layers[:, 768:]
-    shard_head = shard_full[HEAD_AT : HEAD_AT + 64]
-    grad_list = [
-        shard_embed[None],
-        shard_head[None],
-        shard_qkv,
-        shard_attn,
-        shard_gate_up,
-        shard_down,
-    ]
-    master_list = [embed_master[None], head_master[None], attn_in, attn_out, ffn_in, ffn_out]
-    state_list = [
-        embed_rows[None],
-        head_rows[None],
-        layer_rows[:, 0],
-        layer_rows[:, 1],
-        layer_rows[:, 2],
-        ffn_out_rows,
-    ]
-    col_list = [
-        embed_head_cols[0:1],
-        embed_head_cols[1:2],
-        layer_cols[:, : 3 * D],
-        layer_cols[:, 3 * D : 4 * D],
-        layer_cols[:, 4 * D : 4 * D + 2 * FF],
-        layer_cols[:, 4 * D + 2 * FF :],
-    ]
-    total_rows = [VOCAB, D, D, D, D, FF]
-    wide_rate = RATE_SCALE / D**0.5
-    rates = [
-        RATE_SCALE,
-        wide_rate,
-        wide_rate,
-        RATE_SCALE / (D // 8) ** 0.5,
-        wide_rate,
-        RATE_SCALE / FF**0.5,
-    ]
-    square_list = [grad_part * grad_part for grad_part in grad_list]
-    rows_new = [
-        DECAY_RATE * state_list[i]
-        + (1.0 - DECAY_RATE) * (jnp.mean(square_list[i], axis=-1) + STATE_EPS)
-        for i in range(6)
-    ]
-    col_parts = jnp.concatenate([jnp.sum(part, axis=1).reshape(-1) for part in square_list])
-    step_parts = jnp.concatenate(
-        [
-            jnp.sum(square_list[i] * (1.0 / rows_new[i])[:, :, None], axis=1).reshape(-1)
-            for i in range(6)
-        ]
-    )
-    row_parts = jnp.concatenate([jnp.sum(part, axis=-1) for part in rows_new])
-    width = col_parts.shape[0]
-    pieces = jnp.concatenate([0.25 * col_parts, 0.25 * step_parts, 0.25 * row_parts, norm_grads.reshape(-1)])
-    size = pieces.shape[0]
-    pieces = jnp.pad(pieces, (0, 32 * 1152 - size)).reshape(32, 9, 128)
-    sums = total(pieces, 4).reshape(-1)
-    col_sum, step_sum, row_sum = sums[:width], sums[width : 2 * width], sums[2 * width : 2 * width + 10]
-    norm_grad = sums[2 * width + 10 : size].reshape(2 * LAYERS + 1, 2, D)
-    shard_norm = lax.dynamic_slice_in_dim(norm_grad, my_dp * 64, 64, 2)
-    cols_new = []
-    new_weights = []
-    rms_list = []
-    lead_start = 0
-    col_start = 0
-    for i in range(6):
-        lead_count, _, col_width = grad_list[i].shape
-        span = slice(col_start, col_start + lead_count * col_width)
-        row_mean = row_sum[lead_start : lead_start + lead_count] / total_rows[i]
-        col_state_new = DECAY_RATE * col_list[i] + (1.0 - DECAY_RATE) * (
-            col_sum[span].reshape(lead_count, col_width) / total_rows[i] + STATE_EPS
-        )
-        cols_new.append(col_state_new)
-        step_total = jnp.sum(
-            step_sum[span].reshape(lead_count, col_width) * row_mean[:, None] / col_state_new,
-            axis=1,
-        )
-        step_rms = jnp.sqrt(step_total / (total_rows[i] * col_width))
-        rms_list.append(step_rms)
-        row_factor = lax.rsqrt(rows_new[i] / row_mean[:, None]) * (
-            -rates[i] / jnp.maximum(1.0, step_rms / CLIP_LEVEL)[:, None]
-        )
-        new_weights.append(
-            master_list[i]
-            + grad_list[i] * row_factor[:, :, None] * lax.rsqrt(col_state_new)[:, None, :]
-        )
-        lead_start = lead_start + lead_count
-        col_start = col_start + lead_count * col_width
+    shard_grads, table_rows, norm_sum = scatter_grads(
+        all_grads, slot_grads.reshape(8, SLOTS, D), norm_parts_out, plan(PACKED, 4, 0.29), 2
+    )
+    table_slots = asked[:, :, 0, :SLOTS].reshape(1, -1)
+    table_row = embed_rows.reshape(1, -1)
+    row_state = jnp.pad(
+        jnp.concatenate([layer_rows.reshape(6, -1), head_rows.reshape(1, -1)], axis=0), ((0, 1), (0, 0))
+    ).T
+    shared = (shard_grads, norm_sum, table_row, row_state, ffn_out_rows.T)
+
+    def dense_stats():
+        full = jnp.zeros((shard_rows * 8, D), jnp.float32).at[token_ids].add(
+            grad_first.astype(jnp.float32)
+        )
+        full = lax.psum_scatter(full, "dp", scatter_dimension=0, tiled=True)
+        return run_stats(True, (lax.psum(full, "group"),), *shared)
+
+    def slot_stats():
+        return run_stats(False, (table_slots, table_rows.reshape(-1, D)), *shared)
+
+    table_grad, table_row_new, stats, rows_new, down_new = lax.cond(
+        crowded, dense_stats, slot_stats
+    )
+    sums = total(stats, 3)
+    totals = (VOCAB, D, D, D, D, FF)
+    (
+        new_embed, new_table_cols, new_head_cols, new_cols, new_in, new_mix, new_gate, new_low, new_head, rms_row,
+    ) = run_update(
+        totals, sums, table_grad, embed_master, table_row_new, shard_grads, rows_new, down_new,
+        embed_head_cols, layer_cols, (attn_in, attn_out, ffn_in, ffn_out, head_master),
+    )
+    norm_grad = sums.reshape(-1, D)[NORM_ROW : NORM_ROW + 10].reshape(2 * LAYERS + 1, 2, D)
+    shard_norm = lax.dynamic_slice_in_dim(norm_grad, my_dp * norm_state.shape[2], norm_state.shape[2], 2)
     norm_delta, norm_second = unfactored(shard_norm, norm_state)
     scale_delta, scale_state_new = unfactored(grad_scale, scale_state)
+    state_new = rows_new.T
     return (
         loss_value,
-        new_weights[0][0],
-        new_weights[2],
-        new_weights[3],
-        new_weights[4],
-        new_weights[5],
-        new_weights[1][0],
+        new_embed,
+        new_in,
+        new_mix,
+        new_gate,
+        new_low,
+        new_head,
         norm_master + norm_delta,
         log_scale + scale_delta,
-        rows_new[0][0],
-        rows_new[1][0],
-        jnp.stack([rows_new[2], rows_new[3], rows_new[4]], axis=1),
-        rows_new[5],
-        jnp.concatenate([cols_new[2], cols_new[3], cols_new[4], cols_new[5]], axis=1),
-        cols_new[0][0],
-        cols_new[1][0],
+        table_row_new[0],
+        state_new[6],
+        state_new[:6].reshape(layer_rows.shape),
+        down_new.T,
+        new_cols,
+        new_table_cols[0],
+        new_head_cols[0],
         norm_second,
         scale_state_new,
-        jnp.concatenate(rms_list),
+        rms_row[0, :10],
     )
 
 

time: 536 us -> 468 us (0.87)
  other arithmetic: 61.1 us -> 10.4 us
  local copies, waits for them, and re-layouts: 39.7 us -> 16.6 us
  Pallas kernels: 399 us -> 409 us
    add x10 -> x0, other arithmetic: 20.6 us -> none  [the longest x6 20.5 us: fast_shards(): master_list[i]]
    reduce_sum x20 -> x0, other arithmetic: 18 us -> none  [the longest x6 6.88 us: fast_shards(): jnp.mean(square_list[i], axis=-1) + STATE_EPS]
    pallas_call x2, Pallas kernels: 26.6 us -> 37.7 us  [the longest x1 23.6 us: run_stats(): pl.pallas_call(functools.partial(stats_kernel, dense, row_count), grid=(-...]
    gather x1 -> x0, local copies, waits for them, and re-layouts: 5.92 us -> none  [fast_shards(): jnp.take(embed_master, jnp.clip(to_send.reshape(-1), 0, shard_rows - 1),...]
    another operation x9 -> x2, local copies, waits for them, and re-layouts: 6.02 us -> 0.17 us  [the longest x3 4.85 us: fast_shards(): jnp.stack([shard_columns(shard_layers[l, 256:768], 8) for l in range(LAYE...]
where the time goes in v3:
time: 468 us; the launch traced here: 460 us
  Pallas kernels  409 us (87%)
  between operations  23 us (5%)
  local copies, waits for them, and re-layouts  16.6 us (4%)
  other arithmetic  10.4 us (2%)
    pallas_call x1, Pallas kernels, scatter_grads(): pl.pallas_call(functools.partial(scatter_kernel, chunks), out_shape=(jax....  117 us
    pallas_call x1, Pallas kernels, gather_weights(): pl.pallas_call(functools.partial(gather_kernel, chunks), out_shape=(jax.S...  104 us
    pallas_call x1, Pallas kernels, run_backward(): pl.pallas_call(backward_kernel, grid=(LAYERS + 1,), in_specs=[whole((8, D...  77.6 us
    pallas_call x1, Pallas kernels, run_forward(): pl.pallas_call(forward_kernel, grid=(LAYERS,), in_specs=[whole((tokens, D...  36.9 us
    pallas_call x1, Pallas kernels, run_stats(): pl.pallas_call(functools.partial(stats_kernel, dense, row_count), grid=(-...  23.6 us
    pallas_call x1, Pallas kernels, total(): pl.pallas_call(total_kernel, out_shape=jax.ShapeDtypeStruct(v.shape, v.dt...  17.4 us
    pallas_call x1, Pallas kernels, run_contrast(): pl.pallas_call(contrast_kernel, out_shape=[one, jax.ShapeDtypeStruct((8,...  17.2 us
    pallas_call x1, Pallas kernels, run_update(): pl.pallas_call(functools.partial(update_kernel, totals), grid=(-(-row_cou...  14.1 us

profile of v3, /device:TPU:0, one launch (start us, length us, event | category | flops | bytes accessed | tf_op | source)
XLA Modules:
  0.0 460.4 jit_solution(7840456416367270934)
XLA Ops:
  7.2 0.7 multiply_subtract_fusion
  7.9 1.0 select_reduce_fusion.1
  8.9 0.5 convert_reduce_fusion
  9.4 0.6 fusion.8
  10.1 0.3 select_reduce_fusion
  10.4 0.7 concatenate.15.ask_ref
  11.1 1.7 convert.24
  12.8 0.4 copy.103
  13.3 1.3 copy.90
  14.7 0.3 reshape.163
  15.0 0.1 copy.89
  15.2 1.4 pad_maximum_fusion
  16.6 0.1 fusion.1.w_ref
  16.8 104.4 %shard_map.339 = (bf16[8,2144,512]{2,1,0:T(8,128)(2,1)}, bf16[8,96,512]{2,1,0:T(8,128)(2,1)S(1)}, s32[4,8,1,128]{3,2,1,0:T(1,128)S(1)}) custom-call(bf16[2144,512]{1,0:T(8,128)(2,1)S(1)} %fusion.1.w_ref, s32[8,1,128]{2,1,0:T(1,128)S(1)} %concatenate.15.ask_ref, f32[3816,512]{1,0:T(8,128)} %embed_ref.1), custom_call_target="tpu_custom_call" | custom-call | tf_op jit(solution)/shard_map/pallas_call | solution.py:573
  121.2 0.7 slice_reduce_fusion.1
  122.6 2.4 conditional.2
  122.7 2.0 gather_fusion
  124.7 0.1 broadcast_select_fusion
  125.1 0.8 slice_bitcast_fusion
  125.8 0.1 convert_element_type.55
  125.9 0.6 pad_convert_fusion.norm_ref
  126.6 0.2 reduce-window.8
  126.7 0.1 convert_reduce_fusion.1
  126.8 0.9 copy.92.seg_col_ref
  127.7 36.9 %shard_map.340 = (bf16[2,512,512]{2,1,0:T(8,128)(2,1)}, bf16[2,512,1536]{2,1,0:T(8,128)(2,1)}, f32[2,8,1,512]{3,2,1,0:T(1,128)}, bf16[2,512,512]{2,1,0:T(8,128)(...) custom-call(bf16[512,512]{1,0:T(8,128)(2,1)S(1)} %get-tuple-element., ...), custom_call_target="tpu_custom_call" | custom-call | tf_op jit(solution)/shard_map/pallas_call | solution.py:945
  165.2 0.7 copy.93.deal_col_ref
  166.0 17.2 %shard_map.341 = (f32[1,1]{1,0:T(1,128)}, f32[8,512]{1,0:T(8,128)}, f32[1,1]{1,0:T(1,128)}) custom-call(f32[16,128]{1,0:T(8,128)} %get-tuple-element.139.unit_ref, s32[128,1]{1,0:T(8,128)} %copy.93.deal_col_ref, s32[1,128]{1,0:T(1,128)} %bitcast.68, f32[1,1]{1,0:T(1,128)} %bitcast.47.scale_ref), custom_call_target="tpu_custom_call" | custom-call | tf_op jit(solution)/shard_map/pallas_call | solution.py:1032
  183.2 77.6 %shard_map.342 = (bf16[8,2144,512]{2,1,0:T(8,128)(2,1)}, f32[3,8,512]{2,1,0:T(8,128)}, bf16[512,512]{1,0:T(8,128)(2,1)S(1)}) custom-call(f32[8,512]{1,0:T(8,128)} %get-tuple-element.141.own_ref, f32[8,512]{1,0:T(8,128)} %get-tuple-element.142.zed_ref, bf16[8,512]{1,0:T(8,128)(2,1)} %get-tuple-element.143.pool_ref, s32[512,1]{1,0:T(8,128)} %copy.92.seg_col_ref, ...), custom_call_target="tpu_custom_call" | custom-call | tf_op jit(solution)/shard_map/pallas_call | solution.py:1194
  260.7 1.5 fusion.3
  262.2 117.5 %shard_map.343 = (bf16[2144,512]{1,0:T(8,128)(2,1)}, bf16[4,8,96,512]{3,2,1,0:T(8,128)(2,1)}, f32[3,8,512]{2,1,0:T(8,128)S(1)}) custom-call(bf16[8,2144,512]{2,1,0:T(8,128)(2,1)} %get-tuple-element.150.g_ref, bf16[8,96,512]{2,1,0:T(8,128)(2,1)} %bitcast.58, f32[3,8,512]{2,1,0:T(8,128)} %get-tuple-element.152.n_ref), custom_call_target="tpu_custom_call" | custom-call | tf_op jit(solution)/shard_map/pallas_call | solution.py:727
  379.7 0.1 copy.96
  380.0 24.5 %conditional.3 = (bf16[3816,512]{1,0:T(8,128)(2,1)}, f32[1,3816]{1,0:T(1,128)}, f32[32,3,512]{2,1,0:T(4,128)}, f32[64,8]{1,0:T(8,128)}, f32[256,2]{1,0:T(8,128)}, /*index=5*/f32[3816]{0:T(1024)S(1)}) conditional(s32[]{:T(128)} %convert_element_type.52, (s32[4,8,1,128]{3,2,1,0:T(1,128)S(1)}, bf16[4,8,96,512]{3,2,1,0:T(8,128)(2,1)}, ...), branch_computations={%region_9.10_spmd, %region_10.14_spmd} | conditional | flops 2479616 | bytes 325181440 | solution.py:1557
  380.0 0.1 copy.98.refs_5_
  380.2 23.6 %branch_0_fun.1 = (bf16[3816,512]{1,0:T(8,128)(2,1)}, f32[1,3816]{1,0:T(1,128)}, f32[32,3,512]{2,1,0:T(4,128)}, f32[64,8]{1,0:T(8,128)}, f32[256,2]{1,0:T(8,128)}) custom-call(s32[1,3072]{1,0:T(1,128)S(1)} %reshape_squeeze.3.refs_0_, bf16[3072,512]{1,0:T(8,128)(2,1)} %bitcast.53, bf16[2144,512]{1,0:T(8,128)(2,1)} %get-tuple-element.58.refs_2_, ...), custom_call_target="tpu_custom_call" | custom-call | tf_op jit(solution)/shard_map/cond/branch_0_fun/pallas_call | solution.py:1380
  403.8 0.8 reduce.1
  404.5 17.4 %shard_map.344.stat_ref = f32[32,3,512]{2,1,0:T(4,128)} custom-call(f32[32,3,512]{2,1,0:T(4,128)} %get-tuple-element.156.v_ref), custom_call_target="tpu_custom_call" | custom-call | tf_op jit(solution)/shard_map/pallas_call | solution.py:1265
  422.0 1.1 copy-done.3
  423.2 0.9 copy-done.4
  424.1 0.9 copy-done.7
  425.1 0.8 copy-done.9
  425.9 14.1 %shard_map.345 = (f32[3816,512]{1,0:T(8,128)}, f32[1,512]{1,0:T(1,128)}, f32[1,512]{1,0:T(1,128)}, f32[2,6656]{1,0:T(2,128)}, f32[2,64,1536]{2,1,0:T(8,128)}, /*...) custom-call(f32[32,3,512]{2,1,0:T(4,128)S(1)} %copy-done.4, ...), custom_call_target="tpu_custom_call" | custom-call | tf_op jit(solution)/shard_map/pallas_call | solution.py:1460
  440.0 0.5 slice_bitcast_fusion.1
  443.2 0.1 reshape.180
  443.4 1.4 multiply_add_fusion
  444.8 0.8 copy.100
  445.6 0.6 copy.102
  446.2 1.6 copy.101
  447.8 1.5 slice_reduce_fusion
  (65 shorter events, 0.6 us)
Async XLA Ops:
  12.8 1.8 copy-start.2
  13.2 1.8 copy-start.1
  13.3 1.9 copy-start.6
  14.7 1.9 copy-start.8
  14.7 1.9 copy-start.16
  16.8 105.8 %copy-start.12 = (s32[512]{0:T(512)S(1)}, s32[512]{0:T(512)}, u32[]{:S(2)}) copy-start(s32[512]{0:T(512)} %param.24) | copy-start | bytes 6148
  121.2 1.4 copy-start.13
  122.6 4.0 copy-start.23
  126.8 0.9 copy-start.15
  127.7 37.5 %copy-start.21 = (s32[128]{0:T(128)S(1)}, s32[128]{0:T(128)}, u32[]{:S(2)}) copy-start(s32[128]{0:T(128)} %param.27) | copy-start | bytes 1540
  260.7 119.0 %copy-start.11 = (bf16[512,512]{1,0:T(8,128)(2,1)}, bf16[512,512]{1,0:T(8,128)(2,1)S(1)}, u32[]{:S(2)}) copy-start(bf16[512,512]{1,0:T(8,128)(2,1)S(1)} %get-tuple-element.151) | copy-start | bytes 1572868
  262.2 117.5 %copy-start.20 = (f32[2,256]{1,0:T(2,128)S(1)}, f32[2,256]{1,0:T(2,128)}, u32[]{:S(2)}) copy-start(f32[2,256]{1,0:T(2,128)} %param.39) | copy-start | bytes 6148
  262.2 117.7 %copy-start.17 = (f32[3816]{0:T(1024)S(1)}, f32[3816]{0:T(1024)}, u32[]{:S(2)}) copy-start(f32[3816]{0:T(1024)} %param.36) | copy-start | bytes 45796
  262.2 117.7 %copy-start.19 = (f32[2,3,64]{2,0,1:T(2,128)S(1)}, f32[2,3,64]{2,0,1:T(2,128)}, u32[]{:S(2)}) copy-start(f32[2,3,64]{2,0,1:T(2,128)} %param.38) | copy-start | bytes 4612
  262.2 117.7 %copy-start.22 = (f32[64]{0:T(128)S(1)}, f32[64]{0:T(128)}, u32[]{:S(2)}) copy-start(f32[64]{0:T(128)} %param.37) | copy-start | bytes 772
  262.2 117.7 %copy-start.14 = (s32[4,8,1,128]{3,2,1,0:T(1,128)S(1)}, s32[4,8,1,128]{3,2,1,0:T(1,128)}, u32[]{:S(2)}) copy-start(s32[4,8,1,128]{3,2,1,0:T(1,128)} %copy-done.13) | copy-start | bytes 49156
  380.0 42.0 %copy-start = (f32[2,64,4096]{2,1,0:T(8,128)S(1)}, f32[2,64,4096]{2,1,0:T(8,128)}, u32[]{:S(2)}) copy-start(f32[2,64,4096]{2,1,0:T(8,128)} %gate_ref.1) | copy-start | bytes 6291460
  380.0 42.0 %copy-start.10 = (f32[2,512]{1,0:T(2,128)S(1)}, f32[2,512]{1,0:T(2,128)}, u32[]{:S(2)}) copy-start(f32[2,512]{1,0:T(2,128)} %top_cols_ref.1) | copy-start | bytes 12292
  404.5 17.5 %copy-start.18 = (f32[3816]{0:T(1024)}, f32[3816]{0:T(1024)S(1)}, u32[]{:S(2)}) copy-start(f32[3816]{0:T(1024)S(1)} %get-tuple-element.358) | copy-start | bytes 45796
  422.0 1.1 copy-start.3
  423.2 0.9 copy-start.4
  424.1 0.9 copy-start.7
  425.1 0.8 copy-start.9
  425.9 17.4 %copy-start.5 = (f32[32,3,512]{2,1,0:T(4,128)S(1)}, f32[32,3,512]{2,1,0:T(4,128)}, u32[]{:S(2)}) copy-start(f32[32,3,512]{2,1,0:T(4,128)} %shard_map.344.stat_ref) | copy-start | bytes 589828

commit v4 on v3

--- a/solution.py
+++ b/solution.py
@@ -420,7 +420,7 @@
     )
 
 
-SLOTS = 96
+SLOTS = 80
 PART = 1024
 HEAD_AT = 2 * PART
 NORM_AT = HEAD_AT + 64
@@ -579,161 +579,6 @@
         compiler_params=pltpu.CompilerParams(collective_id=cid, has_side_effects=True, vmem_limit_bytes=48 * 2**20),
     )(w, asks, table)
 
-def scatter_kernel(chunks, g_ref, e_ref, n_ref, out_ref, t_ref, n_out, nbuf, acc, b1, b2, b3, b4, b5, fin,
-                   cs, cr, ys, yr, xs, xr, zs, zr, as_, ar, fs, fr, ls, os_, es, er, el, ns, nr):
-    z, x, y, c = place()
-    me = z * 2 + x
-    g = y * 2 + c
-    ep = [(lax.rem(me + k, 8), g) for k in range(8)]
-    zp = [dev((z + k) % 4, x, y, c) for k in range(4)]
-    xp, yp, cp = dev(z, 1 - x, y, c), dev(z, x, 1 - y, c), dev(z, x, y, 1 - c)
-    entry_barrier(ep[1:] + [yp, cp])
-    Q = len(chunks)
-    lo = []; o = 0; lb = []; ob = 0; lh = []; oh = 0; la = []; oa = 0
-    for b, h, nb in chunks:
-        lo.append(o); o += h
-        lb.append(ob); ob += nb
-        lh.append(oh); oh += h - nb
-        la.append(oa); oa += h - 2 * nb
-    nh = [h - nb for b, h, nb in chunks]
-    nbs = [nb for b, h, nb in chunks]
-    na = [h - 2 * nb for b, h, nb in chunks]
-    hs = [mult(lo[q] + y * nbs[q]) for q in range(Q)]
-    mb = [mult(lo[q] + y * nh[q]) for q in range(Q)]
-    ob_ = [mult(lo[q] + (1 - y) * nh[q]) for q in range(Q)]
-    aa = [lo[q] + nbs[q] for q in range(Q)]
-    def rc(src, dst, s, r, d):
-        return pltpu.make_async_remote_copy(src, dst, s, r, device_id=d, device_id_type=MESH)
-    def add(dst, src, n, blk=16):
-        def body(i, _):
-            a = mult(i * blk)
-            d = dst(a, blk); s = src(a, blk)
-            d[...] = (d[...].astype(jnp.float32) + s[...].astype(jnp.float32)).astype(BF)
-            return _
-        lax.fori_loop(0, n // blk, body, 0)
-    order = []
-    for k in (2, 1, 3, 0):
-        for f in (1, 0):
-            order.append((k, f))
-    def owner(k, f):
-        return ((z + k) % 4) * 2 + (x if f == 0 else 1 - x)
-    C1 = {}; Y = {}; X = {}; Z = {}; A = {}; F = {}; L = {}; O = {}; BX = {}
-    for q, (b, h, nb) in enumerate(chunks):
-        for i, (k, f) in enumerate(order):
-            s = owner(k, f)
-            L[q, i] = pltpu.make_async_copy(g_ref.at[s, pl.ds(mult(b + c * h), h)], acc.at[s, pl.ds(lo[q], h)], ls.at[q, i])
-            C1[q, i] = rc(g_ref.at[s, pl.ds(mult(b + (1 - c) * h), h)], b1.at[s, pl.ds(lo[q], h)], cs.at[q, i], cr.at[q, i], cp)
-            Y[q, i] = rc(acc.at[s, pl.ds(ob_[q], nb)], b2.at[s, pl.ds(lb[q], nb)], ys.at[q, i], yr.at[q, i], yp)
-        for k in range(4):
-            X[q, k] = rc(acc.at[owner(k, 1), pl.ds(hs[q], nh[q])], b3.at[k, pl.ds(lh[q], nh[q])], xs.at[q, k], xr.at[q, k], xp)
-            if k:
-                Z[q, k] = rc(acc.at[owner(k, 0), pl.ds(hs[q], nh[q])], b4.at[k - 1, pl.ds(lh[q], nh[q])], zs.at[q, k], zr.at[q, k], zp[k])
-        A[q] = rc(fin.at[pl.ds(aa[q], na[q])], b5.at[pl.ds(la[q], na[q])], as_.at[q, 0], ar.at[q, 0], yp)
-        BX[q] = rc(fin.at[pl.ds(mb[q], nb)], fin.at[pl.ds(mb[q], nb)], as_.at[q, 1], ar.at[q, 1], yp)
-        F[q] = rc(fin.at[pl.ds(lo[q], h)], out_ref.at[pl.ds(mult(b + c * h), h)], fs.at[q], fr.at[q], cp)
-        O[q] = pltpu.make_async_copy(fin.at[pl.ds(lo[q], h)], out_ref.at[pl.ds(mult(b + c * h), h)], os_.at[q])
-    g2 = (1 - y) * 2 + c
-    kept = pltpu.make_async_copy(e_ref.at[me], t_ref.at[g, me], el)
-    E = [rc(e_ref.at[ep[k][0]], t_ref.at[g, me], es.at[k], er.at[k], ep[k]) for k in range(1, 8)]
-    EY = rc(t_ref.at[g], t_ref.at[g], es.at[8], er.at[8], yp)
-    EC = rc(t_ref.at[g], t_ref.at[g], es.at[9], er.at[9], cp)
-    ED = rc(t_ref.at[g2], t_ref.at[g2], es.at[10], er.at[10], cp)
-    NC = rc(n_ref, nbuf.at[0], ns.at[0], nr.at[0], cp)
-    NY = rc(nbuf.at[1], nbuf.at[2], ns.at[1], nr.at[1], yp)
-    def e0():
-        NC.start()
-        kept.start()
-        for v in E: v.start()
-    def e1():
-        NC.wait_recv()
-        nbuf[1] = nbuf[0] + n_ref[...]
-        NY.start()
-        kept.wait()
-        for v in E: v.wait_recv()
-        EY.start(); EC.start()
-    def e2():
-        NY.wait_recv()
-        n_out[...] = nbuf[1] + nbuf[2]
-        EY.wait_recv()
-        ED.start()
-    def e3():
-        EC.wait_recv(); ED.wait_recv()
-        for v in E + [EY, EC, ED, NC, NY]: v.wait_send()
-    ev = {0: e0, 3: e1, 5: e2}
-    def s0(q):
-        for i in range(8):
-            L[q, i].start(); C1[q, i].start()
-    def s1(q):
-        h = chunks[q][1]
-        for i, (k, f) in enumerate(order):
-            s = owner(k, f)
-            L[q, i].wait(); C1[q, i].wait_recv()
-            add(lambda a, n: acc.at[s, pl.ds(lo[q] + a, n)], lambda a, n: b1.at[s, pl.ds(lo[q] + a, n)], h)
-            Y[q, i].start()
-    def s2(q):
-        for i, (k, f) in enumerate(order):
-            s = owner(k, f)
-            if nbs[q]:
-                Y[q, i].wait_recv()
-                add(lambda a, n: acc.at[s, pl.ds(mb[q] + a, n)], lambda a, n: b2.at[s, pl.ds(lb[q] + a, n)], nbs[q])
-            if f == 1:
-                X[q, k].start()
-    def s3(q):
-        for k in (2, 1, 3, 0):
-            s = owner(k, 0)
-            X[q, k].wait_recv()
-            add(lambda a, n: acc.at[s, pl.ds(hs[q] + a, n)], lambda a, n: b3.at[k, pl.ds(lh[q] + a, n)], nh[q])
-            if k: Z[q, k].start()
-    def s4(q):
-        for k in range(1, 4):
-            Z[q, k].wait_recv()
-        def body(i, _):
-            a = mult(i * 16)
-            t = acc[me, pl.ds(hs[q] + a, 16)].astype(jnp.float32)
-            for k in range(3):
-                t += b4[k, pl.ds(lh[q] + a, 16)].astype(jnp.float32)
-            fin[pl.ds(hs[q] + a, 16)] = t.astype(BF)
-            return _
-        lax.fori_loop(0, nh[q] // 16, body, 0)
-        A[q].start()
-        BX[q].start()
-    def s5(q):
-        A[q].wait_recv()
-        A[q].wait_send()
-        add(lambda a, n: fin.at[pl.ds(aa[q] + a, n)], lambda a, n: b5.at[pl.ds(la[q] + a, n)], na[q])
-        BX[q].wait_recv()
-        F[q].start(); O[q].start()
-    st = [s0, s1, s2, s3, s4, s5]
-    for t in range(Q + 5):
-        if t in ev: ev[t]()
-        for i in reversed(range(6)):
-            q = t - i
-            if 0 <= q < Q:
-                st[i](q)
-    for q in range(Q):
-        F[q].wait(); O[q].wait()
-        BX[q].wait_send()
-    for d in (C1, Y, X, Z):
-        for v in d.values(): v.wait_send()
-    e3()
-
-def scatter_grads(g, e, n, chunks, cid):
-    Q = len(chunks)
-    D = pltpu.SemaphoreType.DMA
-    H = sum(h for _, h, _ in chunks); NB = sum(nb for _, _, nb in chunks); NH = H - NB
-    V = lambda *s: pltpu.VMEM(s, BF)
-    anywhere = pl.BlockSpec(memory_space=pl.ANY)
-    near = pl.BlockSpec(memory_space=pltpu.VMEM)
-    return pl.pallas_call(
-        functools.partial(scatter_kernel, chunks),
-        out_shape=(jax.ShapeDtypeStruct(g.shape[1:], g.dtype), jax.ShapeDtypeStruct((4,) + e.shape, e.dtype), jax.ShapeDtypeStruct(n.shape, n.dtype)),
-        in_specs=[anywhere, anywhere, near], out_specs=[anywhere, anywhere, near],
-        scratch_shapes=[pltpu.VMEM((3,) + n.shape, n.dtype), V(8, H, 512), V(8, H, 512), V(8, NB, 512), V(4, NH, 512), V(3, NH, 512), V(H - 2 * NB, 512), V(H, 512),
-            D((Q, 8)), D((Q, 8)), D((Q, 8)), D((Q, 8)), D((Q, 4)), D((Q, 4)), D((Q, 4)), D((Q, 4)), D((Q, 2)), D((Q, 2)), D((Q,)), D((Q,)), D((Q, 8)), D((Q,)),
-            D((11,)), D((11,)), D, D((2,)), D((2,))],
-        compiler_params=pltpu.CompilerParams(collective_id=cid, has_side_effects=True, vmem_limit_bytes=60 * 2**20),
-    )(g, e, n)
-
 def plan(rows, count, share):
     units = rows // 32
     chunks = []
@@ -1039,188 +884,499 @@
     )(unit, deal_order.reshape(128, 1), deal_order.reshape(1, 128), log_scale.reshape(1, 1))
 
 
+GRAD_ROWS = 2 * PART + 64
+GRAD_LAYER = (0, PART + 64)
+GRAD_HEAD = PART
+PIECES = tuple(
+    (stage, half, spare, at)
+    for stage, half, spare, at in (
+        (320, 128, 32, GRAD_LAYER[1] + 256), (576, 128, 48, GRAD_LAYER[1] + 512), (832, 128, 32, GRAD_LAYER[1] + 768),
+        (0, 160, 48, GRAD_HEAD),
+        (320, 128, 32, 256), (576, 128, 48, 512), (832, 128, 32, 768),
+        (64, 128, 32, 0),
+    )
+)
+
+
+def sum_stages(stage, out_ref, acc, b1, b2, b3, b4, b5, fin, sems, free):
+    cs, cr, ys, yr, xs, xr, zs, zr, as_, ar, fs, fr, ls, os_ = sems
+    z, x, y, c = place()
+    me = z * 2 + x
+    zp = [dev((z + k) % 4, x, y, c) for k in range(4)]
+    xp, yp, cp = dev(z, 1 - x, y, c), dev(z, x, 1 - y, c), dev(z, x, y, 1 - c)
+
+    def rc(src, dst, s, r, d):
+        return pltpu.make_async_remote_copy(src, dst, s, r, device_id=d, device_id_type=MESH)
+
+    def owner(k, f):
+        return ((z + k) % 4) * 2 + (x if f == 0 else 1 - x)
+
+    order = [(k, f) for k in (2, 1, 3, 0) for f in (1, 0)]
+    lo, lb, lh, la, l1 = [0], [0], [0], [0], [0]
+    for stage_at, half, spare, at in PIECES:
+        lo.append(lo[-1] + half)
+        lb.append(lb[-1] + spare)
+        lh.append(lh[-1] + half - spare)
+        la.append(la[-1] + half - 2 * spare)
+        l1.append(l1[-1] + half)
+    l1 = l1[:4] + l1[:4]
+
+    def add(dst, src, count):
+        def body(i, carry):
+            at = mult(i * 32)
+            into = dst(at)
+            into[...] = (into[...].astype(jnp.float32) + src(at)[...].astype(jnp.float32)).astype(BF)
+            return carry
+        lax.fori_loop(0, count // 32, body, 0)
+        if count % 32:
+            into = dst(count - 16, 16)
+            into[...] = (into[...].astype(jnp.float32) + src(count - 16, 16)[...].astype(jnp.float32)).astype(BF)
+
+    class Piece:
+        pass
+
+    pieces = []
+    for q, (stage_at, half, spare, at) in enumerate(PIECES):
+        p = Piece()
+        p.q, p.half, p.spare, p.main = q, half, spare, half - spare
+        p.hs = mult(lo[q] + y * spare)
+        p.mb = mult(lo[q] + y * p.main)
+        p.ob = mult(lo[q] + (1 - y) * p.main)
+        p.L, p.C, p.Y, p.X, p.Z = [], [], [], [], []
+        for i, (k, f) in enumerate(order):
+            s = owner(k, f)
+            p.L.append(pltpu.make_async_copy(stage.at[s, pl.ds(mult(stage_at + c * half), half)], acc.at[s, pl.ds(lo[q], half)], ls.at[q, i]))
+            p.C.append(rc(stage.at[s, pl.ds(mult(stage_at + (1 - c) * half), half)], b1.at[s, pl.ds(l1[q], half)], cs.at[q, i], cr.at[q, i], cp))
+            p.Y.append(rc(acc.at[s, pl.ds(p.ob, spare)], b2.at[s, pl.ds(lb[q], spare)], ys.at[q, i], yr.at[q, i], yp))
+        for k in range(4):
+            p.X.append(rc(acc.at[owner(k, 1), pl.ds(p.hs, p.main)], b3.at[k, pl.ds(lh[q], p.main)], xs.at[q, k], xr.at[q, k], xp))
+            p.Z.append(rc(acc.at[owner(k, 0), pl.ds(p.hs, p.main)], b4.at[k - 1, pl.ds(lh[q], p.main)], zs.at[q, k], zr.at[q, k], zp[k]) if k else None)
+        p.aa, p.na = lo[q] + spare, half - 2 * spare
+        p.A = rc(fin.at[pl.ds(p.aa, p.na)], b5.at[pl.ds(la[q], p.na)], as_.at[q, 0], ar.at[q, 0], yp)
+        p.B = rc(fin.at[pl.ds(p.mb, spare)], fin.at[pl.ds(p.mb, spare)], as_.at[q, 1], ar.at[q, 1], yp)
+        p.F = rc(fin.at[pl.ds(lo[q], half)], out_ref.at[pl.ds(mult(at + c * half), half)], fs.at[q], fr.at[q], cp)
+        p.O = pltpu.make_async_copy(fin.at[pl.ds(lo[q], half)], out_ref.at[pl.ds(mult(at + c * half), half)], os_.at[q])
+        pieces.append(p)
+
+    def s0(q):
+        p = pieces[q]
+        if q >= 4:
+            pl.semaphore_wait(free.at[q - 4], 1)
+        for i in range(8):
+            p.C[i].start()
+            p.L[i].start()
+
+    def s1(q):
+        p = pieces[q]
+        for i, (k, f) in enumerate(order):
+            s = owner(k, f)
+            p.L[i].wait()
+            p.C[i].wait_recv()
+            add(lambda a, n=32: acc.at[s, pl.ds(lo[q] + a, n)], lambda a, n=32: b1.at[s, pl.ds(l1[q] + a, n)], p.half)
+            p.Y[i].start()
+        if q < 4:
+            pl.semaphore_signal(free.at[q], inc=1, device_id=cp, device_id_type=MESH)
+
+    def s2(q):
+        p = pieces[q]
+        for i, (k, f) in enumerate(order):
+            s = owner(k, f)
+            p.Y[i].wait_recv()
+            add(lambda a, n=32: acc.at[s, pl.ds(p.mb + a, n)], lambda a, n=32: b2.at[s, pl.ds(lb[q] + a, n)], p.spare)
+            if f == 1:
+                p.X[k].start()
+
+    def s3(q):
+        p = pieces[q]
+        for k in (2, 1, 3, 0):
+            s = owner(k, 0)
+            p.X[k].wait_recv()
+            add(lambda a, n=32: acc.at[s, pl.ds(p.hs + a, n)], lambda a, n=32: b3.at[k, pl.ds(lh[q] + a, n)], p.main)
+            if k:
+                p.Z[k].start()
+
+    def s4(q):
+        p = pieces[q]
+        for k in range(1, 4):
+            p.Z[k].wait_recv()
+        def body(i, carry):
+            at = mult(i * 16)
+            total = acc[me, pl.ds(p.hs + at, 16)].astype(jnp.float32)
+            for k in range(3):
+                total += b4[k, pl.ds(lh[q] + at, 16)].astype(jnp.float32)
+            fin[pl.ds(p.hs + at, 16)] = total.astype(BF)
+            return carry
+        lax.fori_loop(0, p.main // 16, body, 0)
+        p.A.start()
+        p.B.start()
+
+    def s5(q):
+        p = pieces[q]
+        p.A.wait_recv()
+        p.A.wait_send()
+        add(lambda a, n=32: fin.at[pl.ds(p.aa + a, n)], lambda a, n=32: b5.at[pl.ds(la[q] + a, n)], p.na)
+        p.B.wait_recv()
+        p.F.start()
+        p.O.start()
+
+    def sent(q):
+        for copy in pieces[q].C:
+            copy.wait_send()
+
+    def finish():
+        for p in pieces:
+            p.F.wait()
+            p.O.wait()
+            p.B.wait_send()
+            for copy in p.Y + p.X + p.Z[1:]:
+                copy.wait_send()
+
+    return [s0, s1, s2, s3, s4, s5], sent, finish
+
+
+def row_exchange(slots, t_ref, norm_ref, norm_out, nbuf, es, er, el, ns, nr):
+    z, x, y, c = place()
+    me = z * 2 + x
+    g = y * 2 + c
+    g2 = (1 - y) * 2 + c
+    ep = [(lax.rem(me + k, 8), g) for k in range(8)]
+    back = [lax.rem(me + 8 - k, 8) for k in range(8)]
+    yp, cp = dev(z, x, 1 - y, c), dev(z, x, y, 1 - c)
+
+    def rc(src, dst, s, r, d):
+        return pltpu.make_async_remote_copy(src, dst, s, r, device_id=d, device_id_type=MESH)
+
+    kept = pltpu.make_async_copy(slots.at[me], t_ref.at[g, me], el)
+    E = [rc(slots.at[ep[k][0]], t_ref.at[g, me], es.at[0, k], er.at[0, k], ep[k]) for k in range(1, 8)]
+    EY = [rc(t_ref.at[g, back[k]], t_ref.at[g, back[k]], es.at[1, k], er.at[1, k], yp) for k in range(8)]
+    EC = [rc(t_ref.at[g, back[k]], t_ref.at[g, back[k]], es.at[2, k], er.at[2, k], cp) for k in range(8)]
+    ED = [rc(t_ref.at[g2, back[k]], t_ref.at[g2, back[k]], es.at[3, k], er.at[3, k], cp) for k in range(8)]
+    NC = rc(norm_ref, nbuf.at[0], ns.at[0], nr.at[0], cp)
+    NY = rc(nbuf.at[1], nbuf.at[2], ns.at[1], nr.at[1], yp)
+
+    def e0():
+        kept.start()
+        for copy in E:
+            copy.start()
+        NC.start()
+
+    def e1():
+        kept.wait()
+        EY[0].start()
+        EC[0].start()
+        NC.wait_recv()
+        nbuf[1] = nbuf[0] + norm_ref[...]
+        NY.start()
+        for k in range(1, 8):
+            E[k - 1].wait_recv()
+            EY[k].start()
+            EC[k].start()
+
+    def e2():
+        for k in range(8):
+            EY[k].wait_recv()
+            ED[k].start()
+        NY.wait_recv()
+        norm_out[...] = nbuf[1] + nbuf[2]
+
+    def e3():
+        for copy in EC + ED:
+            copy.wait_recv()
+        for copy in E + EY + EC + ED + [NC, NY]:
+            copy.wait_send()
+
+    return [e0, e1, e2, e3]
+
+
 def backward_kernel(
-    own_ref, zed_ref, pool_ref, seg_col_ref, seg_row_ref, valid_ref, w_ref, head_ref, norm_ref,
-    low_ref, qkv_ref, lse_ref, mix_ref, one_ref, two_ref, last_ref,
-    grad_ref, norm_out_ref, first_ref,
-    dx, far, acc, two_s, low_s, mid_s, ups, gates, back,
+    own_ref, zed_ref, pool_ref, seg_col_ref, seg_row_ref, valid_ref, key_ref, norm_ref,
+    w_ref, low_in, qkv_in, lse_in, mix_in, one_in, two_in,
+    out_ref, t_ref, norm_out, first_ref,
+    weights, head, low_ref, qkv_ref, lse_ref, mix_ref, one_ref, two_ref, stage,
+    dx, far, acc, two_s, low_s, mid_s, ups, gates, back, norm_s, slots,
+    total, b1, b2, b3, b4, b5, fin, nbuf,
+    cs, cr, ys, yr, xs, xr, zs, zr, as_, ar, fs, fr, ls, os_, es, er, el, ns, nr, loads, free,
 ):
-    step = pl.program_id(0)
     tokens = dx.shape[0]
     tiles = tokens // TILE
     low_type = jnp.bfloat16
-
-    @pl.when(step == 0)
-    def _():
+    z, x, y, c = place()
+    me = z * 2 + x
+    g = y * 2 + c
+    peers = [(lax.rem(me + k, 8), g) for k in range(1, 8)] + [dev(z, x, 1 - y, c), dev(z, x, y, 1 - c)]
+    barrier = pltpu.get_barrier_semaphore()
+    for peer in peers:
+        pl.semaphore_signal(barrier, inc=1, device_id=peer, device_id_type=MESH)
+    stages, sent, finish = sum_stages(
+        stage, out_ref, total, b1, b2, b3, b4, b5, fin, (cs, cr, ys, yr, xs, xr, zs, zr, as_, ar, fs, fr, ls, os_), free
+    )
+    rows_out = row_exchange(slots, t_ref, norm_s, norm_out, nbuf, es, er, el, ns, nr)
+
+    def loading(layer):
+        base = layer * PART
+        copy = pltpu.make_async_copy
+        return {
+            "two": copy(two_in.at[layer], two_ref, loads.at[layer, 0]),
+            "one": copy(one_in.at[layer], one_ref, loads.at[layer, 1]),
+            "feed": copy(w_ref.at[:, pl.ds(base + 256, 768)], weights.at[:, pl.ds(256, 768)], loads.at[layer, 2]),
+            "mix": copy(mix_in.at[layer], mix_ref, loads.at[layer, 3]),
+            "qkv": copy(qkv_in.at[layer], qkv_ref, loads.at[layer, 4]),
+            "lse": copy(lse_in.at[layer], lse_ref, loads.at[layer, 5]),
+            "low": copy(low_in.at[layer], low_ref, loads.at[layer, 6]),
+            "attend": copy(w_ref.at[:, pl.ds(base, 256)], weights.at[:, pl.ds(0, 256)], loads.at[layer, 7]),
+        }
+
+    load = [loading(layer) for layer in range(LAYERS)]
+    head_load = pltpu.make_async_copy(w_ref.at[:, pl.ds(HEAD_AT, 64)], head, loads.at[0, 8])
+    head_load.start()
+    for copy in load[1].values():
+        copy.start()
+
+    def begin():
         fill_distance(far, seg_col_ref, seg_row_ref)
+        head_load.wait()
+        load[1]["two"].wait()
         zed = zed_ref[...]
         square = jnp.sum(zed * zed, axis=-1, keepdims=True) + UNIT_EPS
         inverse = lax.rsqrt(square)
         own = own_ref[...]
         inner = jnp.sum(own * zed, axis=-1, keepdims=True)
         grad_zed = (inverse * (own - zed * (inner / square))).astype(low_type)
-        head = head_ref[...].reshape(D, D)
-        grad_head = dot_tn(pool_ref[...], grad_zed)
-        grad_ref[:, 0:64, :] = grad_head.reshape(8, 64, D).astype(low_type)
-        grad_ref[:, 64:96, :] = jnp.zeros((8, 32, D), low_type)
+        head_low = head[...].reshape(D, D)
+        stage[:, 0:64, :] = dot_tn(pool_ref[...], grad_zed).reshape(8, 64, D).astype(low_type)
         member = members(seg_row_ref, valid_ref)
         counts = jnp.maximum(jnp.sum(member, axis=1, keepdims=True), 1.0)
-        grad_pooled = dot_nt(grad_zed, head) / counts
+        grad_pooled = dot_nt(grad_zed, head_low) / counts
         grad_final = exact_dot(member, grad_pooled, ((0,), (0,)))
-        gain_last = norm_ref[6:7, :]
-        stream_scaled, _ = norm_parts(last_ref[0])
-        stream = stream_scaled * gain_last + norm_ref[7:8, :]
+        stream_scaled, _ = norm_parts(two_ref[...])
+        stream = stream_scaled * norm_ref[6:7, :] + norm_ref[7:8, :]
         scaled, inverse = norm_parts(stream)
-        norm_out_ref[0, 0:1, :] = jnp.sum(grad_final * scaled, axis=0, keepdims=True)
-        norm_out_ref[0, 1:2, :] = jnp.sum(grad_final, axis=0, keepdims=True)
+        norm_s[...] = jnp.zeros(norm_s.shape, jnp.float32)
+        norm_s[2, 0:1, :] = jnp.sum(grad_final * scaled, axis=0, keepdims=True)
+        norm_s[2, 1:2, :] = jnp.sum(grad_final, axis=0, keepdims=True)
         dx[...] = norm_back(scaled, inverse, grad_final, norm_ref[8:9, :])
 
-    @pl.when(step > 0)
-    def _():
-        at = 4 * (LAYERS - step)
-        norm_out_ref[0] = jnp.zeros((8, D), jnp.float32)
-
-        def enter(i, carry):
+    def enter(layer):
+        at = 4 * layer
+        if layer < LAYERS - 1:
+            load[layer]["two"].wait()
+        load[layer]["one"].wait()
+
+        def body(i, carry):
             rows = pl.ds(pl.multiple_of(i * TILE, TILE), TILE)
-            scaled, inverse = norm_parts(two_ref[0, rows, :])
+            scaled, inverse = norm_parts(two_ref[rows, :])
             grad = dx[rows, :]
-            norm_out_ref[0, 2:3, :] += jnp.sum(grad * scaled, axis=0, keepdims=True)
-            norm_out_ref[0, 3:4, :] += jnp.sum(grad, axis=0, keepdims=True)
-            grad = norm_back(scaled, inverse, grad, norm_ref[pl.ds(at + 2, 1), :])
+            norm_s[layer, 2:3, :] += jnp.sum(grad * scaled, axis=0, keepdims=True)
+            norm_s[layer, 3:4, :] += jnp.sum(grad, axis=0, keepdims=True)
+            grad = norm_back(scaled, inverse, grad, norm_ref[at + 2 : at + 3, :])
             acc[rows, :] = grad
             two_s[rows, :] = grad.astype(low_type)
-            scaled, _ = norm_parts(one_ref[0, rows, :])
-            hidden = scaled * norm_ref[pl.ds(at, 1), :] + norm_ref[pl.ds(at + 1, 1), :]
+            scaled, _ = norm_parts(one_ref[rows, :])
+            hidden = scaled * norm_ref[at : at + 1, :] + norm_ref[at + 1 : at + 2, :]
             low_s[rows, :] = hidden.astype(low_type)
             return carry
 
-        lax.fori_loop(0, tiles, enter, 0)
-        for j in range(4):
-            def feed(i, carry):
-                rows = pl.ds(pl.multiple_of(i * TILE, TILE), TILE)
-                low = low_s[rows, :]
-                gate = dot_nn(low, block(w_ref, 256 + j * 64))
-                up = dot_nn(low, block(w_ref, 512 + j * 64))
-                grad_mid = dot_nt(two_s[rows, :], down_block(w_ref, j))
-                value, slope = gelu_parts(gate)
-                mid_s[rows, :] = (value * up).astype(low_type)
-                grad_gate = (grad_mid * up * slope).astype(low_type)
-                grad_up = (grad_mid * value).astype(low_type)
-                gates[rows, :] = grad_gate
-                ups[rows, :] = grad_up
-                acc[rows, :] += dot_nt(grad_gate, block(w_ref, 256 + j * 64)) + dot_nt(
-                    grad_up, block(w_ref, 512 + j * 64)
-                )
-                return carry
-
-            lax.fori_loop(0, tiles, feed, 0)
-            grad_ref[2 * j : 2 * j + 2, 768:1024, :] = (
-                dot_tn(mid_s[...], two_s[...]).reshape(2, 256, D).astype(low_type)
+        lax.fori_loop(0, tiles, body, 0)
+        if layer > 0:
+            load[layer - 1]["two"].start()
+        load[layer]["feed"].wait()
+
+    def feed(layer, j):
+        def body(i, carry):
+            rows = pl.ds(pl.multiple_of(i * TILE, TILE), TILE)
+            low = low_s[rows, :]
+            gate = dot_nn(low, block(weights, 256 + j * 64))
+            up = dot_nn(low, block(weights, 512 + j * 64))
+            grad_mid = dot_nt(two_s[rows, :], down_block(weights, j))
+            value, slope = gelu_parts(gate)
+            mid_s[rows, :] = (value * up).astype(low_type)
+            grad_gate = (grad_mid * up * slope).astype(low_type)
+            grad_up = (grad_mid * value).astype(low_type)
+            gates[rows, :] = grad_gate
+            ups[rows, :] = grad_up
+            acc[rows, :] += dot_nt(grad_gate, block(weights, 256 + j * 64)) + dot_nt(
+                grad_up, block(weights, 512 + j * 64)
             )
-            grad_ref[:, 256 + j * 64 : 320 + j * 64, :] = (
-                dot_tn(low_s[...], gates[...]).reshape(8, 64, D).astype(low_type)
-            )
-            grad_ref[:, 512 + j * 64 : 576 + j * 64, :] = (
-                dot_tn(low_s[...], ups[...]).reshape(8, 64, D).astype(low_type)
-            )
-
-        def middle(i, carry):
+            return carry
+
+        lax.fori_loop(0, tiles, body, 0)
+        if layer < LAYERS - 1 and j == 0:
+            for q in range(3):
+                sent(q)
+        stage[2 * j : 2 * j + 2, 832:1088, :] = dot_tn(mid_s[...], two_s[...]).reshape(2, 256, D).astype(low_type)
+        stage[:, 320 + j * 64 : 384 + j * 64, :] = dot_tn(low_s[...], gates[...]).reshape(8, 64, D).astype(low_type)
+        stage[:, 576 + j * 64 : 640 + j * 64, :] = dot_tn(low_s[...], ups[...]).reshape(8, 64, D).astype(low_type)
+
+    def middle(layer):
+        at = 4 * layer
+        if layer > 0:
+            load[layer - 1]["feed"].start()
+        load[layer]["attend"].wait()
+        load[layer]["mix"].wait()
+
+        def body(i, carry):
             rows = pl.ds(pl.multiple_of(i * TILE, TILE), TILE)
-            scaled, inverse = norm_parts(one_ref[0, rows, :])
+            scaled, inverse = norm_parts(one_ref[rows, :])
             grad = acc[rows, :]
-            norm_out_ref[0, 0:1, :] += jnp.sum(grad * scaled, axis=0, keepdims=True)
-            norm_out_ref[0, 1:2, :] += jnp.sum(grad, axis=0, keepdims=True)
-            grad = norm_back(scaled, inverse, grad, norm_ref[pl.ds(at, 1), :])
+            norm_s[layer, 0:1, :] += jnp.sum(grad * scaled, axis=0, keepdims=True)
+            norm_s[layer, 1:2, :] += jnp.sum(grad, axis=0, keepdims=True)
+            grad = norm_back(scaled, inverse, grad, norm_ref[at : at + 1, :])
             dx[rows, :] = grad
             low = grad.astype(low_type)
             two_s[rows, :] = low
-            mid_s[rows, :] = dot_nt(low, block(w_ref, 192)).astype(low_type)
+            mid_s[rows, :] = dot_nt(low, block(weights, 192)).astype(low_type)
             return carry
 
-        lax.fori_loop(0, tiles, middle, 0)
-        grad_ref[:, 192:256, :] = dot_nn(mix_ref[0], two_s[...]).reshape(8, 64, D).astype(low_type)
-        for head in range(HEADS):
-            lanes = slice(head * HEAD_DIM, (head + 1) * HEAD_DIM)
-            key_lanes = slice(D + head * HEAD_DIM, D + (head + 1) * HEAD_DIM)
-            val_lanes = slice(2 * D + head * HEAD_DIM, 2 * D + (head + 1) * HEAD_DIM)
-            keys = qkv_ref[0, :, key_lanes]
-            keys_t = keys.T
-            vals = qkv_ref[0, :, val_lanes]
-            slope = 2.0 ** (-8.0 * (head + 1) / HEADS)
-            grad_vals = None
-            grad_keys = None
-            for i in range(tiles):
-                cols = slice(i * TILE, (i + 1) * TILE)
-                query = qkv_ref[0, cols, lanes]
-                grad_mix = mid_s[cols, lanes]
-                scores = dot_nt(keys, query) * HEAD_DIM**-0.5 - slope * far[:, cols]
-                prob = jnp.exp(scores - lse_ref[0, head, :, cols])
-                grad_prob = dot_nt(vals, grad_mix)
-                inner = jnp.sum(prob * grad_prob, axis=0, keepdims=True)
-                grad_raw = (prob * (grad_prob - inner) * HEAD_DIM**-0.5).astype(low_type)
-                back[cols, lanes] = dot_nn(keys_t, grad_raw).T.astype(low_type)
-                value_part = dot_nn(prob.astype(low_type), grad_mix)
-                key_part = dot_nn(grad_raw, query)
-                grad_vals = value_part if grad_vals is None else grad_vals + value_part
-                grad_keys = key_part if grad_keys is None else grad_keys + key_part
-            back[:, key_lanes] = grad_keys.astype(low_type)
-            back[:, val_lanes] = grad_vals.astype(low_type)
-
-        def leave(i, carry):
+        lax.fori_loop(0, tiles, body, 0)
+        if layer > 0:
+            load[layer - 1]["one"].start()
+        else:
+            sent(3)
+        stage[:, 256:320, :] = dot_nn(mix_ref[...], two_s[...]).reshape(8, 64, D).astype(low_type)
+        load[layer]["qkv"].wait()
+        load[layer]["lse"].wait()
+        load[layer]["low"].wait()
+
+    def attend_head(layer, head):
+        lanes = slice(head * HEAD_DIM, (head + 1) * HEAD_DIM)
+        key_lanes = slice(D + head * HEAD_DIM, D + (head + 1) * HEAD_DIM)
+        val_lanes = slice(2 * D + head * HEAD_DIM, 2 * D + (head + 1) * HEAD_DIM)
+        keys = qkv_ref[:, key_lanes]
+        keys_t = keys.T
+        vals = qkv_ref[:, val_lanes]
+        slope = 2.0 ** (-8.0 * (head + 1) / HEADS)
+        grad_vals = None
+        grad_keys = None
+        for i in range(tiles):
+            cols = slice(i * TILE, (i + 1) * TILE)
+            query = qkv_ref[cols, lanes]
+            grad_mix = mid_s[cols, lanes]
+            scores = dot_nt(keys, query) * HEAD_DIM**-0.5 - slope * far[:, cols]
+            prob = jnp.exp(scores - lse_ref[head, :, cols])
+            grad_prob = dot_nt(vals, grad_mix)
+            inner = jnp.sum(prob * grad_prob, axis=0, keepdims=True)
+            grad_raw = (prob * (grad_prob - inner) * HEAD_DIM**-0.5).astype(low_type)
+            back[cols, lanes] = dot_nn(keys_t, grad_raw).T.astype(low_type)
+            value_part = dot_nn(prob.astype(low_type), grad_mix)
+            key_part = dot_nn(grad_raw, query)
+            grad_vals = value_part if grad_vals is None else grad_vals + value_part
+            grad_keys = key_part if grad_keys is None else grad_keys + key_part
+        back[:, key_lanes] = grad_keys.astype(low_type)
+        back[:, val_lanes] = grad_vals.astype(low_type)
+
+    def leave(layer):
+        def body(i, carry):
             rows = pl.ds(pl.multiple_of(i * TILE, TILE), TILE)
-            total = dx[rows, :]
+            grad = dx[rows, :]
             for j in range(3):
-                total = total + dot_nt(back[rows, j * D : (j + 1) * D], block(w_ref, j * 64))
-            dx[rows, :] = total
+                grad = grad + dot_nt(back[rows, j * D : (j + 1) * D], block(weights, j * 64))
+            dx[rows, :] = grad
             return carry
 
-        lax.fori_loop(0, tiles, leave, 0)
+        lax.fori_loop(0, tiles, body, 0)
         for j in range(3):
-            grad_ref[:, j * 64 : (j + 1) * 64, :] = (
-                dot_tn(low_ref[0], back[:, j * D : (j + 1) * D]).reshape(8, 64, D).astype(low_type)
+            stage[:, 64 + j * 64 : 128 + j * 64, :] = (
+                dot_tn(low_ref[...], back[:, j * D : (j + 1) * D]).reshape(8, 64, D).astype(low_type)
             )
-
-        @pl.when(step == LAYERS)
-        def _():
+        if layer > 0:
+            for name in ("mix", "qkv", "lse", "low", "attend"):
+                load[layer - 1][name].start()
+        else:
             first_ref[...] = dx[...].astype(low_type)
-
-
-def run_backward(own, zed, pool, seg_col, seg_row, valid, weights, norms, saved):
+            count = slots.shape[1]
+            for d in range(8):
+                hot = lax.broadcasted_iota(jnp.int32, (count, tokens), 0) + d * count == key_ref[...]
+                slots[d] = dot_nn(jnp.where(hot, 1.0, 0.0).astype(low_type), first_ref[...]).astype(low_type)
+
+    events = []
+    clock = 0.0
+
+    def do(cost, fn, *args):
+        nonlocal clock
+        events.append((clock, len(events), fn, args))
+        clock += cost
+
+    def wait_entry():
+        pl.semaphore_wait(barrier, len(peers))
+
+    ready = []
+    do(3.0, begin)
+    for layer in (1, 0):
+        do(2.5, enter, layer)
+        for j in range(4):
+            do(4.7, feed, layer, j)
+        if layer == 1:
+            do(0.0, wait_entry)
+        ready += [clock] * 3
+        do(0.0, stages[0], len(ready) - 3)
+        do(0.0, stages[0], len(ready) - 2)
+        do(0.0, stages[0], len(ready) - 1)
+        do(2.5, middle, layer)
+        for head_index in range(HEADS):
+            do(1.6, attend_head, layer, head_index)
+        do(4.0, leave, layer)
+        ready.append(clock)
+        if layer == 0:
+            do(0.0, rows_out[0])
+        do(0.0, stages[0], len(ready) - 1)
+    end = clock
+    links = {"c": 0.0, "y": 0.0, "x": 0.0, "z": 0.0}
+    for q in range(8):
+        scale = PIECES[q][1] / 128.0
+        now = ready[q]
+        for number, link, cost in ((1, "c", 3.0), (2, "y", 8.0), (3, "x", 9.5), (4, "z", 9.5), (5, "y", 1.0)):
+            now = max(now, links[link]) + cost * scale
+            if number < 5:
+                links[link] = now
+            else:
+                now += 3.0
+            events.append((now, len(events), stages[number], (q,)))
+    events.append((end + 8.0, len(events), rows_out[1], ()))
+    events.append((end + 26.0, len(events), rows_out[2], ()))
+    for _, _, fn, args in sorted(events, key=lambda event: event[:2]):
+        fn(*args)
+    finish()
+    for q in range(4, 8):
+        sent(q)
+    rows_out[3]()
+
+
+def run_backward(own, zed, pool, seg_col, seg_row, valid, key, weights, norms, saved, cid):
     low_x, qkv, lse, mix, one, two = saved
     tokens = low_x.shape[1]
     low = jnp.bfloat16
-    pick = lambda i: jnp.minimum(LAYERS - i, LAYERS - 1)
-    layered = lambda *s: pl.BlockSpec((1,) + s, lambda i: (pick(i),) + (0,) * len(s))
+    full = jnp.float32
+    vmem = lambda shape, kind=low: pltpu.VMEM(shape, kind)
+    sems = lambda *shape: pltpu.SemaphoreType.DMA(shape)
+    half = sum(p[1] for p in PIECES)
+    spare = sum(p[2] for p in PIECES)
+    near = pl.BlockSpec(memory_space=pltpu.VMEM)
+    anywhere = pl.BlockSpec(memory_space=pl.ANY)
+    norm_shape = (LAYERS + 1, 8, D)
+    square = (tokens, D)
     return pl.pallas_call(
         backward_kernel,
-        grid=(LAYERS + 1,),
-        in_specs=[
-            whole((8, D)), whole((8, D)), whole((8, D)), whole((tokens, 1)), whole((1, tokens)), whole((1, tokens)),
-            pl.BlockSpec((8, PART, D), lambda i: (0, pick(i), 0)),
-            pl.BlockSpec((8, 64, D), lambda i: (0, HEAD_AT // 64, 0)),
-            whole(norms.shape),
-            layered(tokens, D), layered(tokens, 3 * D), layered(HEADS, 1, tokens), layered(D, tokens),
-            layered(tokens, D), layered(tokens, D),
-            pl.BlockSpec((1, tokens, D), lambda i: (LAYERS - 1, 0, 0)),
-        ],
-        out_specs=[
-            pl.BlockSpec((8, PART, D), lambda i: (0, LAYERS - i, 0)),
-            pl.BlockSpec((1, 8, D), lambda i: (LAYERS - i, 0, 0)),
-            whole((tokens, D)),
-        ],
+        in_specs=[near] * 8 + [anywhere] * 7,
+        out_specs=[anywhere, anywhere, near, near],
         out_shape=[
-            jax.ShapeDtypeStruct((8, PACKED, D), low),
-            jax.ShapeDtypeStruct((LAYERS + 1, 8, D), jnp.float32),
-            jax.ShapeDtypeStruct((tokens, D), low),
+            jax.ShapeDtypeStruct((GRAD_ROWS, D), low),
+            jax.ShapeDtypeStruct((4, 8, SLOTS, D), low),
+            jax.ShapeDtypeStruct(norm_shape, full),
+            jax.ShapeDtypeStruct(square, low),
         ],
         scratch_shapes=[
-            pltpu.VMEM((tokens, D), jnp.float32), pltpu.VMEM((tokens, tokens), jnp.float32),
-            pltpu.VMEM((tokens, D), jnp.float32), pltpu.VMEM((tokens, D), low), pltpu.VMEM((tokens, D), low),
-            pltpu.VMEM((tokens, D), low), pltpu.VMEM((tokens, D), low), pltpu.VMEM((tokens, D), low),
-            pltpu.VMEM((tokens, 3 * D), low),
+            vmem((8, PART, D)), vmem((8, 64, D)), vmem(square), vmem((tokens, 3 * D)), vmem((HEADS, 1, tokens), full),
+            vmem((D, tokens)), vmem(square, full), vmem(square, full), vmem((8, PART + 64, D)),
+            vmem(square, full), vmem((tokens, tokens), full), vmem(square, full), vmem(square), vmem(square),
+            vmem(square), vmem(square), vmem(square), vmem((tokens, 3 * D)), vmem(norm_shape, full), vmem((8, SLOTS, D)),
+            vmem((8, half, D)), vmem((8, sum(p[1] for p in PIECES[:4]), D)), vmem((8, spare, D)), vmem((4, half - spare, D)),
+            vmem((3, half - spare, D)), vmem((half - 2 * spare, D)), vmem((half, D)), vmem((3,) + norm_shape, full),
+            sems(8, 8), sems(8, 8), sems(8, 8), sems(8, 8), sems(8, 4), sems(8, 4), sems(8, 4), sems(8, 4),
+            sems(8, 2), sems(8, 2), sems(8), sems(8), sems(8, 8), sems(8), sems(4, 8), sems(4, 8), pltpu.SemaphoreType.DMA,
+            sems(2), sems(2), sems(2, 9), pltpu.SemaphoreType.REGULAR((4,)),
         ],
-        compiler_params=pltpu.CompilerParams(vmem_limit_bytes=62 * 2**20),
-    )(own, zed, pool, seg_col, seg_row, valid, weights, weights, norms, low_x, qkv, lse, mix, one, two, two)
+        compiler_params=pltpu.CompilerParams(collective_id=cid, has_side_effects=True, vmem_limit_bytes=63 * 2**20),
+    )(own, zed, pool, seg_col, seg_row, valid, key, norms, weights, low_x, qkv, lse, mix, one, two)
 
 
 def total_kernel(v_ref, o_ref, got, mine, ss, rs, ts, us, ls):
@@ -1286,7 +1442,7 @@
 
 
 def matrices(layer):
-    at = layer * PART
+    at = GRAD_LAYER[layer]
     first = 2 + 13 * layer
     return (
         (2, at, 64, 3, first), (3, at + 192, 64, 1, first + 3),
@@ -1336,7 +1492,7 @@
                 put(STEP_AT + block_at + j, jnp.sum(squares[j] * inverse, axis=0, keepdims=True))
             return new, jnp.sum(new, axis=0, keepdims=True)
 
-        new, count = part(HEAD_AT, 64, 1, 1, rows_ref[:, 6:7])
+        new, count = part(GRAD_HEAD, 64, 1, 1, rows_ref[:, 6:7])
         rows_out[:, 6:7] = new
         sums += lane_pick(count, 1)
         for layer in range(LAYERS):
@@ -1428,7 +1584,7 @@
         head_cols_out[...] = news[0]
         all_rms += lane_pick(rms, 1)
         row = lax.rsqrt(rows_ref[:, 6:7] / row_mean) * scale
-        head_out[...] = head_ref[...] + grads_ref[HEAD_AT : HEAD_AT + 64, :].astype(jnp.float32) * row * lax.rsqrt(news[0])
+        head_out[...] = head_ref[...] + grads_ref[GRAD_HEAD : GRAD_HEAD + 64, :].astype(jnp.float32) * row * lax.rsqrt(news[0])
         for layer in range(LAYERS):
             for name, first, rows, blocks, block_at in matrices(layer):
                 col_at = (block_at - 2 - 13 * layer) * D
@@ -1526,16 +1682,8 @@
     )
     loss_value, own_rows, grad_scale = run_contrast(unit_parts, deal_order, log_scale, 1)
     loss_value, grad_scale = loss_value[0, 0], grad_scale[0]
-    all_grads, norm_parts_out, grad_first = run_backward(
-        own_rows, head_out, pooled_low, seg_col, seg_row, valid_row, weights, norms, saved
-    )
-    slot_grads = jnp.dot(
-        (jnp.arange(8 * SLOTS, dtype=jnp.int32)[:, None] == key[None, :]).astype(jnp.bfloat16),
-        grad_first,
-        preferred_element_type=jnp.float32,
-    ).astype(jnp.bfloat16)
-    shard_grads, table_rows, norm_sum = scatter_grads(
-        all_grads, slot_grads.reshape(8, SLOTS, D), norm_parts_out, plan(PACKED, 4, 0.29), 2
+    shard_grads, table_rows, norm_sum, grad_first = run_backward(
+        own_rows, head_out, pooled_low, seg_col, seg_row, valid_row, key.reshape(1, -1), weights, norms, saved, 2
     )
     table_slots = asked[:, :, 0, :SLOTS].reshape(1, -1)
     table_row = embed_rows.reshape(1, -1)

time: 468 us -> 424 us (0.906)
  Pallas kernels: 409 us -> 365 us
    pallas_call x2 -> x1, Pallas kernels: 195 us -> 154 us  [run_backward(): pl.pallas_call(backward_kernel, in_specs=[near] * 8 + [anywhere] * 7, out...]
where the time goes in v4:
time: 424 us; the launch traced here: 417 us
  Pallas kernels  365 us (86%)
  between operations  22.9 us (5%)
  local copies, waits for them, and re-layouts  16.1 us (4%)
  other arithmetic  12.1 us (3%)
    pallas_call x1, Pallas kernels, run_backward(): pl.pallas_call(backward_kernel, in_specs=[near] * 8 + [anywhere] * 7, out...  154 us
    pallas_call x1, Pallas kernels, gather_weights(): pl.pallas_call(functools.partial(gather_kernel, chunks), out_shape=(jax.S...  102 us
    pallas_call x1, Pallas kernels, run_forward(): pl.pallas_call(forward_kernel, grid=(LAYERS,), in_specs=[whole((tokens, D...  36.9 us
    pallas_call x1, Pallas kernels, run_stats(): pl.pallas_call(functools.partial(stats_kernel, dense, row_count), grid=(-...  21.3 us
    pallas_call x1, Pallas kernels, run_contrast(): pl.pallas_call(contrast_kernel, out_shape=[one, jax.ShapeDtypeStruct((8,...  19.3 us
    pallas_call x1, Pallas kernels, total(): pl.pallas_call(total_kernel, out_shape=jax.ShapeDtypeStruct(v.shape, v.dt...  17.5 us
    pallas_call x1, Pallas kernels, run_update(): pl.pallas_call(functools.partial(update_kernel, totals), grid=(-(-row_cou...  14.1 us

profile of v4, /device:TPU:0, one launch (start us, length us, event | category | flops | bytes accessed | tf_op | source)
XLA Modules:
  0.0 416.6 jit_solution(9975616199578948659)
XLA Ops:
  7.2 0.7 multiply_subtract_fusion
  7.9 1.0 select_reduce_fusion.1
  8.9 0.5 convert_reduce_fusion
  9.4 0.6 fusion.5
  10.1 0.2 select_reduce_fusion
  10.4 0.7 concatenate.15.ask_ref
  11.1 1.7 convert.24
  12.8 0.4 copy.103
  13.3 0.3 copy.90
  13.6 0.3 copy-done.3
  14.0 0.3 reshape.162
  14.3 0.1 copy.89
  14.4 0.1 copy-done.1
  14.6 1.5 pad_maximum_fusion
  16.1 1.7 fusion.1.w_ref
  17.9 101.6 %shard_map.339 = (bf16[8,2144,512]{2,1,0:T(8,128)(2,1)}, bf16[8,80,512]{2,1,0:T(8,128)(2,1)S(1)}, s32[4,8,1,128]{3,2,1,0:T(1,128)S(1)}) custom-call(bf16[2144,512]{1,0:T(8,128)(2,1)S(1)} %fusion.1.w_ref, s32[8,1,128]{2,1,0:T(1,128)S(1)} %concatenate.15.ask_ref, f32[3816,512]{1,0:T(8,128)} %embed_ref.1), custom_call_target="tpu_custom_call" | custom-call | tf_op jit(solution)/shard_map/pallas_call | solution.py:573
  119.5 0.7 slice_reduce_fusion.1
  120.9 2.4 conditional.2
  120.9 2.0 gather_fusion
  122.9 0.1 broadcast_select_fusion
  123.3 0.8 slice_bitcast_fusion
  124.1 0.1 convert_element_type.51
  124.2 0.6 pad_convert_fusion.norm_ref
  124.8 0.2 reduce-window.8
  125.0 0.1 convert_reduce_fusion.1
  125.1 0.9 copy.92.seg_col_ref
  125.9 36.9 %shard_map.340 = (bf16[2,512,512]{2,1,0:T(8,128)(2,1)}, bf16[2,512,1536]{2,1,0:T(8,128)(2,1)}, f32[2,8,1,512]{3,2,1,0:T(1,128)}, bf16[2,512,512]{2,1,0:T(8,128)(...) custom-call(bf16[512,512]{1,0:T(8,128)(2,1)S(1)} %get-tuple-element., ...), custom_call_target="tpu_custom_call" | custom-call | tf_op jit(solution)/shard_map/pallas_call | solution.py:790
  163.5 0.7 copy.93.deal_col_ref
  164.2 19.3 %shard_map.341 = (f32[1,1]{1,0:T(1,128)}, f32[8,512]{1,0:T(8,128)}, f32[1,1]{1,0:T(1,128)}) custom-call(f32[16,128]{1,0:T(8,128)} %get-tuple-element.137.unit_ref, s32[128,1]{1,0:T(8,128)} %copy.93.deal_col_ref, s32[1,128]{1,0:T(1,128)} %bitcast.67, f32[1,1]{1,0:T(1,128)} %bitcast.46.scale_ref), custom_call_target="tpu_custom_call" | custom-call | tf_op jit(solution)/shard_map/pallas_call | solution.py:877
  186.4 154.4 %shard_map.342 = (bf16[2112,512]{1,0:T(8,128)(2,1)}, bf16[4,8,80,512]{3,2,1,0:T(8,128)(2,1)}, f32[3,8,512]{2,1,0:T(8,128)S(1)}, bf16[512,512]{1,0:T(8,128)(2,1)}) custom-call(f32[8,512]{1,0:T(8,128)} %get-tuple-element.139.own_ref, f32[8,512]{1,0:T(8,128)} %get-tuple-element.140.zed_ref, bf16[8,512]{1,0:T(8,128)(2,1)} %get-tuple-element.141.pool_ref, ...), custom_call_target="tpu_custom_call" | custom-call | tf_op jit(solution)/shard_map/pallas_call | solution.py:1357
  340.8 0.1 copy.96
  341.1 22.5 %conditional.3 = (bf16[3816,512]{1,0:T(8,128)(2,1)}, f32[1,3816]{1,0:T(1,128)}, f32[32,3,512]{2,1,0:T(4,128)}, f32[64,8]{1,0:T(8,128)}, f32[256,2]{1,0:T(8,128)}, /*index=5*/f32[3816]{0:T(1024)S(1)}) conditional(s32[]{:T(128)} %convert_element_type.48, (s32[4,8,1,128]{3,2,1,0:T(1,128)S(1)}, bf16[4,8,80,512]{3,2,1,0:T(8,128)(2,1)}, ...), branch_computations={%region_9.10_spmd, %region_10.14_spmd} | conditional | flops 2479616 | bytes 325181440 | solution.py:1705
  341.2 0.1 reshape_squeeze.3.refs_0_
  341.2 21.3 %branch_0_fun.1 = (bf16[3816,512]{1,0:T(8,128)(2,1)}, f32[1,3816]{1,0:T(1,128)}, f32[32,3,512]{2,1,0:T(4,128)}, f32[64,8]{1,0:T(8,128)}, f32[256,2]{1,0:T(8,128)}) custom-call(s32[1,2560]{1,0:T(1,128)S(1)} %reshape_squeeze.3.refs_0_, bf16[2560,512]{1,0:T(8,128)(2,1)} %bitcast.52, bf16[2112,512]{1,0:T(8,128)(2,1)} %get-tuple-element.58.refs_2_, ...), custom_call_target="tpu_custom_call" | custom-call | tf_op jit(solution)/shard_map/cond/branch_0_fun/pallas_call | solution.py:1536
  362.5 0.8 reduce.1
  363.5 17.5 %shard_map.343.stat_ref = f32[32,3,512]{2,1,0:T(4,128)} custom-call(f32[32,3,512]{2,1,0:T(4,128)} %get-tuple-element.152.v_ref), custom_call_target="tpu_custom_call" | custom-call | tf_op jit(solution)/shard_map/pallas_call | solution.py:1421
  381.1 1.1 copy-done.4
  382.2 0.9 copy-done.5
  383.2 0.9 copy-done.8
  384.1 0.8 copy-done.10
  384.9 14.1 %shard_map.344 = (f32[3816,512]{1,0:T(8,128)}, f32[1,512]{1,0:T(1,128)}, f32[1,512]{1,0:T(1,128)}, f32[2,6656]{1,0:T(2,128)}, f32[2,64,1536]{2,1,0:T(8,128)}, /*...) custom-call(f32[32,3,512]{2,1,0:T(4,128)S(1)} %copy-done.5, ...), custom_call_target="tpu_custom_call" | custom-call | tf_op jit(solution)/shard_map/pallas_call | solution.py:1616
  399.0 0.5 slice_bitcast_fusion.1
  399.5 0.1 reshape.179
  399.7 1.4 multiply_add_fusion
  401.0 0.8 copy.100
  401.9 0.6 copy.102
  402.5 1.6 copy.101
  404.0 1.5 slice_reduce_fusion
  (63 shorter events, 0.6 us)
Async XLA Ops:
  12.8 1.1 copy-start.3
  13.2 1.3 copy-start.1
  13.2 1.3 copy-start.7
  14.0 2.1 copy-start.9
  14.0 2.1 copy-start.16
  17.9 103.0 %copy-start.12 = (s32[512]{0:T(512)S(1)}, s32[512]{0:T(512)}, u32[]{:S(2)}) copy-start(s32[512]{0:T(512)} %param.24) | copy-start | bytes 6148
  119.5 1.4 copy-start.13
  120.9 3.9 copy-start.23
  125.1 0.9 copy-start.15
  125.9 37.5 %copy-start.21 = (s32[128]{0:T(128)S(1)}, s32[128]{0:T(128)}, u32[]{:S(2)}) copy-start(s32[128]{0:T(128)} %param.27) | copy-start | bytes 1540
  186.3 154.5 %copy-start.20 = (f32[2,256]{1,0:T(2,128)S(1)}, f32[2,256]{1,0:T(2,128)}, u32[]{:S(2)}) copy-start(f32[2,256]{1,0:T(2,128)} %param.39) | copy-start | bytes 6148
  186.3 154.6 %copy-start.17 = (f32[3816]{0:T(1024)S(1)}, f32[3816]{0:T(1024)}, u32[]{:S(2)}) copy-start(f32[3816]{0:T(1024)} %param.36) | copy-start | bytes 45796
  186.3 154.6 %copy-start.19 = (f32[2,3,64]{2,0,1:T(2,128)S(1)}, f32[2,3,64]{2,0,1:T(2,128)}, u32[]{:S(2)}) copy-start(f32[2,3,64]{2,0,1:T(2,128)} %param.38) | copy-start | bytes 4612
  186.3 154.7 %copy-start.22 = (f32[64]{0:T(128)S(1)}, f32[64]{0:T(128)}, u32[]{:S(2)}) copy-start(f32[64]{0:T(128)} %param.37) | copy-start | bytes 772
  186.3 154.7 %copy-start.14 = (s32[4,8,1,128]{3,2,1,0:T(1,128)S(1)}, s32[4,8,1,128]{3,2,1,0:T(1,128)}, u32[]{:S(2)}) copy-start(s32[4,8,1,128]{3,2,1,0:T(1,128)} %copy-done.13) | copy-start | bytes 49156
  341.0 40.0 %copy-start = (f32[2,64,4096]{2,1,0:T(8,128)S(1)}, f32[2,64,4096]{2,1,0:T(8,128)}, u32[]{:S(2)}) copy-start(f32[2,64,4096]{2,1,0:T(8,128)} %gate_ref.1) | copy-start | bytes 6291460
  341.0 40.0 %copy-start.2 = (f32[2,256,512]{2,1,0:T(8,128)S(1)}, f32[2,256,512]{2,1,0:T(8,128)}, u32[]{:S(2)}) copy-start(f32[2,256,512]{2,1,0:T(8,128)} %low_ref.1) | copy-start | bytes 3145732
  341.0 40.0 %copy-start.11 = (f32[2,512]{1,0:T(2,128)S(1)}, f32[2,512]{1,0:T(2,128)}, u32[]{:S(2)}) copy-start(f32[2,512]{1,0:T(2,128)} %top_cols_ref.1) | copy-start | bytes 12292
  363.5 17.5 %copy-start.18 = (f32[3816]{0:T(1024)}, f32[3816]{0:T(1024)S(1)}, u32[]{:S(2)}) copy-start(f32[3816]{0:T(1024)S(1)} %get-tuple-element.354) | copy-start | bytes 45796
  381.1 1.1 copy-start.4
  382.2 0.9 copy-start.5
  383.2 0.9 copy-start.8
  384.1 0.8 copy-start.10
  384.9 14.6 %copy-start.6 = (f32[32,3,512]{2,1,0:T(4,128)S(1)}, f32[32,3,512]{2,1,0:T(4,128)}, u32[]{:S(2)}) copy-start(f32[32,3,512]{2,1,0:T(4,128)} %shard_map.343.stat_ref) | copy-start | bytes 589828

commit v5 on v4

--- a/solution.py
+++ b/solution.py
@@ -422,9 +422,6 @@
 
 SLOTS = 80
 PART = 1024
-HEAD_AT = 2 * PART
-NORM_AT = HEAD_AT + 64
-PACKED = NORM_AT + 32
 
 
 MESH = pl.DeviceIdType.MESH
@@ -445,149 +442,6 @@
 
 def mult(v, m=16):
     return pl.multiple_of(v, m)
-
-def gather_kernel(chunks, w_ref, ask_ref, table_ref, ag_ref, got_ref, asks_ref, table, picked, rows_s,
-                  zs, zr, xs, xr, ys, yr, cs, cr, ls, es, er, qs, qr):
-    z, x, y, c = place()
-    me = z * 2 + x
-    g = y * 2 + c
-    g2 = (1 - y) * 2 + c
-    ep = [(lax.rem(me + k, 8), g) for k in range(8)]
-    zp = [dev((z + k) % 4, x, y, c) for k in range(4)]
-    xp, yp, cp = dev(z, 1 - x, y, c), dev(z, x, 1 - y, c), dev(z, x, y, 1 - c)
-    entry_barrier(ep[1:] + [yp, cp])
-    Q = len(chunks)
-    hs = [mult(b + c * h + y * nb) for b, h, nb in chunks]
-    nh = [h - nb for b, h, nb in chunks]
-    bs = [mult(b + c * h + y * (h - nb)) for b, h, nb in chunks]
-    nbs = [nb for b, h, nb in chunks]
-    cb = [mult(b + c * h) for b, h, nb in chunks]
-    nc = [h for b, h, nb in chunks]
-    def rc(src, dst, s, r, d):
-        return pltpu.make_async_remote_copy(src, dst, s, r, device_id=d, device_id_type=MESH)
-    def shard(k, f):
-        return ((z + 4 - k) % 4) * 2 + (x if f == 0 else 1 - x)
-    qc = [rc(ask_ref.at[ep[k][0]], asks_ref.at[g, me], qs.at[k], qr.at[k], ep[k]) for k in range(1, 8)]
-    for copy in qc:
-        copy.start()
-    mine = pltpu.make_async_copy(ask_ref.at[me], asks_ref.at[g, me], ls.at[0])
-    mine.start()
-    near = pltpu.make_async_copy(table_ref, table.at[pl.ds(0, table_ref.shape[0])], ls.at[1])
-    near.start()
-    qy = rc(asks_ref.at[g], asks_ref.at[g], qs.at[8], qr.at[8], yp)
-    qcc = rc(asks_ref.at[g], asks_ref.at[g], qs.at[9], qr.at[9], cp)
-    qd = rc(asks_ref.at[g2], asks_ref.at[g2], qs.at[10], qr.at[10], cp)
-    own = pltpu.make_async_copy(w_ref, ag_ref.at[me], ls.at[2])
-    own.start()
-    kept = pltpu.make_async_copy(rows_s.at[me], got_ref.at[me], ls.at[3])
-    ec = [rc(rows_s.at[ep[k][0]], got_ref.at[me], es.at[k], er.at[k], ep[k]) for k in range(1, 8)]
-    def pick_rows():
-        mine.wait()
-        for copy in qc:
-            copy.wait_recv()
-        qy.start()
-        qcc.start()
-        wanted = asks_ref[pl.ds(g, 1)].reshape(8, 128).astype(jnp.float32).T
-        near.wait()
-        depth = table.shape[0] // 5
-        table[pl.ds(table_ref.shape[0], table.shape[0] - table_ref.shape[0]), :] = jnp.zeros(
-            (table.shape[0] - table_ref.shape[0], 512), jnp.float32
-        )
-        picked[...] = jnp.zeros(picked.shape, jnp.float32)
-        ramp = lax.broadcasted_iota(jnp.int32, (SLOTS, depth), 1).astype(jnp.float32)
-        def body(i, carry):
-            start = pl.multiple_of(i * depth, depth)
-            low = table[pl.ds(start, depth), :].astype(BF)
-            shifted = ramp + (i * depth).astype(jnp.float32)
-            for r in range(8):
-                hot = jnp.where(wanted[:SLOTS, r : r + 1] == shifted, 1.0, 0.0).astype(BF)
-                picked[r] += jnp.dot(hot, low, preferred_element_type=jnp.float32)
-            return carry
-        lax.fori_loop(0, 5, body, 0)
-        rows_s[...] = picked[...].astype(BF)
-        kept.start()
-        for copy in ec:
-            copy.start()
-    zc = {}; xc = {}; yc = {}; cc = {}
-    for q in range(Q):
-        for k in range(1, 4):
-            zc[q, k] = rc(w_ref.at[pl.ds(hs[q], nh[q])], ag_ref.at[me, pl.ds(hs[q], nh[q])], zs.at[q, k], zr.at[q, k], zp[k])
-        for k in range(4):
-            src = w_ref.at[pl.ds(hs[q], nh[q])] if k == 0 else ag_ref.at[shard(k, 0), pl.ds(hs[q], nh[q])]
-            xc[q, k] = rc(src, ag_ref.at[shard(k, 0), pl.ds(hs[q], nh[q])], xs.at[q, k], xr.at[q, k], xp)
-        for k in range(4):
-            for f in range(2):
-                if k == 0 and f == 0: continue
-                s = shard(k, f)
-                yc[q, k, f] = rc(ag_ref.at[s, pl.ds(bs[q], nbs[q])], ag_ref.at[s, pl.ds(bs[q], nbs[q])], ys.at[q, 2 * k + f], yr.at[q, 2 * k + f], yp)
-                cc[q, k, f] = rc(ag_ref.at[s, pl.ds(cb[q], nc[q])], ag_ref.at[s, pl.ds(cb[q], nc[q])], cs.at[q, 2 * k + f], cr.at[q, 2 * k + f], cp)
-    def s0(q):
-        for k in (2, 1, 3):
-            zc[q, k].start()
-        xc[q, 0].start()
-    def s1(q):
-        for k in (1, 3, 2):
-            zc[q, k].wait_recv()
-            xc[q, k].start()
-            yc[q, k, 0].start()
-    def s2(q):
-        for k in (0, 1, 3, 2):
-            xc[q, k].wait_recv()
-            yc[q, k, 1].start()
-    def s3(q):
-        for k, f in ((1, 0), (3, 0), (2, 0), (0, 1), (1, 1), (3, 1), (2, 1)):
-            yc[q, k, f].wait_recv()
-            cc[q, k, f].start()
-    st = [s0, s1, s2, s3]
-    for t in range(Q + 3):
-        for i in reversed(range(4)):
-            q = t - i
-            if 0 <= q < Q:
-                st[i](q)
-        if t == 0:
-            pick_rows()
-        if t == 2:
-            qy.wait_recv()
-            qd.start()
-    for q in range(Q):
-        for k in range(4):
-            for f in range(2):
-                if k or f: cc[q, k, f].wait_recv()
-    for d in (zc, xc, cc) + (yc,):
-        for v in d.values(): v.wait_send()
-    for copy in ec:
-        copy.wait()
-    qcc.wait_recv()
-    qd.wait_recv()
-    for copy in qc + [qy, qcc, qd]:
-        copy.wait_send()
-    own.wait()
-    kept.wait()
-
-def gather_weights(w, asks, table, chunks, cid):
-    Q = len(chunks)
-    D = pltpu.SemaphoreType.DMA
-    anywhere = pl.BlockSpec(memory_space=pl.ANY)
-    near = pl.BlockSpec(memory_space=pltpu.VMEM)
-    padded = -(-table.shape[0] // 640) * 640
-    return pl.pallas_call(
-        functools.partial(gather_kernel, chunks),
-        out_shape=(jax.ShapeDtypeStruct((8,) + w.shape, w.dtype), jax.ShapeDtypeStruct((8, SLOTS, 512), BF), jax.ShapeDtypeStruct((4,) + asks.shape, asks.dtype)),
-        in_specs=[anywhere, near, anywhere], out_specs=[anywhere, anywhere, near],
-        scratch_shapes=[pltpu.VMEM((padded, 512), jnp.float32), pltpu.VMEM((8, SLOTS, 512), jnp.float32), pltpu.VMEM((8, SLOTS, 512), BF),
-            D((Q, 4)), D((Q, 4)), D((Q, 4)), D((Q, 4)), D((Q, 8)), D((Q, 8)), D((Q, 8)), D((Q, 8)), D((4,)), D((8,)), D((8,)), D((11,)), D((11,))],
-        compiler_params=pltpu.CompilerParams(collective_id=cid, has_side_effects=True, vmem_limit_bytes=48 * 2**20),
-    )(w, asks, table)
-
-def plan(rows, count, share):
-    units = rows // 32
-    chunks = []
-    base = 0
-    for i in range(count):
-        size = units // count + (1 if i < units % count else 0)
-        chunks.append((base, 16 * size, 16 * int(round(size * share))))
-        base += 32 * size
-    return chunks
 
 
 def slot_plan(token_ids, shard_rows):
@@ -627,7 +481,7 @@
         norm_master.reshape(10, -1).astype(jnp.bfloat16), ((0, 22), (0, D - norm_master.shape[2]))
     )
     return jnp.concatenate(
-        [layers.reshape(-1, D), head_master.astype(jnp.bfloat16), norm_rows], axis=0
+        [norm_rows, layers.reshape(-1, D), head_master.astype(jnp.bfloat16)], axis=0
     )
 
 
@@ -759,18 +613,7 @@
 
     @pl.when(layer == LAYERS - 1)
     def _():
-        scaled, _ = norm_parts(x_s[...])
-        final = scaled * norm_ref[8:9, :] + norm_ref[9:10, :]
-        member = members(seg_row_ref, valid_ref)
-        counts = jnp.maximum(jnp.sum(member, axis=1, keepdims=True), 1.0)
-        pooled = (exact_dot(member, final) / counts).astype(jnp.bfloat16)
-        pool_ref[...] = pooled
-        zed = dot_nn(pooled, head_ref[...].reshape(D, D))
-        zed_ref[...] = zed
-        unit = zed * lax.rsqrt(jnp.sum(zed * zed, axis=-1, keepdims=True) + UNIT_EPS)
-        for s in range(4):
-            for part in range(4):
-                unit_ref[4 * s + part : 4 * s + part + 1, :] = unit[s : s + 1, part * 128 : (part + 1) * 128]
+        pool_units(x_s, norm_ref, seg_row_ref, valid_ref, head_ref, unit_ref, pool_ref, zed_ref)
 
 
 def members(seg_row_ref, valid_ref):
@@ -793,7 +636,7 @@
         in_specs=[
             whole((tokens, D)), whole((tokens, 1)), whole((1, tokens)), whole((1, tokens)),
             pl.BlockSpec((8, PART, D), lambda i: (0, i, 0)),
-            pl.BlockSpec((8, 64, D), lambda i: (0, HEAD_AT // 64, 0)),
+            pl.BlockSpec((8, 64, D), lambda i: (0, 2 * PART // 64, 0)),
             whole(norms.shape),
         ],
         out_specs=[
@@ -817,6 +660,395 @@
         ],
         compiler_params=pltpu.CompilerParams(vmem_limit_bytes=60 * 2**20),
     )(first, seg_col, seg_row, valid, weights, weights, norms)
+
+
+PACK_LAYER = (32, 32 + PART)
+PACK_HEAD = 32 + 2 * PART
+PARCELS = (
+    (0, 144, 64), (288, 128, 48), (544, 128, 48), (800, 128, 48),
+    (1056, 128, 48), (1312, 128, 48), (1568, 128, 48), (1824, 160, 32),
+)
+GATHER_ORDER = (
+    "ask", "s00", "s01", "s02", "s03", "set", "ans", "z00", "z10", "x03", "z20", "x13", "x23", "rel", "x33", "y000",
+    "z30", "y100", "y031", "y131", "z01", "z11", "y200", "z21", "y231", "y300", "z31", "y331", "y010", "x00", "y210",
+    "y110", "x10", "z02", "s04", "x20", "y001", "y310", "x01", "z12", "s05", "x11", "y101", "y020", "x30", "z22",
+    "s06", "z40", "y011", "x21", "y201", "z32", "s07", "x31", "y301", "y111", "z50", "y120", "y400", "y220", "x02",
+    "y211", "x43", "z41", "y311", "y320", "z60", "x12", "y500", "z42", "z51", "x53", "z70", "y021", "y431", "z52",
+    "y410", "x40", "z61", "x22", "y600", "x63", "a0", "y121", "z62", "y420", "y510", "rows", "y531", "z71", "x50",
+    "x32", "y700", "p0", "x73", "y401", "a1", "y520", "y221", "z72", "h00", "y610", "y631", "h01", "x60", "x41",
+    "x42", "h02", "x51", "a2", "y620", "h03", "y321", "y501", "y710", "x70", "h04", "y731", "x52", "h05", "x61",
+    "y720", "a3", "h06", "y601", "y411", "h07", "y421", "m0", "y511", "x62", "y701", "x71", "f00", "y521", "y611",
+    "a4", "x72", "f01", "y621", "a5", "y711", "p1", "h10", "y721", "a6", "h11", "h12", "h13", "h14", "a7", "h15",
+    "h16", "h17", "m1", "f10", "f11", "end",
+)
+
+
+def nearest(z):
+    return (z + 1 - 2 * (z % 2), 2 - z // 2, 3 - 3 * (z // 2), z)
+
+
+def gather_stages(w_ref, ag_ref, zs, zr, xs, xr, ys, yr, cs, cr):
+    z, x, y, c = place()
+    me = z * 2 + x
+    inner = (z == 1) | (z == 2)
+    pair = dev(z + 1 - 2 * (z % 2), x, y, c)
+    across = dev(3 - z, x, y, c)
+    outward = dev((3 * z + 1) % 4, x, y, c)
+    xp, yp, cp = dev(z, 1 - x, y, c), dev(z, x, 1 - y, c), dev(z, x, y, 1 - c)
+    near = nearest(z)
+
+    def rc(src, dst, s, r, d):
+        return pltpu.make_async_remote_copy(src, dst, s, r, device_id=d, device_id_type=MESH)
+
+    def shard(n, f):
+        return near[n] * 2 + (x if f == 0 else 1 - x)
+
+    steps = {}
+    always, within = [], []
+    others = [(0, 0), (1, 0), (2, 0), (3, 1), (0, 1), (1, 1), (2, 1)]
+
+    def parcel(q, base, half, spare):
+        main = pl.ds(mult(base + c * half + y * spare), half - spare)
+        extra = pl.ds(mult(base + c * half + y * (half - spare)), spare)
+        every = pl.ds(mult(base + c * half), half)
+
+        def at(n, f, rows):
+            return ag_ref.at[shard(n, f), rows]
+
+        own = w_ref.at[main]
+        to_pair = rc(own, at(3, 0, main), zs.at[q, 0], zr.at[q, 0], pair)
+        to_across = rc(own, at(3, 0, main), zs.at[q, 1], zr.at[q, 1], across)
+        on = [
+            rc(at(0, 0, main), at(0, 0, main), zs.at[q, 2], zr.at[q, 2], across),
+            rc(at(1, 0, main), at(1, 0, main), zs.at[q, 3], zr.at[q, 1], outward),
+            rc(at(2, 0, main), at(2, 0, main), zs.at[q, 4], zr.at[q, 2], outward),
+        ]
+        over = [rc(own if n == 3 else at(n, 0, main), at(n, 0, main), xs.at[q, n], xr.at[q, n], xp) for n in range(4)]
+        planes, cores = {}, {}
+        for n, f in others:
+            planes[n, f] = rc(at(n, f, extra), at(n, f, extra), ys.at[q, 2 * n + f], yr.at[q, 2 * n + f], yp)
+            cores[n, f] = rc(at(n, f, every), at(n, f, every), cs.at[q, 2 * n + f], cr.at[q, 2 * n + f], cp)
+        always.extend([to_pair] + over + list(planes.values()) + list(cores.values()))
+        within.extend([to_across] + on)
+        landed = [rc(own, at(n, 0, main), zs.at[q, 0], zr.at[q, n], pair) for n in range(3)]
+
+        def issue():
+            pl.when(inner)(to_across.start)
+            to_pair.start()
+            over[3].start()
+
+        def along(n):
+            landed[n].wait_recv()
+            pl.when(inner)(on[n].start)
+            over[n].start()
+            planes[n, 0].start()
+
+        def sideways(n):
+            over[n].wait_recv()
+            planes[n, 1].start()
+
+        def plane(n, f):
+            planes[n, f].wait_recv()
+            cores[n, f].start()
+
+        def arrived():
+            for copy in cores.values():
+                copy.wait_recv()
+
+        steps["s0%d" % q] = (issue,)
+        for n in range(3):
+            steps["z%d%d" % (q, n)] = (along, n)
+        for n in range(4):
+            steps["x%d%d" % (q, n)] = (sideways, n)
+        for n, f in others:
+            steps["y%d%d%d" % (q, n, f)] = (plane, n, f)
+        steps["a%d" % q] = (arrived,)
+
+    for q, spec in enumerate(PARCELS):
+        parcel(q, *spec)
+
+    def finish():
+        for copy in always:
+            copy.wait_send()
+
+        @pl.when(inner)
+        def _():
+            for copy in within:
+                copy.wait_send()
+
+    return steps, finish
+
+
+def request_stages(ask_ref, asks_ref, table_ref, table, picked, rows_s, got, sems, es, er, qs, qr):
+    z, x, y, c = place()
+    me = z * 2 + x
+    g = y * 2 + c
+    g2 = (1 - y) * 2 + c
+    ep = [(lax.rem(me + k, 8), g) for k in range(8)]
+    yp, cp = dev(z, x, 1 - y, c), dev(z, x, y, 1 - c)
+
+    def rc(src, dst, s, r, d):
+        return pltpu.make_async_remote_copy(src, dst, s, r, device_id=d, device_id_type=MESH)
+
+    count = rows_s.shape[1]
+    to_owner = [rc(ask_ref.at[ep[k][0]], asks_ref.at[g, me], qs.at[k], qr.at[k], ep[k]) for k in range(1, 8)]
+    mine = pltpu.make_async_copy(ask_ref.at[me], asks_ref.at[g, me], sems.at[0])
+    near = pltpu.make_async_copy(table_ref, table.at[pl.ds(0, table_ref.shape[0])], sems.at[1])
+    to_plane = rc(asks_ref.at[g], asks_ref.at[g], qs.at[8], qr.at[8], yp)
+    to_core = rc(asks_ref.at[g], asks_ref.at[g], qs.at[9], qr.at[9], cp)
+    on_core = rc(asks_ref.at[g2], asks_ref.at[g2], qs.at[10], qr.at[10], cp)
+    kept = pltpu.make_async_copy(rows_s.at[me], got.at[me], sems.at[2])
+    answers = [rc(rows_s.at[ep[k][0]], got.at[me], es.at[k], er.at[k], ep[k]) for k in range(1, 8)]
+
+    def load():
+        near.start()
+
+    def ask():
+        for copy in to_owner:
+            copy.start()
+        mine.start()
+
+    def answer():
+        mine.wait()
+        for copy in to_owner:
+            copy.wait_recv()
+        to_plane.start()
+        to_core.start()
+        wanted = asks_ref[pl.ds(g, 1)].reshape(8, 128).astype(jnp.float32).T
+        near.wait()
+        depth = table.shape[0] // 5
+        rest = table.shape[0] - table_ref.shape[0]
+        table[pl.ds(table_ref.shape[0], rest), :] = jnp.zeros((rest, D), jnp.float32)
+        picked[...] = jnp.zeros(picked.shape, jnp.float32)
+        ramp = lax.broadcasted_iota(jnp.int32, (count, depth), 1).astype(jnp.float32)
+
+        def body(i, carry):
+            low = table[pl.ds(pl.multiple_of(i * depth, depth), depth), :].astype(BF)
+            shifted = ramp + (i * depth).astype(jnp.float32)
+            for r in range(8):
+                hot = jnp.where(wanted[:count, r : r + 1] == shifted, 1.0, 0.0).astype(BF)
+                picked[r] += dot_nn(hot, low)
+            return carry
+
+        lax.fori_loop(0, 5, body, 0)
+        rows_s[...] = picked[...].astype(BF)
+        kept.start()
+        for copy in answers:
+            copy.start()
+
+    def relay():
+        to_plane.wait_recv()
+        on_core.start()
+
+    def take():
+        kept.wait()
+        for copy in answers:
+            copy.wait_recv()
+
+    def finish():
+        to_core.wait_recv()
+        on_core.wait_recv()
+        for copy in answers + to_owner + [to_plane, to_core, on_core]:
+            copy.wait_send()
+
+    return load, ask, answer, relay, take, finish
+
+
+def gather_forward_kernel(
+    w_ref, ask_ref, table_ref, key_ref, seg_col_ref, seg_row_ref, valid_ref,
+    ag_ref, asks_ref, low_out, qkv_out, lse_out, mix_out, one_out, two_out, unit_ref, pool_ref, zed_ref, norm_ref,
+    table, picked, rows_s, got, weights, head, norm_low, low_s, qkv_s, lse_s, mix_s, one_s, two_s, x_s, far, acc,
+    zs, zr, xs, xr, ys, yr, cs, cr, sems, es, er, qs, qr, loads, saves,
+):
+    z, x, y, c = place()
+    me = z * 2 + x
+    g = y * 2 + c
+    tokens = x_s.shape[0]
+    tiles = tokens // TILE
+    peers = [(lax.rem(me + k, 8), g) for k in range(1, 8)] + [dev(z, x, 1 - y, c), dev(z, x, y, 1 - c)]
+    barrier = pltpu.get_barrier_semaphore()
+    for peer in peers:
+        pl.semaphore_signal(barrier, inc=1, device_id=peer, device_id_type=MESH)
+    steps, finish = gather_stages(w_ref, ag_ref, zs, zr, xs, xr, ys, yr, cs, cr)
+    load, ask, answer, relay, take, ask_finish = request_stages(
+        ask_ref, asks_ref, table_ref, table, picked, rows_s, got, sems, es, er, qs, qr
+    )
+    own = pltpu.make_async_copy(w_ref, ag_ref.at[me], sems.at[3])
+
+    def loading(slot, rows, count, into):
+        return pltpu.make_async_copy(ag_ref.at[:, pl.ds(rows, count)], into, loads.at[slot])
+
+    fetch = {("norm", 0): loading(8, 0, 32, norm_low), ("head", 0): loading(9, PACK_HEAD, 64, head)}
+    for layer in range(LAYERS):
+        for part in range(4):
+            fetch[layer, part] = loading(
+                4 * layer + part, PACK_LAYER[layer] + 256 * part, 256, weights.at[layer, :, pl.ds(256 * part, 256)]
+            )
+    saving = {}
+    for layer in range(LAYERS):
+        for i, (source, target) in enumerate(
+            ((low_s, low_out), (qkv_s, qkv_out), (lse_s, lse_out), (mix_s, mix_out), (one_s, one_out), (two_s, two_out))
+        ):
+            saving[layer, i] = pltpu.make_async_copy(source.at[layer], target.at[layer], saves.at[layer, i])
+
+    def begin():
+        load()
+        own.start()
+
+    def arrive(q):
+        arrived[q]()
+        if q == 0:
+            own.wait()
+            fetch["norm", 0].start()
+        fetch[q // 4, q % 4].start()
+        if q == 7:
+            fetch["head", 0].start()
+
+    def set_up():
+        fill_distance(far, seg_col_ref, seg_row_ref)
+
+    def first_rows():
+        take()
+        slots = lax.broadcasted_iota(jnp.int32, (tokens, got.shape[0] * got.shape[1]), 1)
+        picks = jnp.where(slots == key_ref[...], 1.0, 0.0).astype(BF)
+        x_s[...] = dot_nn(picks, got[...].reshape(-1, D))
+        fetch["norm", 0].wait()
+        norm_ref[...] = jnp.concatenate([norm_low[d, 0:16, 0:64].astype(jnp.float32) for d in range(8)], axis=1)
+
+    def project(layer):
+        fetch[layer, 0].wait()
+
+        def body(i, carry):
+            rows = pl.ds(pl.multiple_of(i * TILE, TILE), TILE)
+            low = x_s[rows, :].astype(BF)
+            low_s[layer, rows, :] = low
+            for j in range(3):
+                qkv_s[layer, rows, j * D : (j + 1) * D] = dot_nn(low, block(weights.at[layer], j * 64)).astype(BF)
+            return carry
+
+        lax.fori_loop(0, tiles, body, 0)
+        saving[layer, 0].start()
+        saving[layer, 1].start()
+
+    def attend_head(layer, head):
+        lanes = slice(head * HEAD_DIM, (head + 1) * HEAD_DIM)
+        keys = qkv_s[layer, :, D + head * HEAD_DIM : D + (head + 1) * HEAD_DIM]
+        vals_t = qkv_s[layer, :, 2 * D + head * HEAD_DIM : 2 * D + (head + 1) * HEAD_DIM].T
+        slope = 2.0 ** (-8.0 * (head + 1) / HEADS)
+        for i in range(tiles):
+            cols = slice(i * TILE, (i + 1) * TILE)
+            scores = dot_nt(keys, qkv_s[layer, cols, lanes]) * HEAD_DIM**-0.5 - slope * far[:, cols]
+            top = jnp.max(scores, axis=0, keepdims=True)
+            raised = jnp.exp(scores - top)
+            total = jnp.sum(raised, axis=0, keepdims=True)
+            lse_s[layer, head, :, cols] = top + jnp.log(total)
+            prob = (raised * (1.0 / total)).astype(BF)
+            mix_s[layer, lanes, cols] = dot_nn(vals_t, prob).astype(BF)
+
+    def mix(layer):
+        saving[layer, 2].start()
+        saving[layer, 3].start()
+        acc[...] = dot_tn(mix_s[layer], block(weights.at[layer], 192))
+
+    def feed(layer, i):
+        if i == 0:
+            for part in (1, 2, 3):
+                fetch[layer, part].wait()
+        rows = pl.ds(i * TILE, TILE)
+        resid = x_s[rows, :] + acc[rows, :]
+        one_s[layer, rows, :] = resid
+        at = 4 * layer
+        scaled, _ = norm_parts(resid)
+        hidden = scaled * norm_ref[at : at + 1, :] + norm_ref[at + 1 : at + 2, :]
+        low = hidden.astype(BF)
+        total = hidden
+        for j in range(4):
+            gate = dot_nn(low, block(weights.at[layer], 256 + j * 64))
+            up = dot_nn(low, block(weights.at[layer], 512 + j * 64))
+            bend = jnp.tanh(GELU_SCALE * (gate + GELU_CUBE * gate * gate * gate))
+            mid = (0.5 * gate * (1.0 + bend) * up).astype(BF)
+            total = total + dot_nn(mid, down_block(weights.at[layer], j))
+        two_s[layer, rows, :] = total
+        scaled, _ = norm_parts(total)
+        x_s[rows, :] = scaled * norm_ref[at + 2 : at + 3, :] + norm_ref[at + 3 : at + 4, :]
+        if i == tiles - 1:
+            saving[layer, 4].start()
+            saving[layer, 5].start()
+
+    def end():
+        fetch["head", 0].wait()
+        pool_units(x_s, norm_ref, seg_row_ref, valid_ref, head, unit_ref, pool_ref, zed_ref)
+
+    arrived = [steps["a%d" % q][0] for q in range(8)]
+    for q in range(8):
+        steps["a%d" % q] = (arrive, q)
+    steps["ask"], steps["ans"], steps["rel"] = (ask,), (answer,), (relay,)
+    steps["set"], steps["rows"], steps["end"] = (set_up,), (first_rows,), (end,)
+    for layer in range(LAYERS):
+        steps["p%d" % layer], steps["m%d" % layer] = (project, layer), (mix, layer)
+        for head_index in range(HEADS):
+            steps["h%d%d" % (layer, head_index)] = (attend_head, layer, head_index)
+        for i in range(tiles):
+            steps["f%d%d" % (layer, i)] = (feed, layer, i)
+    begin()
+    pl.semaphore_wait(barrier, len(peers))
+    for name in GATHER_ORDER:
+        fn, *rest = steps.pop(name)
+        fn(*rest)
+    assert not steps
+    finish()
+    ask_finish()
+    for copy in saving.values():
+        copy.wait()
+
+
+def pool_units(x_s, norm_ref, seg_row_ref, valid_ref, head, unit_ref, pool_ref, zed_ref):
+    scaled, _ = norm_parts(x_s[...])
+    final = scaled * norm_ref[8:9, :] + norm_ref[9:10, :]
+    member = members(seg_row_ref, valid_ref)
+    counts = jnp.maximum(jnp.sum(member, axis=1, keepdims=True), 1.0)
+    pooled = (exact_dot(member, final) / counts).astype(BF)
+    pool_ref[...] = pooled
+    zed = dot_nn(pooled, head[...].reshape(D, D))
+    zed_ref[...] = zed
+    unit = zed * lax.rsqrt(jnp.sum(zed * zed, axis=-1, keepdims=True) + UNIT_EPS)
+    for s in range(4):
+        for part in range(4):
+            unit_ref[4 * s + part : 4 * s + part + 1, :] = unit[s : s + 1, part * 128 : (part + 1) * 128]
+
+
+def run_gather_forward(packed, asks, embed, key_col, seg_col, seg_row, valid, cid):
+    tokens = key_col.shape[0]
+    low, full = jnp.bfloat16, jnp.float32
+    near = pl.BlockSpec(memory_space=pltpu.VMEM)
+    anywhere = pl.BlockSpec(memory_space=pl.ANY)
+    shape = jax.ShapeDtypeStruct
+    vmem = lambda dims, kind=low: pltpu.VMEM(dims, kind)
+    sems = lambda *dims: pltpu.SemaphoreType.DMA(dims)
+    padded = -(-embed.shape[0] // 640) * 640
+    saved = [
+        ((LAYERS, tokens, D), low), ((LAYERS, tokens, 3 * D), low), ((LAYERS, HEADS, 1, tokens), full),
+        ((LAYERS, D, tokens), low), ((LAYERS, tokens, D), full), ((LAYERS, tokens, D), full),
+    ]
+    return pl.pallas_call(
+        gather_forward_kernel,
+        in_specs=[anywhere, near, anywhere, near, near, near, near],
+        out_specs=[anywhere, near] + [anywhere] * 6 + [near] * 4,
+        out_shape=[shape((8,) + packed.shape, low), shape((4,) + asks.shape, asks.dtype)]
+        + [shape(*v) for v in saved]
+        + [shape((16, 128), full), shape((8, D), low), shape((8, D), full), shape((16, D), full)],
+        scratch_shapes=[
+            vmem((padded, D), full), vmem((8, SLOTS, D), full), vmem((8, SLOTS, D)), vmem((8, SLOTS, D)),
+            vmem((LAYERS, 8, PART, D)), vmem((8, 64, D)), vmem((8, 32, D)),
+        ]
+        + [vmem(*v) for v in saved]
+        + [
+            vmem((tokens, D), full), vmem((tokens, tokens), full), vmem((tokens, D), full),
+            sems(8, 5), sems(8, 3), sems(8, 4), sems(8, 4), sems(8, 8), sems(8, 8), sems(8, 8), sems(8, 8),
+            sems(4), sems(8), sems(8), sems(11), sems(11), sems(10), sems(2, 6),
+        ],
+        compiler_params=pltpu.CompilerParams(collective_id=cid, has_side_effects=True, vmem_limit_bytes=62 * 2**20),
+    )(packed, asks, embed, key_col, seg_col, seg_row, valid)
 
 
 def contrast_kernel(unit_ref, deal_col_ref, deal_row_ref, scale_ref, loss_ref, own_ref, slope_ref, every, ss, rs, ls):
@@ -1113,7 +1345,7 @@
     rows_out = row_exchange(slots, t_ref, norm_s, norm_out, nbuf, es, er, el, ns, nr)
 
     def loading(layer):
-        base = layer * PART
+        base = PACK_LAYER[layer]
         copy = pltpu.make_async_copy
         return {
             "two": copy(two_in.at[layer], two_ref, loads.at[layer, 0]),
@@ -1127,7 +1359,7 @@
         }
 
     load = [loading(layer) for layer in range(LAYERS)]
-    head_load = pltpu.make_async_copy(w_ref.at[:, pl.ds(HEAD_AT, 64)], head, loads.at[0, 8])
+    head_load = pltpu.make_async_copy(w_ref.at[:, pl.ds(PACK_HEAD, 64)], head, loads.at[0, 8])
     head_load.start()
     for copy in load[1].values():
         copy.start()
@@ -1660,25 +1892,20 @@
         [wanted.reshape(8, 1, SLOTS), jnp.broadcast_to(most, (8, 1, 128 - SLOTS))], axis=2
     ).astype(jnp.int32)
     packed = pack_weights(attn_in, attn_out, ffn_in, ffn_out, head_master, norm_master)
-    weights, got_rows, asked = gather_weights(packed, asks, embed_master, plan(PACKED, 4, 0.36), 0)
-    crowded = jnp.max(asked[:, :, 0, SLOTS:]) >= SLOTS
-
-    def dense_rows():
-        table = lax.all_gather(embed_master.astype(jnp.bfloat16), "dp", axis=0, tiled=True)
-        return jnp.take(table, token_ids, axis=0)
-
-    def slot_rows():
-        return jnp.take(got_rows.reshape(-1, D), jnp.minimum(key, 8 * SLOTS - 1), axis=0)
-
-    stream = lax.cond(crowded, dense_rows, slot_rows)
-    norms = jnp.pad(
-        weights[:, NORM_AT : NORM_AT + 10, :64].transpose(1, 0, 2).reshape(10, D).astype(jnp.float32),
-        ((0, 6), (0, 0)),
-    )
     seg_col, seg_row = segment.reshape(-1, 1), segment.reshape(1, -1)
     valid_row = valid_mask.reshape(1, -1)
-    *saved, unit_parts, pooled_low, head_out = run_forward(
-        stream, seg_col, seg_row, valid_row, weights, norms
+    weights, asked, *saved, norms = run_gather_forward(
+        packed, asks, embed_master, key.reshape(-1, 1), seg_col, seg_row, valid_row, 0
+    )
+    crowded = jnp.max(asked[:, :, 0, SLOTS:]) >= SLOTS
+
+    def dense_forward(state):
+        table = lax.all_gather(embed_master.astype(jnp.bfloat16), "dp", axis=0, tiled=True)
+        first = jnp.take(table, token_ids, axis=0)
+        return (False, *run_forward(first, seg_col, seg_row, valid_row, weights[:, 32:], norms))
+
+    _, *saved, unit_parts, pooled_low, head_out = lax.while_loop(
+        lambda state: state[0], dense_forward, (crowded, *saved)
     )
     loss_value, own_rows, grad_scale = run_contrast(unit_parts, deal_order, log_scale, 1)
     loss_value, grad_scale = loss_value[0, 0], grad_scale[0]

time: 424 us -> 397 us (0.936)
  Pallas kernels: 365 us -> 337 us
    pallas_call x2 -> x1, Pallas kernels: 138 us -> 117 us  [run_gather_forward(): pl.pallas_call(gather_forward_kernel, in_specs=[anywhere, near, anywhere,...]
    pallas_call x1, Pallas kernels: 19.3 us -> 12.6 us  [run_contrast(): pl.pallas_call(contrast_kernel, out_shape=[one, jax.ShapeDtypeStruct((8,...]
    unnamed x0 -> x1, other arithmetic: none -> 5.64 us
where the time goes in v5:
time: 397 us; the launch traced here: 391 us
  Pallas kernels  337 us (85%)
  between operations  22.5 us (6%)
  other arithmetic  16 us (4%)
  local copies, waits for them, and re-layouts  15.5 us (4%)
    pallas_call x1, Pallas kernels, run_backward(): pl.pallas_call(backward_kernel, in_specs=[near] * 8 + [anywhere] * 7, out...  154 us
    pallas_call x1, Pallas kernels, run_gather_forward(): pl.pallas_call(gather_forward_kernel, in_specs=[anywhere, near, anywhere,...  117 us
    pallas_call x1, Pallas kernels, run_stats(): pl.pallas_call(functools.partial(stats_kernel, dense, row_count), grid=(-...  21.3 us
    pallas_call x1, Pallas kernels, total(): pl.pallas_call(total_kernel, out_shape=jax.ShapeDtypeStruct(v.shape, v.dt...  17.6 us
    pallas_call x1, Pallas kernels, run_update(): pl.pallas_call(functools.partial(update_kernel, totals), grid=(-(-row_cou...  14.1 us
    pallas_call x1, Pallas kernels, run_contrast(): pl.pallas_call(contrast_kernel, out_shape=[one, jax.ShapeDtypeStruct((8,...  12.6 us

profile of v5, /device:TPU:0, one launch (start us, length us, event | category | flops | bytes accessed | tf_op | source)
XLA Modules:
  0.0 391.3 jit_solution(13328649339909155967)
XLA Ops:
  7.2 0.7 multiply_subtract_fusion
  7.9 1.0 select_reduce_fusion.1
  8.9 0.5 convert_reduce_fusion
  9.4 0.6 fusion.6
  10.1 0.2 select_reduce_fusion
  10.3 0.1 reshape.171
  10.4 1.2 concatenate.15.ask_ref
  11.7 0.9 copy.93.key_ref
  12.5 0.8 reduce-window.8
  13.3 0.1 convert_reduce_fusion.1
  13.4 0.1 copy.94.seg_col_ref
  13.6 1.7 convert.20
  15.3 0.4 copy.106
  15.7 0.1 bitcast_bitcast_fusion
  15.8 1.3 copy.92
  17.2 0.3 reshape.167
  17.5 0.1 copy.91
  17.6 0.1 convert.21
  17.7 1.0 copy-done.13
  18.7 0.1 pad_maximum_fusion
  18.9 1.5 fusion.2.w_ref
  20.4 116.9 %shard_map.339 = (bf16[8,2144,512]{2,1,0:T(8,128)(2,1)}, s32[4,8,1,128]{3,2,1,0:T(1,128)S(1)}, bf16[2,512,512]{2,1,0:T(8,128)(2,1)}, bf16[2,512,1536]{2,1,0:T(8,...) custom-call(bf16[2144,512]{1,0:T(8,128)(2,1)} %fusion.2.w_ref, ...), custom_call_target="tpu_custom_call" | custom-call | tf_op jit(solution)/shard_map/pallas_call | solution.py:1033
  137.3 0.7 slice_reduce_fusion.1
  138.7 5.6 %convert.28 = bf16[3816,512]{1,0:T(8,128)(2,1)} convert(f32[3816,512]{1,0:T(8,128)} %embed_ref.1) | non-fusion elementwise | flops 1953792 | bytes 11722752
  144.3 0.1 while.25
  145.2 0.7 copy.96.deal_col_ref
  145.9 12.6 %shard_map.340 = (f32[1,1]{1,0:T(1,128)}, f32[8,512]{1,0:T(8,128)}, f32[1,1]{1,0:T(1,128)}) custom-call(f32[16,128]{1,0:T(8,128)} %get-tuple-element.225.unit_ref, s32[128,1]{1,0:T(8,128)} %copy.96.deal_col_ref, s32[1,128]{1,0:T(1,128)} %bitcast.69, f32[1,1]{1,0:T(1,128)} %bitcast.46.scale_ref), custom_call_target="tpu_custom_call" | custom-call | tf_op jit(solution)/shard_map/pallas_call | solution.py:1109
  161.0 154.4 %shard_map.341 = (bf16[2112,512]{1,0:T(8,128)(2,1)}, bf16[4,8,80,512]{3,2,1,0:T(8,128)(2,1)}, f32[3,8,512]{2,1,0:T(8,128)S(1)}, bf16[512,512]{1,0:T(8,128)(2,1)}) custom-call(f32[8,512]{1,0:T(8,128)} %get-tuple-element.227.own_ref, f32[8,512]{1,0:T(8,128)} %get-tuple-element.228.zed_ref, bf16[8,512]{1,0:T(8,128)(2,1)} %get-tuple-element.229.pool_ref, ...), custom_call_target="tpu_custom_call" | custom-call | tf_op jit(solution)/shard_map/pallas_call | solution.py:1589
  315.4 0.1 copy.99
  315.7 22.5 %conditional.1 = (bf16[3816,512]{1,0:T(8,128)(2,1)}, f32[1,3816]{1,0:T(1,128)}, f32[32,3,512]{2,1,0:T(4,128)}, f32[64,8]{1,0:T(8,128)}, f32[256,2]{1,0:T(8,128)}, /*index=5*/f32[3816]{0:T(1024)S(1)}) conditional(s32[]{:T(128)} %convert_element_type.39, (s32[4,8,1,128]{3,2,1,0:T(1,128)S(1)}, bf16[4,8,80,512]{3,2,1,0:T(8,128)(2,1)}, ...), branch_computations={%region_9.10_spmd, %region_10.14_spmd} | conditional | flops 2479616 | bytes 325181440 | solution.py:1932
  315.7 0.1 copy.101.refs_5_
  315.8 0.1 reshape_squeeze.3.refs_0_
  315.9 21.3 %branch_0_fun.1 = (bf16[3816,512]{1,0:T(8,128)(2,1)}, f32[1,3816]{1,0:T(1,128)}, f32[32,3,512]{2,1,0:T(4,128)}, f32[64,8]{1,0:T(8,128)}, f32[256,2]{1,0:T(8,128)}) custom-call(s32[1,2560]{1,0:T(1,128)S(1)} %reshape_squeeze.3.refs_0_, bf16[2560,512]{1,0:T(8,128)(2,1)} %bitcast.51, bf16[2112,512]{1,0:T(8,128)(2,1)} %get-tuple-element.128.refs_2_, ...), custom_call_target="tpu_custom_call" | custom-call | tf_op jit(solution)/shard_map/cond/branch_0_fun/pallas_call | solution.py:1768
  337.2 0.8 reduce.1
  338.2 0.0 copy-start.20
  338.2 17.6 %shard_map.342.stat_ref = f32[32,3,512]{2,1,0:T(4,128)} custom-call(f32[32,3,512]{2,1,0:T(4,128)} %get-tuple-element.240.v_ref), custom_call_target="tpu_custom_call" | custom-call | tf_op jit(solution)/shard_map/pallas_call | solution.py:1653
  355.8 1.1 copy-done.4
  356.9 0.9 copy-done.5
  357.9 0.9 copy-done.8
  358.8 0.8 copy-done.11
  359.7 14.1 %shard_map.343 = (f32[3816,512]{1,0:T(8,128)}, f32[1,512]{1,0:T(1,128)}, f32[1,512]{1,0:T(1,128)}, f32[2,6656]{1,0:T(2,128)}, f32[2,64,1536]{2,1,0:T(8,128)}, /*...) custom-call(f32[32,3,512]{2,1,0:T(4,128)S(1)} %copy-done.5, ...), custom_call_target="tpu_custom_call" | custom-call | tf_op jit(solution)/shard_map/pallas_call | solution.py:1848
  373.7 0.5 slice_bitcast_fusion
  374.2 0.1 reshape.184
  374.4 1.4 multiply_add_fusion
  375.8 0.8 copy.103
  376.6 0.6 copy.105
  377.2 1.6 copy.104
  378.8 1.5 slice_reduce_fusion
  (57 shorter events, 0.3 us)
Async XLA Ops:
  10.1 5.7 %copy-start.16 = (s32[512]{0:T(512)}, s32[512]{0:T(512)S(1)}, u32[]{:S(2)}) copy-start(s32[512]{0:T(512)S(1)} %get-tuple-element.503) | copy-start | bytes 6148
  15.3 1.8 copy-start.3
  15.7 1.8 copy-start.1
  15.8 1.8 copy-start.7
  17.4 1.2 copy-start.13
  17.6 1.3 copy-start.9
  17.6 1.3 copy-start.17
  18.8 1.6 copy-start.15
  138.7 5.7 %copy-start.14 = (s32[512]{0:T(512)S(1)}, s32[512]{0:T(512)}, u32[]{:S(2)}) copy-start(s32[512]{0:T(512)} %param.24) | copy-start | bytes 6148
  144.3 0.8 copy-start.23
  160.9 154.5 %copy-start.22 = (f32[2,256]{1,0:T(2,128)S(1)}, f32[2,256]{1,0:T(2,128)}, u32[]{:S(2)}) copy-start(f32[2,256]{1,0:T(2,128)} %param.39) | copy-start | bytes 6148
  160.9 154.6 %copy-start.19 = (f32[3816]{0:T(1024)S(1)}, f32[3816]{0:T(1024)}, u32[]{:S(2)}) copy-start(f32[3816]{0:T(1024)} %param.36) | copy-start | bytes 45796
  161.0 154.6 %copy-start.21 = (f32[2,3,64]{2,0,1:T(2,128)S(1)}, f32[2,3,64]{2,0,1:T(2,128)}, u32[]{:S(2)}) copy-start(f32[2,3,64]{2,0,1:T(2,128)} %param.38) | copy-start | bytes 4612
  161.0 154.6 %copy-start.24 = (f32[64]{0:T(128)S(1)}, f32[64]{0:T(128)}, u32[]{:S(2)}) copy-start(f32[64]{0:T(128)} %param.37) | copy-start | bytes 772
  315.6 40.1 %copy-start = (f32[2,64,4096]{2,1,0:T(8,128)S(1)}, f32[2,64,4096]{2,1,0:T(8,128)}, u32[]{:S(2)}) copy-start(f32[2,64,4096]{2,1,0:T(8,128)} %gate_ref.1) | copy-start | bytes 6291460
  315.6 40.1 %copy-start.2 = (f32[2,256,512]{2,1,0:T(8,128)S(1)}, f32[2,256,512]{2,1,0:T(8,128)}, u32[]{:S(2)}) copy-start(f32[2,256,512]{2,1,0:T(8,128)} %low_ref.1) | copy-start | bytes 3145732
  315.6 40.1 %copy-start.10 = (f32[64,512]{1,0:T(8,128)S(1)}, f32[64,512]{1,0:T(8,128)}, u32[]{:S(2)}) copy-start(f32[64,512]{1,0:T(8,128)} %head_ref.1) | copy-start | bytes 393220
  315.7 40.1 %copy-start.12 = (f32[2,512]{1,0:T(2,128)S(1)}, f32[2,512]{1,0:T(2,128)}, u32[]{:S(2)}) copy-start(f32[2,512]{1,0:T(2,128)} %top_cols_ref.1) | copy-start | bytes 12292
  338.2 17.6 %copy-start.20 = (f32[3816]{0:T(1024)}, f32[3816]{0:T(1024)S(1)}, u32[]{:S(2)}) copy-start(f32[3816]{0:T(1024)S(1)} %get-tuple-element.612) | copy-start | bytes 45796
  355.8 1.1 copy-start.4
  356.9 0.9 copy-start.5
  357.9 0.9 copy-start.8
  358.8 0.8 copy-start.11
  359.6 14.6 %copy-start.6 = (f32[32,3,512]{2,1,0:T(4,128)S(1)}, f32[32,3,512]{2,1,0:T(4,128)}, u32[]{:S(2)}) copy-start(f32[32,3,512]{2,1,0:T(4,128)} %shard_map.342.stat_ref) | copy-start | bytes 589828
  359.7 14.7 %copy-start.18 = (f32[5,2,64]{2,1,0:T(2,128)S(1)}, f32[5,2,64]{2,1,0:T(2,128)}, u32[]{:S(2)}) copy-start(f32[5,2,64]{2,1,0:T(2,128)} %param.35) | copy-start | bytes 7684

commit v6 on v5

--- a/solution.py
+++ b/solution.py
@@ -503,6 +503,10 @@
     )
 
 
+def step_id(kind, first=0, second=0, third=0):
+    return ord(kind) * 1000 + first * 100 + second * 10 + third
+
+
 GELU_SCALE = (2.0 / 3.141592653589793) ** 0.5
 GELU_CUBE = 0.044715
 TILE = 256
@@ -669,17 +673,18 @@
     (1056, 128, 48), (1312, 128, 48), (1568, 128, 48), (1824, 160, 32),
 )
 GATHER_ORDER = (
-    "ask", "s00", "s01", "s02", "s03", "set", "ans", "z00", "z10", "x03", "z20", "x13", "x23", "rel", "x33", "y000",
-    "z30", "y100", "y031", "y131", "z01", "z11", "y200", "z21", "y231", "y300", "z31", "y331", "y010", "x00", "y210",
-    "y110", "x10", "z02", "s04", "x20", "y001", "y310", "x01", "z12", "s05", "x11", "y101", "y020", "x30", "z22",
-    "s06", "z40", "y011", "x21", "y201", "z32", "s07", "x31", "y301", "y111", "z50", "y120", "y400", "y220", "x02",
-    "y211", "x43", "z41", "y311", "y320", "z60", "x12", "y500", "z42", "z51", "x53", "z70", "y021", "y431", "z52",
-    "y410", "x40", "z61", "x22", "y600", "x63", "a0", "y121", "z62", "y420", "y510", "rows", "y531", "z71", "x50",
-    "x32", "y700", "p0", "x73", "y401", "a1", "y520", "y221", "z72", "h00", "y610", "y631", "h01", "x60", "x41",
-    "x42", "h02", "x51", "a2", "y620", "h03", "y321", "y501", "y710", "x70", "h04", "y731", "x52", "h05", "x61",
-    "y720", "a3", "h06", "y601", "y411", "h07", "y421", "m0", "y511", "x62", "y701", "x71", "f00", "y521", "y611",
-    "a4", "x72", "f01", "y621", "a5", "y711", "p1", "h10", "y721", "a6", "h11", "h12", "h13", "h14", "a7", "h15",
-    "h16", "h17", "m1", "f10", "f11", "end",
+    113000, 115000, 115100, 115200, 115300, 116000, 110000, 122000, 122100, 120030, 122200, 120130, 120230, 114000,
+    120330, 121000, 122300, 121100, 121031, 121131, 122010, 122110, 121200, 122210, 121231, 121300, 122310, 121331,
+    121010, 120000, 121210, 121110, 120100, 122020, 115400, 120200, 121001, 121310, 120010, 122120, 115500, 120110,
+    121101, 121020, 120300, 122220, 115600, 122400, 121011, 120210, 121201, 122320, 115700, 120310, 121301, 121111,
+    122500, 121120, 121400, 121220, 120020, 121211, 120430, 122410, 121311, 121320, 122600, 120120, 121500, 122420,
+    122510, 120530, 122700, 121021, 121431, 122520, 121410, 120400, 122610, 120220, 121600, 120630, 97000, 121121,
+    122620, 121420, 121510, 119000, 121531, 122710, 120500, 120320, 121700, 112000, 120730, 121401, 97100, 121520,
+    121221, 122720, 104000, 121610, 121631, 104010, 120600, 120410, 120420, 104020, 120510, 97200, 121620, 104030,
+    121321, 121501, 121710, 120700, 104040, 121731, 120520, 104050, 120610, 121720, 97300, 104060, 121601, 121411,
+    104070, 121421, 109000, 121511, 120620, 121701, 120710, 102000, 121521, 121611, 97400, 120720, 102010, 121621,
+    97500, 121711, 112100, 104100, 121721, 97600, 104110, 104120, 104130, 104140, 97700, 104150, 104160, 104170,
+    109100, 102100, 102110, 118000,
 )
 
 
@@ -755,14 +760,14 @@
             for copy in cores.values():
                 copy.wait_recv()
 
-        steps["s0%d" % q] = (issue,)
+        steps[step_id("s", q)] = (issue,)
         for n in range(3):
-            steps["z%d%d" % (q, n)] = (along, n)
+            steps[step_id("z", q, n)] = (along, n)
         for n in range(4):
-            steps["x%d%d" % (q, n)] = (sideways, n)
+            steps[step_id("x", q, n)] = (sideways, n)
         for n, f in others:
-            steps["y%d%d%d" % (q, n, f)] = (plane, n, f)
-        steps["a%d" % q] = (arrived,)
+            steps[step_id("y", q, n, f)] = (plane, n, f)
+        steps[step_id("a", q)] = (arrived,)
 
     for q, spec in enumerate(PARCELS):
         parcel(q, *spec)
@@ -979,17 +984,17 @@
         fetch["head", 0].wait()
         pool_units(x_s, norm_ref, seg_row_ref, valid_ref, head, unit_ref, pool_ref, zed_ref)
 
-    arrived = [steps["a%d" % q][0] for q in range(8)]
+    arrived = [steps[step_id("a", q)][0] for q in range(8)]
     for q in range(8):
-        steps["a%d" % q] = (arrive, q)
-    steps["ask"], steps["ans"], steps["rel"] = (ask,), (answer,), (relay,)
-    steps["set"], steps["rows"], steps["end"] = (set_up,), (first_rows,), (end,)
+        steps[step_id("a", q)] = (arrive, q)
+    steps[step_id("q")], steps[step_id("n")], steps[step_id("r")] = (ask,), (answer,), (relay,)
+    steps[step_id("t")], steps[step_id("w")], steps[step_id("v")] = (set_up,), (first_rows,), (end,)
     for layer in range(LAYERS):
-        steps["p%d" % layer], steps["m%d" % layer] = (project, layer), (mix, layer)
+        steps[step_id("p", layer)], steps[step_id("m", layer)] = (project, layer), (mix, layer)
         for head_index in range(HEADS):
-            steps["h%d%d" % (layer, head_index)] = (attend_head, layer, head_index)
+            steps[step_id("h", layer, head_index)] = (attend_head, layer, head_index)
         for i in range(tiles):
-            steps["f%d%d" % (layer, i)] = (feed, layer, i)
+            steps[step_id("f", layer, i)] = (feed, layer, i)
     begin()
     pl.semaphore_wait(barrier, len(peers))
     for name in GATHER_ORDER:
@@ -1122,11 +1127,30 @@
 PIECES = tuple(
     (stage, half, spare, at)
     for stage, half, spare, at in (
-        (320, 128, 32, GRAD_LAYER[1] + 256), (576, 128, 48, GRAD_LAYER[1] + 512), (832, 128, 32, GRAD_LAYER[1] + 768),
-        (0, 160, 48, GRAD_HEAD),
-        (320, 128, 32, 256), (576, 128, 48, 512), (832, 128, 32, 768),
+        (320, 128, 32, GRAD_LAYER[1] + 256), (576, 128, 32, GRAD_LAYER[1] + 512), (832, 128, 32, GRAD_LAYER[1] + 768),
+        (0, 160, 32, GRAD_HEAD),
+        (320, 128, 32, 256), (576, 128, 32, 512), (832, 128, 32, 768),
         (64, 128, 32, 0),
     )
+)
+
+
+BACKWARD_ORDER = (
+    98000, 101100, 102100, 102110, 102120, 102130, 115000, 115100, 115200, 109100, 67000, 67010, 67020, 67030, 104100,
+    67040, 67050, 67060, 89000, 67070, 67100, 67110, 89010, 67120, 67130, 67140, 67150, 67160, 89020, 67170, 89030,
+    104110, 89040, 89050, 67200, 67210, 88020, 89060, 67220, 67230, 67240, 67250, 89070, 67260, 67270, 88010, 104120,
+    89100, 89110, 89120, 104130, 88030, 89130, 89140, 89150, 104140, 89160, 88000, 89170, 104150, 89200, 89210, 88120,
+    104160, 89220, 89230, 90000, 89240, 88110, 104170, 89250, 89260, 88130, 89270, 108100, 70000, 115300, 88100,
+    88220, 101000, 88210, 90100, 102000, 67300, 88230, 67310, 88200, 67320, 67330, 67340, 67350, 67360, 67370, 70100,
+    102010, 89300, 90200, 89310, 89320, 89330, 89340, 102020, 88320, 89350, 89360, 89370, 70200, 102030, 115400,
+    115500, 88310, 115600, 88330, 88300, 109000, 67400, 67410, 67420, 67430, 67440, 67450, 67460, 67470, 67500,
+    104000, 89400, 67510, 89410, 67520, 67530, 67540, 89420, 67550, 67560, 67570, 67600, 89430, 67610, 67620, 67630,
+    89440, 90300, 67640, 89450, 67650, 88420, 67660, 104010, 89460, 89470, 67670, 89500, 88410, 104020, 89510, 89520,
+    89530, 88430, 104030, 89540, 89550, 104040, 89560, 88400, 89570, 104050, 89600, 89610, 88520, 104060, 90400,
+    89620, 88510, 89630, 104070, 70300, 89640, 89650, 88530, 89660, 108000, 115700, 73000, 69000, 89670, 88500, 70400,
+    88620, 67700, 67710, 67720, 88610, 67730, 67740, 67750, 68000, 67760, 67770, 78000, 89700, 89710, 89720, 89730,
+    88630, 89740, 69200, 89750, 90500, 69400, 89760, 69600, 69300, 89770, 69500, 69100, 69700, 88600, 70500, 68200,
+    68600, 68400, 68700, 68100, 68300, 68500, 88720, 88710, 88730, 90600, 88700, 70600, 90700, 70700, 118000,
 )
 
 
@@ -1190,7 +1214,7 @@
         p.O = pltpu.make_async_copy(fin.at[pl.ds(lo[q], half)], out_ref.at[pl.ds(mult(at + c * half), half)], os_.at[q])
         pieces.append(p)
 
-    def s0(q):
+    def issue(q):
         p = pieces[q]
         if q >= 4:
             pl.semaphore_wait(free.at[q - 4], 1)
@@ -1198,36 +1222,34 @@
             p.C[i].start()
             p.L[i].start()
 
-    def s1(q):
+    def core(q, i):
         p = pieces[q]
-        for i, (k, f) in enumerate(order):
-            s = owner(k, f)
-            p.L[i].wait()
-            p.C[i].wait_recv()
-            add(lambda a, n=32: acc.at[s, pl.ds(lo[q] + a, n)], lambda a, n=32: b1.at[s, pl.ds(l1[q] + a, n)], p.half)
-            p.Y[i].start()
-        if q < 4:
+        s = owner(*order[i])
+        p.L[i].wait()
+        p.C[i].wait_recv()
+        add(lambda a, n=32: acc.at[s, pl.ds(lo[q] + a, n)], lambda a, n=32: b1.at[s, pl.ds(l1[q] + a, n)], p.half)
+        p.Y[i].start()
+        if i == 7 and q < 4:
             pl.semaphore_signal(free.at[q], inc=1, device_id=cp, device_id_type=MESH)
 
-    def s2(q):
+    def plane(q, i):
         p = pieces[q]
-        for i, (k, f) in enumerate(order):
-            s = owner(k, f)
-            p.Y[i].wait_recv()
-            add(lambda a, n=32: acc.at[s, pl.ds(p.mb + a, n)], lambda a, n=32: b2.at[s, pl.ds(lb[q] + a, n)], p.spare)
-            if f == 1:
-                p.X[k].start()
-
-    def s3(q):
+        k, f = order[i]
+        s = owner(k, f)
+        p.Y[i].wait_recv()
+        add(lambda a, n=32: acc.at[s, pl.ds(p.mb + a, n)], lambda a, n=32: b2.at[s, pl.ds(lb[q] + a, n)], p.spare)
+        if f == 1:
+            p.X[k].start()
+
+    def sideways(q, k):
         p = pieces[q]
-        for k in (2, 1, 3, 0):
-            s = owner(k, 0)
-            p.X[k].wait_recv()
-            add(lambda a, n=32: acc.at[s, pl.ds(p.hs + a, n)], lambda a, n=32: b3.at[k, pl.ds(lh[q] + a, n)], p.main)
-            if k:
-                p.Z[k].start()
-
-    def s4(q):
+        s = owner(k, 0)
+        p.X[k].wait_recv()
+        add(lambda a, n=32: acc.at[s, pl.ds(p.hs + a, n)], lambda a, n=32: b3.at[k, pl.ds(lh[q] + a, n)], p.main)
+        if k:
+            p.Z[k].start()
+
+    def along(q):
         p = pieces[q]
         for k in range(1, 4):
             p.Z[k].wait_recv()
@@ -1242,7 +1264,7 @@
         p.A.start()
         p.B.start()
 
-    def s5(q):
+    def last(q):
         p = pieces[q]
         p.A.wait_recv()
         p.A.wait_send()
@@ -1251,6 +1273,14 @@
         p.F.start()
         p.O.start()
 
+    steps = {}
+    for q in range(8):
+        steps[step_id("s", q)], steps[step_id("Z", q)], steps[step_id("F", q)] = (issue, q), (along, q), (last, q)
+        for i in range(8):
+            steps[step_id("C", q, i)], steps[step_id("Y", q, i)] = (core, q, i), (plane, q, i)
+        for k in range(4):
+            steps[step_id("X", q, k)] = (sideways, q, k)
+
     def sent(q):
         for copy in pieces[q].C:
             copy.wait_send()
@@ -1263,7 +1293,7 @@
             for copy in p.Y + p.X + p.Z[1:]:
                 copy.wait_send()
 
-    return [s0, s1, s2, s3, s4, s5], sent, finish
+    return steps, sent, finish
 
 
 def row_exchange(slots, t_ref, norm_ref, norm_out, nbuf, es, er, el, ns, nr):
@@ -1286,38 +1316,41 @@
     NC = rc(norm_ref, nbuf.at[0], ns.at[0], nr.at[0], cp)
     NY = rc(nbuf.at[1], nbuf.at[2], ns.at[1], nr.at[1], yp)
 
-    def e0():
+    def issue():
         kept.start()
         for copy in E:
             copy.start()
         NC.start()
 
-    def e1():
-        kept.wait()
-        EY[0].start()
-        EC[0].start()
+    def norms():
         NC.wait_recv()
         nbuf[1] = nbuf[0] + norm_ref[...]
         NY.start()
-        for k in range(1, 8):
+
+    def relay(k):
+        if k:
             E[k - 1].wait_recv()
-            EY[k].start()
-            EC[k].start()
-
-    def e2():
-        for k in range(8):
-            EY[k].wait_recv()
-            ED[k].start()
+        else:
+            kept.wait()
+        EY[k].start()
+        EC[k].start()
+
+    def relay_core(k):
+        EY[k].wait_recv()
+        ED[k].start()
+
+    def end():
         NY.wait_recv()
         norm_out[...] = nbuf[1] + nbuf[2]
-
-    def e3():
         for copy in EC + ED:
             copy.wait_recv()
         for copy in E + EY + EC + ED + [NC, NY]:
             copy.wait_send()
 
-    return [e0, e1, e2, e3]
+    steps = {step_id("I"): (issue,), step_id("N"): (norms,), step_id("v"): (end,)}
+    for k in range(8):
+        steps[step_id("E", k)], steps[step_id("D", k)] = (relay, k), (relay_core, k)
+    return steps
 
 
 def backward_kernel(
@@ -1339,10 +1372,10 @@
     barrier = pltpu.get_barrier_semaphore()
     for peer in peers:
         pl.semaphore_signal(barrier, inc=1, device_id=peer, device_id_type=MESH)
-    stages, sent, finish = sum_stages(
+    steps, sent, finish = sum_stages(
         stage, out_ref, total, b1, b2, b3, b4, b5, fin, (cs, cr, ys, yr, xs, xr, zs, zr, as_, ar, fs, fr, ls, os_), free
     )
-    rows_out = row_exchange(slots, t_ref, norm_s, norm_out, nbuf, es, er, el, ns, nr)
+    steps |= row_exchange(slots, t_ref, norm_s, norm_out, nbuf, es, er, el, ns, nr)
 
     def loading(layer):
         base = PACK_LAYER[layer]
@@ -1520,57 +1553,22 @@
                 hot = lax.broadcasted_iota(jnp.int32, (count, tokens), 0) + d * count == key_ref[...]
                 slots[d] = dot_nn(jnp.where(hot, 1.0, 0.0).astype(low_type), first_ref[...]).astype(low_type)
 
-    events = []
-    clock = 0.0
-
-    def do(cost, fn, *args):
-        nonlocal clock
-        events.append((clock, len(events), fn, args))
-        clock += cost
-
-    def wait_entry():
-        pl.semaphore_wait(barrier, len(peers))
-
-    ready = []
-    do(3.0, begin)
-    for layer in (1, 0):
-        do(2.5, enter, layer)
+    steps[step_id("b")] = (begin,)
+    for layer in range(LAYERS):
+        steps[step_id("e", layer)], steps[step_id("m", layer)], steps[step_id("l", layer)] = (enter, layer), (middle, layer), (leave, layer)
         for j in range(4):
-            do(4.7, feed, layer, j)
-        if layer == 1:
-            do(0.0, wait_entry)
-        ready += [clock] * 3
-        do(0.0, stages[0], len(ready) - 3)
-        do(0.0, stages[0], len(ready) - 2)
-        do(0.0, stages[0], len(ready) - 1)
-        do(2.5, middle, layer)
+            steps[step_id("f", layer, j)] = (feed, layer, j)
         for head_index in range(HEADS):
-            do(1.6, attend_head, layer, head_index)
-        do(4.0, leave, layer)
-        ready.append(clock)
-        if layer == 0:
-            do(0.0, rows_out[0])
-        do(0.0, stages[0], len(ready) - 1)
-    end = clock
-    links = {"c": 0.0, "y": 0.0, "x": 0.0, "z": 0.0}
-    for q in range(8):
-        scale = PIECES[q][1] / 128.0
-        now = ready[q]
-        for number, link, cost in ((1, "c", 3.0), (2, "y", 8.0), (3, "x", 9.5), (4, "z", 9.5), (5, "y", 1.0)):
-            now = max(now, links[link]) + cost * scale
-            if number < 5:
-                links[link] = now
-            else:
-                now += 3.0
-            events.append((now, len(events), stages[number], (q,)))
-    events.append((end + 8.0, len(events), rows_out[1], ()))
-    events.append((end + 26.0, len(events), rows_out[2], ()))
-    for _, _, fn, args in sorted(events, key=lambda event: event[:2]):
-        fn(*args)
+            steps[step_id("h", layer, head_index)] = (attend_head, layer, head_index)
+    for name in BACKWARD_ORDER:
+        if name == step_id("s"):
+            pl.semaphore_wait(barrier, len(peers))
+        fn, *rest = steps.pop(name)
+        fn(*rest)
+    assert not steps
     finish()
     for q in range(4, 8):
         sent(q)
-    rows_out[3]()
 
 
 def run_backward(own, zed, pool, seg_col, seg_row, valid, key, weights, norms, saved, cid):
@@ -1691,6 +1689,7 @@
 
 
 def stats_kernel(dense, row_count, *refs):
+    *refs, low_hot = refs
     if dense:
         full_ref, grads_ref, norm_ref, table_row_ref, rows_ref, down_ref, *outs = refs
     else:
@@ -1743,7 +1742,20 @@
     if dense:
         grad = jnp.where(index < row_count, full_ref[...], 0.0)
     else:
-        picks = jnp.where(index == slot_ref[...], 1.0, 0.0).astype(jnp.bfloat16)
+        high = slot_ref[...] // 64
+
+        @pl.when(step == 0)
+        def _():
+            low = lax.broadcasted_iota(jnp.int32, low_hot.shape, 0)
+            low_hot[...] = jnp.where(low == slot_ref[...] - 64 * high, 1.0, 0.0).astype(jnp.bfloat16)
+
+        picks = jnp.concatenate(
+            [
+                low_hot[...] * jnp.where(high == step * (ROW_TILE // 64) + i, 1.0, 0.0).astype(jnp.bfloat16)
+                for i in range(ROW_TILE // 64)
+            ],
+            axis=0,
+        )
         grad = jnp.dot(picks, slot_rows_ref[...], preferred_element_type=jnp.float32)
     low = grad.astype(jnp.bfloat16)
     table_ref[...] = low
@@ -1775,16 +1787,23 @@
             jax.ShapeDtypeStruct(stat, jnp.float32), jax.ShapeDtypeStruct(rows.shape, jnp.float32),
             jax.ShapeDtypeStruct(down.shape, jnp.float32),
         ],
+        scratch_shapes=[pltpu.VMEM((64, 8 if dense else heads[0].shape[1]), jnp.bfloat16)],
         compiler_params=pltpu.CompilerParams(vmem_limit_bytes=48 * 2**20),
     )(*heads, grads, norm, table_row, rows, down)
 
 
 def update_kernel(
-    totals, stat_ref, table_ref, embed_ref, table_row_ref, grads_ref, rows_ref, down_ref, top_cols_ref, cols_ref,
-    in_ref, mix_ref, gate_ref, low_ref, head_ref,
-    embed_out, table_cols_out, head_cols_out, cols_out, in_out, mix_out, gate_out, low_out, head_out, rms_out, factors,
+    totals, stat_ref, table_ref, embed_ref, table_row_ref, rows_ref, down_ref, top_cols_ref, cols_ref,
+    grads_in, in_in, mix_in, gate_in, low_in, head_in,
+    embed_out, table_cols_out, head_cols_out, cols_out, rms_out, in_to, mix_to, gate_to, low_to, head_to,
+    factors, grads_ref, in_ref, mix_ref, gate_ref, low_ref, head_ref, loads, stores,
 ):
     step = pl.program_id(0)
+    sources = (grads_in, in_in, mix_in, gate_in, low_in, head_in)
+    held = (grads_ref, in_ref, mix_ref, gate_ref, low_ref, head_ref)
+    targets = (in_to, mix_to, gate_to, low_to, head_to)
+    load = [pltpu.make_async_copy(sources[i], held[i], loads.at[i]) for i in range(6)]
+    store = [pltpu.make_async_copy(held[i + 1], targets[i], stores.at[i]) for i in range(5)]
 
     def stat(at):
         return stat_ref[at // 3, at % 3 : at % 3 + 1, :]
@@ -1806,17 +1825,25 @@
 
     @pl.when(step == 0)
     def _():
+        for copy in load:
+            copy.start()
         news, row_mean, rms, scale = columns(0, 1, lambda j: top_cols_ref[0:1, :], 0, 0)
         table_cols_out[...] = news[0]
         factors[0:1, :] = lax.rsqrt(news[0])
         factors[1:2, :] = jnp.broadcast_to(row_mean, (1, D))
         factors[2:3, :] = jnp.broadcast_to(scale, (1, D))
-        all_rms = lane_pick(rms, 0)
+        factors[3:4, :] = lane_pick(rms, 0)
+
+    @pl.when(step == pl.num_programs(0) - 1)
+    def _():
+        for copy in load:
+            copy.wait()
+        all_rms = factors[3:4, :]
         news, row_mean, rms, scale = columns(1, 1, lambda j: top_cols_ref[1:2, :], 1, 1)
         head_cols_out[...] = news[0]
         all_rms += lane_pick(rms, 1)
         row = lax.rsqrt(rows_ref[:, 6:7] / row_mean) * scale
-        head_out[...] = head_ref[...] + grads_ref[GRAD_HEAD : GRAD_HEAD + 64, :].astype(jnp.float32) * row * lax.rsqrt(news[0])
+        head_ref[...] = head_ref[...] + grads_ref[GRAD_HEAD : GRAD_HEAD + 64, :].astype(jnp.float32) * row * lax.rsqrt(news[0])
         for layer in range(LAYERS):
             for name, first, rows, blocks, block_at in matrices(layer):
                 col_at = (block_at - 2 - 13 * layer) * D
@@ -1826,16 +1853,23 @@
                 lane = 3 * layer + name - 2
                 state = down_ref[:, layer : layer + 1] if name == 5 else rows_ref[:, lane : lane + 1]
                 row = lax.rsqrt(state / row_mean) * scale
-                source, target = ((in_ref, in_out), (mix_ref, mix_out), (gate_ref, gate_out), (low_ref, low_out))[name - 2]
+                held_ref = (in_ref, mix_ref, gate_ref, low_ref)[name - 2]
                 for j in range(blocks):
                     cols_out[layer : layer + 1, col_at + j * D : col_at + (j + 1) * D] = news[j]
                     span = slice(j * D, (j + 1) * D)
                     grad = grads_ref[first + j * rows : first + (j + 1) * rows, :].astype(jnp.float32)
-                    target[layer, :, span] = source[layer, :, span] + grad * row * lax.rsqrt(news[j])
+                    held_ref[layer, :, span] = held_ref[layer, :, span] + grad * row * lax.rsqrt(news[j])
         rms_out[...] = all_rms
+        for copy in store:
+            copy.start()
 
     row = lax.rsqrt(turn(table_row_ref[...] / factors[1:2, :ROW_TILE])) * factors[2:3, 0:1]
     embed_out[...] = embed_ref[...] + table_ref[...].astype(jnp.float32) * row * factors[0:1, :]
+
+    @pl.when(step == pl.num_programs(0) - 1)
+    def _():
+        for copy in store:
+            copy.wait()
 
 
 def run_update(totals, stat, table, embed, table_row, grads, rows, down, top_cols, cols, others):
@@ -1844,18 +1878,21 @@
     lane = pl.BlockSpec((1, ROW_TILE), lambda i: (0, i))
     shape = lambda v: jax.ShapeDtypeStruct(v.shape, jnp.float32)
     one = jax.ShapeDtypeStruct((1, D), jnp.float32)
-    outs = [shape(embed), one, one, shape(cols)] + [shape(v) for v in others] + [one]
+    outs = [shape(embed), one, one, shape(cols), one]
+    anywhere = pl.BlockSpec(memory_space=pl.ANY)
     return pl.pallas_call(
         functools.partial(update_kernel, totals),
         grid=(-(-row_count // ROW_TILE),),
         in_specs=[whole(stat.shape), tile, tile, lane]
-        + [whole(v.shape) for v in (grads, rows, down, top_cols, cols)]
-        + [whole(v.shape) for v in others],
-        out_specs=[tile] + [whole(v.shape) for v in outs[1:]],
-        out_shape=outs,
-        scratch_shapes=[pltpu.VMEM((8, D), jnp.float32)],
-        compiler_params=pltpu.CompilerParams(vmem_limit_bytes=48 * 2**20),
-    )(stat, table, embed, table_row, grads, rows, down, top_cols, cols, *others)
+        + [whole(v.shape) for v in (rows, down, top_cols, cols)]
+        + [anywhere] * 6,
+        out_specs=[tile] + [whole(v.shape) for v in outs[1:]] + [anywhere] * 5,
+        out_shape=outs + [shape(v) for v in others],
+        scratch_shapes=[pltpu.VMEM((8, D), jnp.float32), pltpu.VMEM(grads.shape, jnp.bfloat16)]
+        + [pltpu.VMEM(v.shape, jnp.float32) for v in others]
+        + [pltpu.SemaphoreType.DMA((6,)), pltpu.SemaphoreType.DMA((5,))],
+        compiler_params=pltpu.CompilerParams(vmem_limit_bytes=62 * 2**20),
+    )(stat, table, embed, table_row, rows, down, top_cols, cols, grads, *others)
 
 
 def fast_shards(
@@ -1900,8 +1937,8 @@
     crowded = jnp.max(asked[:, :, 0, SLOTS:]) >= SLOTS
 
     def dense_forward(state):
-        table = lax.all_gather(embed_master.astype(jnp.bfloat16), "dp", axis=0, tiled=True)
-        first = jnp.take(table, token_ids, axis=0)
+        table = lax.all_gather(embed_master, "dp", axis=0, tiled=True)
+        first = jnp.take(table, token_ids, axis=0).astype(jnp.bfloat16)
         return (False, *run_forward(first, seg_col, seg_row, valid_row, weights[:, 32:], norms))
 
     _, *saved, unit_parts, pooled_low, head_out = lax.while_loop(
@@ -1935,7 +1972,7 @@
     sums = total(stats, 3)
     totals = (VOCAB, D, D, D, D, FF)
     (
-        new_embed, new_table_cols, new_head_cols, new_cols, new_in, new_mix, new_gate, new_low, new_head, rms_row,
+        new_embed, new_table_cols, new_head_cols, new_cols, rms_row, new_in, new_mix, new_gate, new_low, new_head,
     ) = run_update(
         totals, sums, table_grad, embed_master, table_row_new, shard_grads, rows_new, down_new,
         embed_head_cols, layer_cols, (attn_in, attn_out, ffn_in, ffn_out, head_master),

time: 397 us -> 380 us (0.957)
  Pallas kernels: 337 us -> 326 us
  local copies, waits for them, and re-layouts: 15.5 us -> 9.92 us
    pallas_call x1, Pallas kernels: 154 us -> 145 us  [run_backward(): pl.pallas_call(backward_kernel, in_specs=[near] * 8 + [anywhere] * 7, out...]
where the time goes in v6:
time: 380 us; the launch traced here: 374 us
  Pallas kernels  326 us (86%)
  between operations  22.6 us (6%)
  other arithmetic  15.4 us (4%)
  local copies, waits for them, and re-layouts  9.92 us (3%)
    pallas_call x1, Pallas kernels, run_backward(): pl.pallas_call(backward_kernel, in_specs=[near] * 8 + [anywhere] * 7, out...  145 us
    pallas_call x1, Pallas kernels, run_gather_forward(): pl.pallas_call(gather_forward_kernel, in_specs=[anywhere, near, anywhere,...  117 us
    pallas_call x1, Pallas kernels, run_stats(): pl.pallas_call(functools.partial(stats_kernel, dense, row_count), grid=(-...  21.1 us
    pallas_call x1, Pallas kernels, total(): pl.pallas_call(total_kernel, out_shape=jax.ShapeDtypeStruct(v.shape, v.dt...  15.3 us
    pallas_call x1, Pallas kernels, run_update(): pl.pallas_call(functools.partial(update_kernel, totals), grid=(-(-row_cou...  15.2 us
    pallas_call x1, Pallas kernels, run_contrast(): pl.pallas_call(contrast_kernel, out_shape=[one, jax.ShapeDtypeStruct((8,...  12.6 us

profile of v6, /device:TPU:0, one launch (start us, length us, event | category | flops | bytes accessed | tf_op | source)
XLA Modules:
  0.0 374.5 jit_solution(4280518845961701810)
XLA Ops:
  7.2 0.7 multiply_subtract_fusion
  7.9 1.0 select_reduce_fusion.1
  8.9 0.5 convert_reduce_fusion
  9.4 0.6 fusion.6
  10.1 0.2 select_reduce_fusion
  10.3 0.1 reshape.171
  10.4 1.2 concatenate.15.ask_ref
  11.7 0.9 copy.93.key_ref
  12.5 0.8 reduce-window.8
  13.3 0.1 convert_reduce_fusion.1
  13.4 0.1 copy.94.seg_col_ref
  13.6 1.7 convert.20
  15.3 0.4 copy.106
  15.7 0.0 copy-start.1
  15.7 0.1 bitcast_bitcast_fusion
  15.8 1.3 copy.92
  17.2 0.3 reshape.167
  17.4 0.0 copy-start.2
  17.5 0.1 copy.91
  17.6 0.0 copy-start.6
  17.6 0.1 convert.21
  17.7 1.0 copy-done.2
  18.7 0.1 pad_maximum_fusion
  18.9 1.5 fusion.2.w_ref
  20.4 116.9 %shard_map.339 = (bf16[8,2144,512]{2,1,0:T(8,128)(2,1)}, s32[4,8,1,128]{3,2,1,0:T(1,128)S(1)}, bf16[2,512,512]{2,1,0:T(8,128)(2,1)}, bf16[2,512,1536]{2,1,0:T(8,...) custom-call(bf16[2144,512]{1,0:T(8,128)(2,1)} %fusion.2.w_ref, ...), custom_call_target="tpu_custom_call" | custom-call | tf_op jit(solution)/shard_map/pallas_call | solution.py:1038
  137.3 0.7 slice_reduce_fusion.1
  138.7 0.0 copy-start.7
  138.7 5.6 %convert.28 = bf16[3816,512]{1,0:T(8,128)(2,1)} convert(f32[3816,512]{1,0:T(8,128)} %embed_ref.1) | non-fusion elementwise | flops 1953792 | bytes 11722752
  144.3 0.2 while.25
  145.2 0.7 copy.96.deal_col_ref
  145.9 12.6 %shard_map.340 = (f32[1,1]{1,0:T(1,128)}, f32[8,512]{1,0:T(8,128)}, f32[1,1]{1,0:T(1,128)}) custom-call(f32[16,128]{1,0:T(8,128)} %get-tuple-element.225.unit_ref, s32[128,1]{1,0:T(8,128)} %copy.96.deal_col_ref, s32[1,128]{1,0:T(1,128)} %bitcast.69, f32[1,1]{1,0:T(1,128)} %bitcast.46.scale_ref), custom_call_target="tpu_custom_call" | custom-call | tf_op jit(solution)/shard_map/pallas_call | solution.py:1114
  161.2 145.1 %shard_map.341 = (bf16[2112,512]{1,0:T(8,128)(2,1)}, bf16[4,8,80,512]{3,2,1,0:T(8,128)(2,1)}, f32[3,8,512]{2,1,0:T(8,128)S(1)}, bf16[512,512]{1,0:T(8,128)(2,1)S(1)}) custom-call(f32[8,512]{1,0:T(8,128)} %get-tuple-element.227.own_ref, f32[8,512]{1,0:T(8,128)} %get-tuple-element.228.zed_ref, bf16[8,512]{1,0:T(8,128)(2,1)} %get-tuple-element.229.pool_ref, ...), custom_call_target="tpu_custom_call" | custom-call | tf_op jit(solution)/shard_map/pallas_call | solution.py:1587
  306.3 0.1 copy.99
  306.5 22.2 %conditional.1 = (bf16[3816,512]{1,0:T(8,128)(2,1)}, f32[1,3816]{1,0:T(1,128)}, f32[32,3,512]{2,1,0:T(4,128)S(1)}, f32[64,8]{1,0:T(8,128)S(1)}, f32[256,2]{1,0:T(8,128)S(1)}, /*index=5*/f32[3816]{0:T(1024)S(1)}) conditional(s32[]{:T(128)} %convert_element_type.39, (s32[4,8,1,128]{3,2,1,0:T(1,128)S(1)}, bf16[4,8,80,512]{3,2,1,0:T(8,128)(2,1)}, ...), branch_computations={%region_9.10_spmd, %region_10.14_spmd} | conditional | flops 2479616 | bytes 333832192 | solution.py:1969
  306.5 0.1 copy.101.refs_5_
  306.6 0.1 reshape_squeeze.3.refs_0_
  306.7 21.1 %branch_0_fun.1 = (bf16[3816,512]{1,0:T(8,128)(2,1)}, f32[1,3816]{1,0:T(1,128)}, f32[32,3,512]{2,1,0:T(4,128)S(1)}, f32[64,8]{1,0:T(8,128)S(1)}, f32[256,2]{1,0:T(8,128)S(1)}) custom-call(s32[1,2560]{1,0:T(1,128)S(1)} %reshape_squeeze.3.refs_0_, bf16[2560,512]{1,0:T(8,128)(2,1)} %bitcast.51, bf16[2112,512]{1,0:T(8,128)(2,1)} %get-tuple-element.128.refs_2_, ...), custom_call_target="tpu_custom_call" | custom-call | tf_op jit(solution)/shard_map/cond/branch_0_fun/pallas_call | solution.py:1780
  327.8 0.8 reduce.1
  328.8 0.0 copy-start.13
  328.8 15.3 %shard_map.342.stat_ref = f32[32,3,512]{2,1,0:T(4,128)} custom-call(f32[32,3,512]{2,1,0:T(4,128)S(1)} %get-tuple-element.240.v_ref), custom_call_target="tpu_custom_call" | custom-call | tf_op jit(solution)/shard_map/pallas_call | solution.py:1651
  344.1 15.2 %shard_map.343 = (f32[3816,512]{1,0:T(8,128)}, f32[1,512]{1,0:T(1,128)}, f32[1,512]{1,0:T(1,128)}, f32[2,6656]{1,0:T(2,128)}, f32[1,512]{1,0:T(1,128)}, /*index=...) custom-call(f32[32,3,512]{2,1,0:T(4,128)} %shard_map.342.stat_ref, ...), custom_call_target="tpu_custom_call" | custom-call | tf_op jit(solution)/shard_map/pallas_call | solution.py:1883
  359.4 1.2 slice_bitcast_fusion
  360.6 0.1 reshape.184
  360.7 0.7 multiply_add_fusion
  361.4 0.1 copy.103
  361.5 0.6 copy.105
  362.1 0.7 copy.104
  362.8 0.7 slice_reduce_fusion
  (43 shorter events, 0.3 us)
Async XLA Ops:
  10.1 5.7 %copy-start.9 = (s32[512]{0:T(512)}, s32[512]{0:T(512)S(1)}, u32[]{:S(2)}) copy-start(s32[512]{0:T(512)S(1)} %get-tuple-element.503) | copy-start | bytes 6148
  15.3 1.8 copy-start.3
  15.7 1.8 copy-start.1
  15.8 1.8 copy-start.5
  17.4 1.2 copy-start.2
  17.6 1.3 copy-start.6
  17.6 1.3 copy-start.10
  18.8 1.6 copy-start.8
  138.7 5.7 %copy-start.7 = (s32[512]{0:T(512)S(1)}, s32[512]{0:T(512)}, u32[]{:S(2)}) copy-start(s32[512]{0:T(512)} %param.24) | copy-start | bytes 6148
  144.3 0.8 copy-start.17
  161.2 145.1 %copy-start.16 = (f32[2,256]{1,0:T(2,128)S(1)}, f32[2,256]{1,0:T(2,128)}, u32[]{:S(2)}) copy-start(f32[2,256]{1,0:T(2,128)} %param.39) | copy-start | bytes 6148
  161.2 145.3 %copy-start.12 = (f32[3816]{0:T(1024)S(1)}, f32[3816]{0:T(1024)}, u32[]{:S(2)}) copy-start(f32[3816]{0:T(1024)} %param.36) | copy-start | bytes 45796
  161.2 145.3 %copy-start.15 = (f32[2,3,64]{2,0,1:T(2,128)S(1)}, f32[2,3,64]{2,0,1:T(2,128)}, u32[]{:S(2)}) copy-start(f32[2,3,64]{2,0,1:T(2,128)} %param.38) | copy-start | bytes 4612
  161.2 145.3 %copy-start.18 = (f32[64]{0:T(128)S(1)}, f32[64]{0:T(128)}, u32[]{:S(2)}) copy-start(f32[64]{0:T(128)} %param.37) | copy-start | bytes 772
  328.8 30.6 %copy-start.13 = (f32[3816]{0:T(1024)}, f32[3816]{0:T(1024)S(1)}, u32[]{:S(2)}) copy-start(f32[3816]{0:T(1024)S(1)} %get-tuple-element.612) | copy-start | bytes 45796
  344.1 16.5 %copy-start.4 = (f32[32,3,512]{2,1,0:T(4,128)S(1)}, f32[32,3,512]{2,1,0:T(4,128)}, u32[]{:S(2)}) copy-start(f32[32,3,512]{2,1,0:T(4,128)} %shard_map.342.stat_ref) | copy-start | bytes 589828
  344.1 16.6 %copy-start.11 = (f32[5,2,64]{2,1,0:T(2,128)S(1)}, f32[5,2,64]{2,1,0:T(2,128)}, u32[]{:S(2)}) copy-start(f32[5,2,64]{2,1,0:T(2,128)} %param.35) | copy-start | bytes 7684
  344.1 16.6 %copy-start.14 = (f32[5,2,64]{2,1,0:T(2,128)S(1)}, f32[5,2,64]{2,1,0:T(2,128)}, u32[]{:S(2)}) copy-start(f32[5,2,64]{2,1,0:T(2,128)} %param.42) | copy-start | bytes 7684

commit v7 on v6

--- a/solution.py
+++ b/solution.py
@@ -1664,7 +1664,8 @@
 STEP_AT = 28
 SUM_AT = 56
 NORM_ROW = 57
-ROW_TILE = 512
+ROW_TILE = 1024
+STAT_TILE = 1024
 RATES = (
     RATE_SCALE, RATE_SCALE / D**0.5, RATE_SCALE / D**0.5, RATE_SCALE / (D // 8) ** 0.5,
     RATE_SCALE / D**0.5, RATE_SCALE / FF**0.5,
@@ -1738,7 +1739,7 @@
                 sums += lane_pick(count, 2 * name - 2 + layer)
         put(SUM_AT, sums)
 
-    index = lax.broadcasted_iota(jnp.int32, (ROW_TILE, 1), 0) + step * ROW_TILE
+    index = lax.broadcasted_iota(jnp.int32, (STAT_TILE, 1), 0) + step * STAT_TILE
     if dense:
         grad = jnp.where(index < row_count, full_ref[...], 0.0)
     else:
@@ -1751,8 +1752,8 @@
 
         picks = jnp.concatenate(
             [
-                low_hot[...] * jnp.where(high == step * (ROW_TILE // 64) + i, 1.0, 0.0).astype(jnp.bfloat16)
-                for i in range(ROW_TILE // 64)
+                low_hot[...] * jnp.where(high == step * (STAT_TILE // 64) + i, 1.0, 0.0).astype(jnp.bfloat16)
+                for i in range(STAT_TILE // 64)
             ],
             axis=0,
         )
@@ -1761,9 +1762,9 @@
     table_ref[...] = low
     squares = low.astype(jnp.float32) ** 2
     mean = jnp.mean(squares, axis=-1, keepdims=True)
-    mean_row = jnp.broadcast_to(mean, (ROW_TILE, 128)).T[0:1, :]
+    mean_row = jnp.broadcast_to(mean, (STAT_TILE, 128)).T[0:1, :]
     new = DECAY_RATE * table_row_ref[...] + (1.0 - DECAY_RATE) * (mean_row + STATE_EPS)
-    real = lax.broadcasted_iota(jnp.int32, (1, ROW_TILE), 1) + step * ROW_TILE < row_count
+    real = lax.broadcasted_iota(jnp.int32, (1, STAT_TILE), 1) + step * STAT_TILE < row_count
     new = jnp.where(real, new, 1.0)
     table_row_out[...] = new
     add(0, jnp.sum(squares, axis=0, keepdims=True))
@@ -1773,13 +1774,13 @@
 
 def run_stats(dense, heads, grads, norm, table_row, rows, down):
     row_count = table_row.shape[1]
-    tile = pl.BlockSpec((ROW_TILE, D), lambda i: (i, 0))
-    lane = pl.BlockSpec((1, ROW_TILE), lambda i: (0, i))
+    tile = pl.BlockSpec((STAT_TILE, D), lambda i: (i, 0))
+    lane = pl.BlockSpec((1, STAT_TILE), lambda i: (0, i))
     head_specs = [tile] if dense else [whole(v.shape) for v in heads]
     stat = (32, 3, D)
     return pl.pallas_call(
         functools.partial(stats_kernel, dense, row_count),
-        grid=(-(-row_count // ROW_TILE),),
+        grid=(-(-row_count // STAT_TILE),),
         in_specs=head_specs + [whole(grads.shape), whole(norm.shape), lane, whole(rows.shape), whole(down.shape)],
         out_specs=[tile, lane, whole(stat), whole(rows.shape), whole(down.shape)],
         out_shape=[
@@ -1863,7 +1864,7 @@
         for copy in store:
             copy.start()
 
-    row = lax.rsqrt(turn(table_row_ref[...] / factors[1:2, :ROW_TILE])) * factors[2:3, 0:1]
+    row = lax.rsqrt(turn(table_row_ref[...] / factors[1:2, 0:1])) * factors[2:3, 0:1]
     embed_out[...] = embed_ref[...] + table_ref[...].astype(jnp.float32) * row * factors[0:1, :]
 
     @pl.when(step == pl.num_programs(0) - 1)
@@ -1921,8 +1922,11 @@
     shard_rows = embed_master.shape[0]
     my_dp = lax.axis_index("dp")
     position = jnp.arange(tokens, dtype=jnp.int32)
-    bounds = jnp.cumsum(seq_lengths[0])
-    segment = jnp.sum((position[:, None] >= bounds[None, :]).astype(jnp.int32), axis=1)
+    segment = jnp.zeros_like(position)
+    bound = 0
+    for s in range(seq_lengths.shape[1]):
+        bound = bound + seq_lengths[0, s]
+        segment = segment + (position >= bound).astype(jnp.int32)
 
     key, wanted, most = slot_plan(token_ids, shard_rows)
     asks = jnp.concatenate(

time: 380 us -> 381 us (level)
  Pallas kernels: 326 us -> 322 us
where the time goes in v7:
time: 381 us; the launch traced here: 375 us
  Pallas kernels  322 us (85%)
  between operations  24.9 us (7%)
  other arithmetic  17.1 us (4%)
  local copies, waits for them, and re-layouts  10.2 us (3%)
    pallas_call x1, Pallas kernels, run_backward(): pl.pallas_call(backward_kernel, in_specs=[near] * 8 + [anywhere] * 7, out...  145 us
    pallas_call x1, Pallas kernels, run_gather_forward(): pl.pallas_call(gather_forward_kernel, in_specs=[anywhere, near, anywhere,...  117 us
    pallas_call x1, Pallas kernels, run_stats(): pl.pallas_call(functools.partial(stats_kernel, dense, row_count), grid=(-...  19.7 us
    pallas_call x1, Pallas kernels, total(): pl.pallas_call(total_kernel, out_shape=jax.ShapeDtypeStruct(v.shape, v.dt...  15.2 us
    pallas_call x1, Pallas kernels, run_update(): pl.pallas_call(functools.partial(update_kernel, totals), grid=(-(-row_cou...  13.1 us
    pallas_call x1, Pallas kernels, run_contrast(): pl.pallas_call(contrast_kernel, out_shape=[one, jax.ShapeDtypeStruct((8,...  12.6 us

profile of v7, /device:TPU:0, one launch (start us, length us, event | category | flops | bytes accessed | tf_op | source)
XLA Modules:
  0.0 375.0 jit_solution(7002978857168303321)
XLA Ops:
  7.2 1.4 fusion.17
  11.2 1.5 convert_add_fusion.1.seg_col_ref
  12.6 1.2 fusion.14.seg_row_ref
  13.9 0.7 multiply_subtract_fusion
  14.6 1.0 select_reduce_fusion.1
  15.6 0.5 convert_reduce_fusion
  16.1 0.6 fusion.16
  16.8 0.2 select_reduce_fusion
  17.0 0.1 reshape.235
  17.1 1.2 concatenate.15.ask_ref
  18.3 0.9 copy.98.key_ref
  19.2 1.7 convert.20
  20.9 0.0 copy-start.2
  20.9 0.4 copy.111
  21.3 0.0 copy-start.1
  21.3 0.1 bitcast_bitcast_fusion
  21.4 0.3 copy.96
  21.8 0.3 copy-done.2
  22.1 0.3 reshape.231
  22.4 0.1 copy.95
  22.5 0.1 copy-done.1
  22.6 0.1 convert.21
  22.7 0.1 pad_maximum_fusion
  22.9 0.5 copy-done.5
  23.5 1.5 fusion.9.w_ref
  25.0 116.9 %shard_map.339 = (bf16[8,2144,512]{2,1,0:T(8,128)(2,1)}, s32[4,8,1,128]{3,2,1,0:T(1,128)S(1)}, bf16[2,512,512]{2,1,0:T(8,128)(2,1)}, bf16[2,512,1536]{2,1,0:T(8,...) custom-call(bf16[2144,512]{1,0:T(8,128)(2,1)} %fusion.9.w_ref, ...), custom_call_target="tpu_custom_call" | custom-call | tf_op jit(solution)/shard_map/pallas_call | solution.py:1038
  141.9 0.7 slice_reduce_fusion.1
  143.3 5.6 %convert.28 = bf16[3816,512]{1,0:T(8,128)(2,1)} convert(f32[3816,512]{1,0:T(8,128)} %embed_ref.1) | non-fusion elementwise | flops 1953792 | bytes 11722752
  148.9 0.4 while.27
  150.0 0.7 copy.99.deal_col_ref
  150.7 12.6 %shard_map.340 = (f32[1,1]{1,0:T(1,128)}, f32[8,512]{1,0:T(8,128)}, f32[1,1]{1,0:T(1,128)}) custom-call(f32[16,128]{1,0:T(8,128)} %get-tuple-element.225.unit_ref, s32[128,1]{1,0:T(8,128)} %copy.99.deal_col_ref, s32[1,128]{1,0:T(1,128)} %bitcast.66, f32[1,1]{1,0:T(1,128)} %bitcast.46.scale_ref), custom_call_target="tpu_custom_call" | custom-call | tf_op jit(solution)/shard_map/pallas_call | solution.py:1114
  165.8 144.6 %shard_map.341 = (bf16[2112,512]{1,0:T(8,128)(2,1)}, bf16[4,8,80,512]{3,2,1,0:T(8,128)(2,1)}, f32[3,8,512]{2,1,0:T(8,128)S(1)}, bf16[512,512]{1,0:T(8,128)(2,1)S(1)}) custom-call(f32[8,512]{1,0:T(8,128)} %get-tuple-element.227.own_ref, f32[8,512]{1,0:T(8,128)} %get-tuple-element.228.zed_ref, bf16[8,512]{1,0:T(8,128)(2,1)} %get-tuple-element.229.pool_ref, ...), custom_call_target="tpu_custom_call" | custom-call | tf_op jit(solution)/shard_map/pallas_call | solution.py:1587
  310.4 0.1 copy.101
  310.6 20.8 %conditional.1 = (bf16[3816,512]{1,0:T(8,128)(2,1)}, f32[1,3816]{1,0:T(1,128)}, f32[32,3,512]{2,1,0:T(4,128)S(1)}, f32[64,8]{1,0:T(8,128)S(1)}, f32[256,2]{1,0:T(8,128)S(1)}, /*index=5*/f32[3816]{0:T(1024)S(1)}) conditional(s32[]{:T(128)} %convert_element_type.119, (s32[4,8,1,128]{3,2,1,0:T(1,128)S(1)}, bf16[4,8,80,512]{3,2,1,0:T(8,128)(2,1)}, ...), branch_computations={%region_7.8_spmd, %region_8.12_spmd} | conditional | flops 2479616 | bytes 333832192 | solution.py:1973
  310.6 0.1 copy.103.refs_5_
  310.7 0.1 reshape_squeeze.3.refs_0_
  310.8 19.7 %branch_0_fun.1 = (bf16[3816,512]{1,0:T(8,128)(2,1)}, f32[1,3816]{1,0:T(1,128)}, f32[32,3,512]{2,1,0:T(4,128)S(1)}, f32[64,8]{1,0:T(8,128)S(1)}, f32[256,2]{1,0:T(8,128)S(1)}) custom-call(s32[1,2560]{1,0:T(1,128)S(1)} %reshape_squeeze.3.refs_0_, bf16[2560,512]{1,0:T(8,128)(2,1)} %bitcast.51, bf16[2112,512]{1,0:T(8,128)(2,1)} %get-tuple-element.128.refs_2_, ...), custom_call_target="tpu_custom_call" | custom-call | tf_op jit(solution)/shard_map/cond/branch_0_fun/pallas_call | solution.py:1781
  330.5 0.8 reduce.1
  331.4 0.0 copy-start.12
  331.5 15.2 %shard_map.342.stat_ref = f32[32,3,512]{2,1,0:T(4,128)} custom-call(f32[32,3,512]{2,1,0:T(4,128)S(1)} %get-tuple-element.240.v_ref), custom_call_target="tpu_custom_call" | custom-call | tf_op jit(solution)/shard_map/pallas_call | solution.py:1651
  346.7 13.1 %shard_map.343 = (f32[3816,512]{1,0:T(8,128)}, f32[1,512]{1,0:T(1,128)}, f32[1,512]{1,0:T(1,128)}, f32[2,6656]{1,0:T(2,128)}, f32[1,512]{1,0:T(1,128)}, /*index=...) custom-call(f32[32,3,512]{2,1,0:T(4,128)} %shard_map.342.stat_ref, ...), custom_call_target="tpu_custom_call" | custom-call | tf_op jit(solution)/shard_map/pallas_call | solution.py:1884
  359.9 1.2 slice_bitcast_fusion
  361.1 0.1 reshape.244
  361.2 0.7 multiply_add_fusion
  361.9 0.1 copy.105
  362.0 0.6 copy.107
  362.6 0.7 copy.106
  363.3 0.7 slice_reduce_fusion
  (41 shorter events, 0.2 us)
Async XLA Ops:
  16.8 4.7 %copy-start.8 = (s32[512]{0:T(512)}, s32[512]{0:T(512)S(1)}, u32[]{:S(2)}) copy-start(s32[512]{0:T(512)S(1)} %get-tuple-element.576) | copy-start | bytes 6148
  20.9 1.1 copy-start.2
  21.3 1.3 copy-start.1
  21.4 1.3 copy-start.4
  22.5 1.0 copy-start.5
  22.6 0.8 copy-start.9
  22.9 2.1 copy-start.7
  143.3 5.7 %copy-start.6 = (s32[512]{0:T(512)S(1)}, s32[512]{0:T(512)}, u32[]{:S(2)}) copy-start(s32[512]{0:T(512)} %param.24) | copy-start | bytes 6148
  148.9 1.0 copy-start.16
  165.7 144.6 %copy-start.15 = (f32[2,256]{1,0:T(2,128)S(1)}, f32[2,256]{1,0:T(2,128)}, u32[]{:S(2)}) copy-start(f32[2,256]{1,0:T(2,128)} %param.39) | copy-start | bytes 6148
  165.7 144.8 %copy-start.11 = (f32[3816]{0:T(1024)S(1)}, f32[3816]{0:T(1024)}, u32[]{:S(2)}) copy-start(f32[3816]{0:T(1024)} %param.36) | copy-start | bytes 45796
  165.8 144.8 %copy-start.14 = (f32[2,3,64]{2,0,1:T(2,128)S(1)}, f32[2,3,64]{2,0,1:T(2,128)}, u32[]{:S(2)}) copy-start(f32[2,3,64]{2,0,1:T(2,128)} %param.38) | copy-start | bytes 4612
  165.8 144.8 %copy-start.17 = (f32[64]{0:T(128)S(1)}, f32[64]{0:T(128)}, u32[]{:S(2)}) copy-start(f32[64]{0:T(128)} %param.37) | copy-start | bytes 772
  331.4 28.5 %copy-start.12 = (f32[3816]{0:T(1024)}, f32[3816]{0:T(1024)S(1)}, u32[]{:S(2)}) copy-start(f32[3816]{0:T(1024)S(1)} %get-tuple-element.697) | copy-start | bytes 45796
  346.7 14.4 %copy-start.3 = (f32[32,3,512]{2,1,0:T(4,128)S(1)}, f32[32,3,512]{2,1,0:T(4,128)}, u32[]{:S(2)}) copy-start(f32[32,3,512]{2,1,0:T(4,128)} %shard_map.342.stat_ref) | copy-start | bytes 589828
  346.7 14.5 %copy-start.10 = (f32[5,2,64]{2,1,0:T(2,128)S(1)}, f32[5,2,64]{2,1,0:T(2,128)}, u32[]{:S(2)}) copy-start(f32[5,2,64]{2,1,0:T(2,128)} %param.35) | copy-start | bytes 7684
  346.7 14.5 %copy-start.13 = (f32[5,2,64]{2,1,0:T(2,128)S(1)}, f32[5,2,64]{2,1,0:T(2,128)}, u32[]{:S(2)}) copy-start(f32[5,2,64]{2,1,0:T(2,128)} %param.42) | copy-start | bytes 7684
